TPU v7x, 256 devices: a whole 4x4x8 slice. The times are simulated.
256 devices in a mesh: seq: 64 (over x, z, core), head: 4 (over y).
Axes of the slice: x: 4, y: 4, z: 8, core: 2. Of those that a mesh axis runs over, the one named last changes fastest.
Arguments:
- queries: bfloat16 [32768, 2048], P('seq', 'head'), may hold values from -128 to 128
- out_grad: bfloat16 [32768, 2048], P('seq', 'head'), may hold values from -6 to 6
- neighbours: bfloat16 [2048, 128, 4096], P('seq', None, 'head'), may hold values from -400 to 400
- placement: int32 [512, 2], P('seq'), may hold values from 0 to 2047, as said below
Outputs:
- attended: bfloat16 [32768, 2048], P('seq', 'head')
- query_grad: bfloat16 [32768, 2048], P('seq', 'head')
Inputs may be any that keep to these rules, and one draw needn't show every extreme that they name: placement[c, n] is the slot holding the n-th neighbour of span c; slot s is stored on index s // 32 of seq, and no slot is named twice. The 16 entries of one index of seq (aligned blocks of 8 rows) name at most 1 slots of one owner, and some index names exactly 1 of some owner; some owner has all its 32 slots named.
All inputs are finite; a program needn't handle non-finite values.
Results may differ from a plain program's by a relative error of at most 0.019.
The roundings to bfloat16 on the way count: a program that leaves them out, or rounds other values in their place, can miss the bound.
Values may be sent and summed in bfloat16 or wider, within the bound.
No kernel may reach another device: no remote copies, remote signals or barrier semaphores. Data moves between devices by JAX's collectives and lax.ppermute only.
A program may use at most 128 MiB of HBM per device.

v0:
```python
import math

import jax
import jax.numpy as jnp
from jax import lax
from jax.sharding import PartitionSpec as P

D = 4096
HD = 128
SPAN = 64
R = 128


def encode(span_queries, stored, row_scale):
    batch = stored.shape[0]
    heads_here = span_queries.shape[2]
    scale_factor = 1.0 / math.sqrt(HD)
    normed = stored.astype(jnp.float32) * row_scale[:, :, None]
    normed = normed.reshape(batch, R, heads_here, 2, HD)
    key_rows = normed[:, :, :, 0, :].astype(jnp.bfloat16)
    cond_scores = (
        jnp.einsum("irhd,ithd->irht", key_rows, span_queries, preferred_element_type=jnp.float32)
        * scale_factor
    )
    cond_weights = jax.nn.softmax(cond_scores, axis=-1).astype(jnp.bfloat16)
    conditioned = jnp.einsum(
        "irht,ithd->irhd", cond_weights, span_queries, preferred_element_type=jnp.float32
    )
    value_rows = (normed[:, :, :, 1, :] + conditioned).astype(jnp.bfloat16)
    return (key_rows, value_rows)


def attend(span_queries, key_rows, value_rows):
    scale_factor = 1.0 / math.sqrt(HD)
    scores = (
        jnp.einsum("ithd,irhd->ithr", span_queries, key_rows, preferred_element_type=jnp.float32)
        * scale_factor
    )
    row_top = jnp.max(scores, axis=-1).astype(jnp.bfloat16)
    exponent = jnp.exp(scores - lax.optimization_barrier(row_top).astype(jnp.float32)[..., None])
    row_total = jnp.sum(exponent, axis=-1).astype(jnp.bfloat16)
    partial_out = jnp.einsum(
        "ithr,irhd->ithd",
        exponent.astype(jnp.bfloat16),
        value_rows,
        preferred_element_type=jnp.float32,
    ).astype(jnp.bfloat16)
    return (exponent, row_top, row_total, partial_out)


def back_terms(exponent, key_rows, value_rows, grad_rows):
    prob_grad = jnp.einsum(
        "ithd,irhd->ithr", grad_rows, value_rows, preferred_element_type=jnp.float32
    )
    term_a = jnp.einsum(
        "ithr,irhd->ithd",
        (exponent * prob_grad).astype(jnp.bfloat16),
        key_rows,
        preferred_element_type=jnp.float32,
    ).astype(jnp.bfloat16)
    term_b = jnp.einsum(
        "ithr,irhd->ithd",
        exponent.astype(jnp.bfloat16),
        key_rows,
        preferred_element_type=jnp.float32,
    ).astype(jnp.bfloat16)
    return (term_a, term_b)


def combine(partial_out, row_top, row_total, grad_spans):
    top_float = lax.optimization_barrier(row_top).astype(jnp.float32)
    total_float = lax.optimization_barrier(row_total).astype(jnp.float32)
    highest = jnp.max(top_float, axis=1, keepdims=True)
    factor = jnp.exp(top_float - highest)
    denominator = jnp.sum(factor * total_float, axis=1, keepdims=True)
    weight_low = (factor / denominator).astype(jnp.bfloat16)
    weight = lax.optimization_barrier(weight_low).astype(jnp.float32)
    partial_float = partial_out.astype(jnp.float32)
    attended = jnp.sum(weight[..., None] * partial_float, axis=1).astype(jnp.bfloat16)
    products = jnp.sum(grad_spans.astype(jnp.float32)[:, None] * partial_float, axis=-1)
    delta_low = jnp.sum(weight * products, axis=1).astype(jnp.bfloat16)
    return (attended, weight_low, delta_low)


def scaled_terms(weight_low, delta_low, term_a, term_b):
    scale_factor = 1.0 / math.sqrt(HD)
    weight = lax.optimization_barrier(weight_low).astype(jnp.float32)
    delta = lax.optimization_barrier(delta_low).astype(jnp.float32)
    return (
        weight[..., None]
        * (term_a.astype(jnp.float32) - delta[..., None] * term_b.astype(jnp.float32))
        * scale_factor
    )


def slot_positions(got_slots, total_count):
    matches = got_slots[None, :] == jnp.arange(total_count, dtype=jnp.int32)[:, None]
    where_from = jnp.arange(got_slots.shape[0], dtype=jnp.int32)[None, :]
    return jnp.sum(jnp.where(matches, where_from, 0), axis=1)


def spread(rows_in, target, total_count):
    return jnp.zeros((total_count,) + rows_in.shape[1:], rows_in.dtype).at[target].set(rows_in)


def per_span(rows_in):
    return rows_in.reshape((rows_in.shape[0] // 2, 2) + rows_in.shape[1:])


def local(queries, out_grad, neighbours, placement):
    seq_count = lax.axis_size("seq")
    width_here = queries.shape[1]
    heads_here = width_here // HD
    span_count = placement.shape[0]
    item_count = 2 * span_count
    slot_count = neighbours.shape[0]
    pair_slots = max(1, (2 * item_count + seq_count - 1) // seq_count)
    block_count = seq_count * pair_slots
    query_spans = queries.reshape(span_count, SPAN, heads_here, HD)
    grad_spans = out_grad.reshape(span_count, SPAN, heads_here, HD)
    slot_flat = placement.reshape(item_count)
    owner_dev = slot_flat // slot_count
    local_slot = slot_flat % slot_count
    item_order = jnp.arange(item_count, dtype=jnp.int32)
    earlier = (owner_dev[:, None] == owner_dev[None, :]) & (
        item_order[:, None] > item_order[None, :]
    )
    target = owner_dev * pair_slots + jnp.sum(earlier, axis=1)
    slot_request = jnp.full((block_count,), -1, jnp.int32).at[target].set(local_slot)
    query_items = jnp.repeat(query_spans, 2, axis=0)
    grad_items = jnp.repeat(grad_spans, 2, axis=0)
    square_sums = jnp.sum(jnp.square(neighbours.astype(jnp.float32)), axis=-1)
    row_scale = lax.rsqrt(lax.psum(square_sums, "head") / D + 1e-06)
    query_send = spread(query_items, target, block_count)
    grad_send = spread(grad_items, target, block_count)
    got_queries, got_slots = (
        lax.all_to_all(query_send, "seq", split_axis=0, concat_axis=0, tiled=True),
        lax.all_to_all(slot_request, "seq", split_axis=0, concat_axis=0, tiled=True),
    )
    position = slot_positions(got_slots, slot_count)
    back_index = jnp.clip(got_slots, 0, slot_count - 1)
    slot_queries = got_queries[position]
    key_rows, value_rows = encode(slot_queries, neighbours, row_scale)
    exponent, row_top, row_total, partial_out = attend(slot_queries, key_rows, value_rows)
    back_part, back_top, back_total = (
        lax.all_to_all(partial_out[back_index], "seq", split_axis=0, concat_axis=0, tiled=True),
        lax.all_to_all(row_top[back_index], "seq", split_axis=0, concat_axis=0, tiled=True),
        lax.all_to_all(row_total[back_index], "seq", split_axis=0, concat_axis=0, tiled=True),
    )
    attended, weight_low, delta_low = combine(
        per_span(back_part[target]),
        per_span(back_top[target]),
        per_span(back_total[target]),
        grad_spans,
    )
    weight_send = spread(
        weight_low.reshape((item_count,) + weight_low.shape[2:]), target, block_count
    )
    delta_send = spread(jnp.repeat(delta_low, 2, axis=0), target, block_count)
    got_grads, got_weights, got_deltas = (
        lax.all_to_all(grad_send, "seq", split_axis=0, concat_axis=0, tiled=True),
        lax.all_to_all(weight_send, "seq", split_axis=0, concat_axis=0, tiled=True),
        lax.all_to_all(delta_send, "seq", split_axis=0, concat_axis=0, tiled=True),
    )
    term_a, term_b = back_terms(exponent, key_rows, value_rows, got_grads[position])
    slot_terms = scaled_terms(got_weights[position], got_deltas[position], term_a, term_b)
    returned_terms = lax.all_to_all(
        slot_terms[back_index], "seq", split_axis=0, concat_axis=0, tiled=True
    )
    query_terms = per_span(returned_terms[target])
    query_grad = jnp.sum(query_terms, axis=1).astype(jnp.bfloat16)
    return (attended.reshape(-1, width_here), query_grad.reshape(-1, width_here))


def solution(mesh):
    in_specs = (P("seq", "head"), P("seq", "head"), P("seq", None, "head"), P("seq", None))
    out_specs = (P("seq", "head"), P("seq", "head"))
    return jax.shard_map(local, mesh=mesh, in_specs=in_specs, out_specs=out_specs, check_vma=False)
```

profile of v0, /device:TPU:1, one launch (start us, length us, event | category | flops | bytes accessed | tf_op | source)
XLA Modules:
  0.0 616.3 jit_solution(5678438594815823495)
XLA Ops:
  3.1 13.0 %all-to-all-start.1 = ((s32[64,1,1]{2,1,0:T(1,128)}), s32[64,1,1]{2,1,0:T(1,128)S(1)}, u32[]{:S(2)}, u32[]{:S(2)}) async-start(s32[64,1,1]{2,1,0:T(1,128)} %copy.60), calls=%async_computation.1 | async-start | bytes 65536 | tf_op jit(solution)/shard_map/all_to_all | solution.py:138
  25.3 9.0 %all-to-all-start = ((bf16[64,64,4,128]{3,1,2,0:T(8,128)(2,1)}), bf16[64,64,4,128]{3,1,2,0:T(8,128)(2,1)}, u32[]{:S(2)}, u32[]{:S(2)}) async-start(bf16[64,64,4,128]{3,1,2,0:T(8,128)(2,1)} %scatter_fusion), calls=%async_computation | async-start | bytes 8388608 | tf_op jit(solution)/shard_map/all_to_all | solution.py:137
  40.9 89.2 %all-to-all-done = bf16[64,64,4,128]{3,1,2,0:T(8,128)(2,1)} async-done(((bf16[64,64,4,128]{3,1,2,0:T(8,128)(2,1)}), bf16[64,64,4,128]{3,1,2,0:T(8,128)(2,1)}, u32[]{:S(2)}, u32[]{:S(2)}) %all-to-all-start) | async-done | bytes 4194336 | tf_op jit(solution)/shard_map/all_to_all | solution.py:137
  130.2 5.9 all-to-all-start.6
  136.1 11.9 %copy.55 = bf16[32,128,1024]{1,2,0:T(8,128)(2,1)} copy(bf16[32,128,1024]{2,1,0:T(8,128)(2,1)} %param.6) | data formatting | bytes 16777216 | tf_op args[2]
  153.1 15.0 %psum.7 = f32[32,128]{1,0:T(8,128)S(1)} all-reduce(f32[32,128]{1,0:T(8,128)S(1)} %fusion.1), channel_id=1, replica_groups=mesh['seq'=64,'head'=4] {'head'}, use_global_device_ids=true, to_apply=%region_1.2 | all-reduce | flops 4096 | bytes 32768 | tf_op jit(solution)/shard_map/psum | solution.py:133
  168.1 11.2 %convert_multiply_fusion = f32[32,128,1024]{1,2,0:T(8,128)} fusion(bf16[32,128,1024]{1,2,0:T(8,128)(2,1)} %copy.55, f32[32,128]{1,0:T(8,128)S(1)} %add_rsqrt_fusion), kind=kLoop, calls=%fused_computation.18 | loop fusion | flops 8388608 | bytes 25182208 | tf_op jit(solution)/shard_map/mul | solution.py:18
  179.3 6.4 %slice.33 = bf16[32,128,4,1,128]{1,4,3,2,0:T(8,128)(2,1)} slice(f32[32,128,4,2,128]{1,4,3,2,0:T(8,128)} %bitcast.116), slice={[0:32], [0:128], [0:4], [0:1], [0:128]} | slice | bytes 8388608 | tf_op jit(solution)/shard_map/slice | solution.py:20
  185.6 6.4 %copy.71 = bf16[32,128,4,1,128]{4,1,2,0,3:T(8,128)(2,1)} copy(bf16[32,128,4,1,128]{1,4,3,2,0:T(8,128)(2,1)} %slice.33) | data formatting | bytes 8388608
  197.7 7.2 %bitcast_reduce_fusion.1 = (bf16[32,64,4]{1,2,0:T(4,128)(2,1)S(1)}, f32[32,4,128,64]{2,3,1,0:T(8,128)}) fusion(bf16[32,64,4,128]{3,1,2,0:T(8,128)(2,1)S(1)} %gather_fusion, bf16[32,128,4,1,128]{4,1,2,0,3:T(8,128)(2,1)} %copy.71), kind=kOutput, calls=%fused_computation.35 | convolution fusion | flops 270524416 | bytes 10502144 | tf_op jit(solution)/shard_map/ithd,irhd->ithr/dot_general | solution.py:36
  211.4 6.0 fusion.44
  217.4 7.1 %fusion.3 = bf16[32,128,4,128]{1,3,2,0:T(8,128)(2,1)} fusion(f32[32,128,4,2,128]{1,4,3,2,0:T(8,128)} %bitcast.117, bf16[32,64,4,128]{3,1,2,0:T(8,128)(2,1)S(1)} %gather_fusion, f32[32,128,4,64]{1,3,2,0:T(8,128)S(1)} %get-tuple-element.9, f32[32,128,4]{1,2,0:T(4,128)S(1)} %get-tuple-element.8), kind=kOutput, calls=%fused_computation.23 | convolution fusion | flops 274726912 | bytes 18939904 | tf_op jit(solution)/shard_map/irht,ithd->irhd/dot_general | solution.py:26
  224.5 7.5 %all-to-all-done.6 = bf16[64,64,4,128]{3,1,2,0:T(8,128)(2,1)} async-done(((bf16[64,64,4,128]{3,1,2,0:T(8,128)(2,1)}), bf16[64,64,4,128]{3,1,2,0:T(8,128)(2,1)}, u32[]{:S(2)}, u32[]{:S(2)}) %all-to-all-start.6) | async-done | bytes 4194336 | tf_op jit(solution)/shard_map/all_to_all | solution.py:161
  232.0 5.8 all-to-all-start.2
  247.0 6.5 %all-to-all-start.3 = ((bf16[64,2,128]{2,1,0:T(2,128)(2,1)}), bf16[64,2,128]{2,1,0:T(2,128)(2,1)S(1)}, u32[]{:S(2)}, u32[]{:S(2)}) async-start(bf16[64,2,128]{2,1,0:T(2,128)(2,1)} %reshape.392), calls=%async_computation.3 | async-start | bytes 65536 | tf_op jit(solution)/shard_map/all_to_all | solution.py:148
  253.5 7.6 %convert_bitcast_fusion = bf16[32,64,4,128]{3,1,2,0:T(8,128)(2,1)S(1)} fusion(bf16[32,128,4,128]{1,3,2,0:T(8,128)(2,1)} %fusion.3, f32[32,4,128,64]{2,3,1,0:T(8,128)} %get-tuple-element.7, f32[32,64,4]{1,2,0:T(4,128)S(1)} %convert_element_type.116), kind=kOutput, calls=%fused_computation.54 | convolution fusion | flops 272629760 | bytes 10518528 | tf_op jit(solution)/shard_map/ithr,irhd->ithd/dot_general | solution.py:42
  264.1 10.5 %all-to-all-start.4 = ((bf16[64,64,4,128]{3,1,2,0:T(8,128)(2,1)}), bf16[64,64,4,128]{3,1,2,0:T(8,128)(2,1)}, u32[]{:S(2)}, u32[]{:S(2)}) async-start(bf16[64,64,4,128]{3,1,2,0:T(8,128)(2,1)} %gather_fusion.5), calls=%async_computation.4 | async-start | bytes 8388608 | tf_op jit(solution)/shard_map/all_to_all | solution.py:146
  282.4 88.1 %all-to-all-done.4 = bf16[64,64,4,128]{3,1,2,0:T(8,128)(2,1)} async-done(((bf16[64,64,4,128]{3,1,2,0:T(8,128)(2,1)}), bf16[64,64,4,128]{3,1,2,0:T(8,128)(2,1)}, u32[]{:S(2)}, u32[]{:S(2)}) %all-to-all-start.4) | async-done | bytes 4194336 | tf_op jit(solution)/shard_map/all_to_all | solution.py:146
  385.5 6.5 %all-to-all-start.7 = ((bf16[64,2,128]{2,1,0:T(2,128)(2,1)}), bf16[64,2,128]{2,1,0:T(2,128)(2,1)S(1)}, u32[]{:S(2)}, u32[]{:S(2)}) async-start(bf16[64,2,128]{2,1,0:T(2,128)(2,1)} %reshape.394), calls=%async_computation.7 | async-start | bytes 65536 | tf_op jit(solution)/shard_map/all_to_all | solution.py:163
  392.0 6.6 %fusion.11 = bf16[32,4,128,64]{2,3,1,0:T(8,128)(2,1)S(1)} fusion(bf16[32,128,4,1,128]{4,1,2,0,3:T(8,128)(2,1)} %copy.71, f32[32,4,128,64]{2,3,1,0:T(8,128)} %get-tuple-element.7, bf16[32,64,4,128]{3,1,2,0:T(8,128)(2,1)} %gather_fusion.8, bf16[32,128,4,128]{1,3,2,0:T(8,128)(2,1)} %fusion.3, f32[32,64,4]{1,2,0:T(4,128)S(1)} %convert_element_type.116), kind=kOutput, calls=%fused_computation.37 | convolution fusion | flops 541065216 | bytes 16809984 | tf_op jit(solution)/shard_map/ithr,irhd->ithd/dot_general | solution.py:55
  402.0 7.7 %fusion.6 = f32[32,64,4,128]{3,1,2,0:T(8,128)} fusion(f32[32,64,4]{1,2,0:T(4,128)S(1)} %convert_element_type.137, bf16[32,4,128,64]{2,3,1,0:T(8,128)(2,1)S(1)} %fusion.11, f32[32,64,4]{1,2,0:T(4,128)S(1)} %convert_element_type.130, bf16[32,128,4,1,128]{4,1,2,0,3:T(8,128)(2,1)} %copy.71, f32[32,4,128,64]{2,3,1,0:T(8,128)} %get-tuple-element.7, ...), kind=kOutput, calls=%fused_computation.27 | convolution fusion | flops 278921216 | bytes 14778368 | tf_op jit(solution)/shard_map/ithr,irhd->ithd/dot_general | solution.py:61
  409.7 6.5 %gather_fusion.10 = f32[64,64,4,128]{3,1,2,0:T(8,128)} fusion(f32[32,64,4,128]{3,1,2,0:T(8,128)} %fusion.6, s32[1024]{0:T(1024)S(1)} %pad_clamp_fusion.1), kind=kCustom, calls=%fused_computation.10 | custom fusion | bytes 16777472 | tf_op jit(solution)/shard_map/gather | solution.py:168
  416.1 8.6 %all-to-all-start.8 = ((f32[64,64,4,128]{3,1,2,0:T(8,128)}), f32[64,64,4,128]{3,1,2,0:T(8,128)}, u32[]{:S(2)}, u32[]{:S(2)}) async-start(f32[64,64,4,128]{3,1,2,0:T(8,128)} %gather_fusion.10), calls=%async_computation.8 | async-start | bytes 16777216 | tf_op jit(solution)/shard_map/all_to_all | solution.py:167
  426.0 184.5 %all-to-all-done.8 = f32[64,64,4,128]{3,1,2,0:T(8,128)} async-done(((f32[64,64,4,128]{3,1,2,0:T(8,128)}), f32[64,64,4,128]{3,1,2,0:T(8,128)}, u32[]{:S(2)}, u32[]{:S(2)}) %all-to-all-start.8) | async-done | bytes 8388640 | tf_op jit(solution)/shard_map/all_to_all | solution.py:167
  (77 shorter events, 80.6 us)
Async XLA Ops:
  3.1 22.2 %all-to-all-start.1 = ((s32[64,1,1]{2,1,0:T(1,128)}), s32[64,1,1]{2,1,0:T(1,128)S(1)}, u32[]{:S(2)}, u32[]{:S(2)}) async-start(s32[64,1,1]{2,1,0:T(1,128)} %copy.60), calls=%async_computation.1 | async-start | bytes 65536 | tf_op jit(solution)/shard_map/all_to_all | solution.py:138
  23.7 10.6 %copy-start = (bf16[512,512]{1,0:T(8,128)(2,1)S(1)}, bf16[512,512]{1,0:T(8,128)(2,1)}, u32[]{:S(2)}) copy-start(bf16[512,512]{1,0:T(8,128)(2,1)} %param.5) | copy-start | bytes 1572868
  25.3 104.9 %all-to-all-start = ((bf16[64,64,4,128]{3,1,2,0:T(8,128)(2,1)}), bf16[64,64,4,128]{3,1,2,0:T(8,128)(2,1)}, u32[]{:S(2)}, u32[]{:S(2)}) async-start(bf16[64,64,4,128]{3,1,2,0:T(8,128)(2,1)} %scatter_fusion), calls=%async_computation | async-start | bytes 8388608 | tf_op jit(solution)/shard_map/all_to_all | solution.py:137
  130.2 101.8 %all-to-all-start.6 = ((bf16[64,64,4,128]{3,1,2,0:T(8,128)(2,1)}), bf16[64,64,4,128]{3,1,2,0:T(8,128)(2,1)}, u32[]{:S(2)}, u32[]{:S(2)}) async-start(bf16[64,64,4,128]{3,1,2,0:T(8,128)(2,1)} %scatter_fusion.2), calls=%async_computation.6 | async-start | bytes 8388608 | tf_op jit(solution)/shard_map/all_to_all | solution.py:161
  232.0 15.0 %all-to-all-start.2 = ((bf16[64,2,128]{2,1,0:T(2,128)(2,1)}), bf16[64,2,128]{2,1,0:T(2,128)(2,1)S(1)}, u32[]{:S(2)}, u32[]{:S(2)}) async-start(bf16[64,2,128]{2,1,0:T(2,128)(2,1)} %reshape.390), calls=%async_computation.2 | async-start | bytes 65536 | tf_op jit(solution)/shard_map/all_to_all | solution.py:147
  247.0 17.1 %all-to-all-start.3 = ((bf16[64,2,128]{2,1,0:T(2,128)(2,1)}), bf16[64,2,128]{2,1,0:T(2,128)(2,1)S(1)}, u32[]{:S(2)}, u32[]{:S(2)}) async-start(bf16[64,2,128]{2,1,0:T(2,128)(2,1)} %reshape.392), calls=%async_computation.3 | async-start | bytes 65536 | tf_op jit(solution)/shard_map/all_to_all | solution.py:148
  264.1 106.4 %all-to-all-start.4 = ((bf16[64,64,4,128]{3,1,2,0:T(8,128)(2,1)}), bf16[64,64,4,128]{3,1,2,0:T(8,128)(2,1)}, u32[]{:S(2)}, u32[]{:S(2)}) async-start(bf16[64,64,4,128]{3,1,2,0:T(8,128)(2,1)} %gather_fusion.5), calls=%async_computation.4 | async-start | bytes 8388608 | tf_op jit(solution)/shard_map/all_to_all | solution.py:146
  370.5 15.0 %all-to-all-start.5 = ((bf16[64,2,128]{2,1,0:T(2,128)(2,1)}), bf16[64,2,128]{2,1,0:T(2,128)(2,1)S(1)}, u32[]{:S(2)}, u32[]{:S(2)}) async-start(bf16[64,2,128]{2,1,0:T(2,128)(2,1)} %reshape.396), calls=%async_computation.5 | async-start | bytes 65536 | tf_op jit(solution)/shard_map/all_to_all | solution.py:162
  385.5 15.7 %all-to-all-start.7 = ((bf16[64,2,128]{2,1,0:T(2,128)(2,1)}), bf16[64,2,128]{2,1,0:T(2,128)(2,1)S(1)}, u32[]{:S(2)}, u32[]{:S(2)}) async-start(bf16[64,2,128]{2,1,0:T(2,128)(2,1)} %reshape.394), calls=%async_computation.7 | async-start | bytes 65536 | tf_op jit(solution)/shard_map/all_to_all | solution.py:163
  416.1 194.4 %all-to-all-start.8 = ((f32[64,64,4,128]{3,1,2,0:T(8,128)}), f32[64,64,4,128]{3,1,2,0:T(8,128)}, u32[]{:S(2)}, u32[]{:S(2)}) async-start(f32[64,64,4,128]{3,1,2,0:T(8,128)} %gather_fusion.10), calls=%async_computation.8 | async-start | bytes 16777216 | tf_op jit(solution)/shard_map/all_to_all | solution.py:167
where the time goes:
time: 618 us; the launch traced here: 616 us
  waiting for transfers between devices  381 us (62%)
  local copies, waits for them, and re-layouts  76.3 us (12%)
  starting transfers between devices  71.5 us (12%)
  matrix products  41.2 us (7%)
  other arithmetic  30.6 us (5%)
  blocking collectives  15 us (2%)
    all_to_all x1, waiting for transfers between devices, local(): lax.all_to_all(slot_terms[back_index], 'seq', split_axis=0, concat_axis=0...  185 us
    all_to_all x1, waiting for transfers between devices, local(): lax.all_to_all(query_send, 'seq', split_axis=0, concat_axis=0, tiled=True)  89.2 us
    all_to_all x1, waiting for transfers between devices, local(): lax.all_to_all(partial_out[back_index], 'seq', split_axis=0, concat_axis=...  88.1 us
    unnamed x13, local copies, waits for them, and re-layouts  22.3 us
    psum x1, blocking collectives, local(): row_scale = lax.rsqrt(lax.psum(square_sums, 'head') / D + 1e-06)  15 us
    all_to_all x1, starting transfers between devices, local(): lax.all_to_all(slot_request, 'seq', split_axis=0, concat_axis=0, tiled=True)  13 us
  transfers between devices with their start and end apart: 9, of which 8 were waited for; matrix products, arithmetic and copies ran while one was open for 20% of the time, Pallas kernels for 0%

commit v1 on v0

v1 whole, which is shorter than its diff:
```python
import math

import jax
import jax.numpy as jnp
from jax import lax
from jax.sharding import PartitionSpec as P

D = 4096
HD = 128
SPAN = 64
R = 128
BF = jnp.bfloat16
F32 = jnp.float32


def swap(rows):
    return lax.all_to_all(rows, "seq", split_axis=0, concat_axis=0, tiled=True)


def encode(span_queries, stored, row_scale):
    batch = stored.shape[0]
    heads_here = span_queries.shape[1]
    scale_factor = 1.0 / math.sqrt(HD)
    normed = stored.astype(F32) * row_scale[:, :, None]
    normed = normed.reshape(batch, R, heads_here, 2, HD)
    key_rows = normed[:, :, :, 0, :].astype(BF)
    cond_scores = (
        jnp.einsum("irhd,ihtd->irht", key_rows, span_queries, preferred_element_type=F32)
        * scale_factor
    )
    cond_weights = jax.nn.softmax(cond_scores, axis=-1).astype(BF)
    conditioned = jnp.einsum(
        "irht,ihtd->irhd", cond_weights, span_queries, preferred_element_type=F32
    )
    value_rows = (normed[:, :, :, 1, :] + conditioned).astype(BF)
    return key_rows, value_rows


def attend(span_queries, key_rows, value_rows):
    scale_factor = 1.0 / math.sqrt(HD)
    scores = (
        jnp.einsum("ihtd,irhd->ihtr", span_queries, key_rows, preferred_element_type=F32)
        * scale_factor
    )
    row_top = jnp.max(scores, axis=-1).astype(BF)
    exponent = jnp.exp(scores - lax.optimization_barrier(row_top).astype(F32)[..., None])
    row_total = jnp.sum(exponent, axis=-1).astype(BF)
    low = exponent.astype(BF)
    partial_out = jnp.einsum(
        "ihtr,irhd->ihtd", low, value_rows, preferred_element_type=F32
    ).astype(BF)
    term_b = jnp.einsum("ihtr,irhd->ihtd", low, key_rows, preferred_element_type=F32).astype(BF)
    return exponent, row_top, row_total, partial_out, term_b


def back_term(exponent, key_rows, value_rows, grad_rows):
    prob_grad = jnp.einsum("ihtd,irhd->ihtr", grad_rows, value_rows, preferred_element_type=F32)
    return jnp.einsum(
        "ihtr,irhd->ihtd", (exponent * prob_grad).astype(BF), key_rows, preferred_element_type=F32
    ).astype(BF)


def local(queries, out_grad, neighbours, placement):
    n = lax.axis_size("seq")
    width = queries.shape[1]
    heads = width // HD
    spans = placement.shape[0]
    slots = neighbours.shape[0]
    scale_factor = 1.0 / math.sqrt(HD)
    unit = SPAN * heads // n
    blocks = SPAN // unit
    all_spans, all_slots = n * spans, n * slots

    def to_pieces(rows):
        cut = rows.reshape(spans, blocks, unit, heads, HD)
        return cut.transpose(3, 1, 0, 2, 4).reshape(n, spans * unit, HD)

    pair = lax.all_gather(placement, "seq", axis=0, tiled=True)
    square_sums = jnp.sum(jnp.square(neighbours.astype(F32)), axis=-1)
    row_scale = lax.rsqrt(lax.psum(square_sums, "head") / D + 1e-06)

    first = swap(jnp.stack([to_pieces(queries), to_pieces(out_grad)], axis=1))
    first = first.reshape(n, 2, spans, unit * HD)
    q_piece = first[:, 0].reshape(all_spans, unit * HD)
    g_piece = first[:, 1].reshape(all_spans, unit * HD)

    slot_ids = jnp.arange(all_slots, dtype=jnp.int32)
    hit_a = (pair[:, 0][:, None] == slot_ids[None, :]).astype(BF)
    hit_b = (pair[:, 1][:, None] == slot_ids[None, :]).astype(BF)
    hit = hit_a + hit_b

    def to_owners(piece):
        picked = jnp.einsum("cs,cw->sw", hit, piece, preferred_element_type=F32).astype(BF)
        got = swap(picked.reshape(n, slots * unit, HD))
        got = got.reshape(n, slots, unit, HD).transpose(1, 0, 2, 3)
        return got.reshape(slots, heads, SPAN, HD)

    slot_queries = to_owners(q_piece)
    slot_grads = to_owners(g_piece)
    key_rows, value_rows = encode(slot_queries, neighbours, row_scale)
    exponent, top, total, partial_out, term_b = attend(slot_queries, key_rows, value_rows)

    def by_piece(rows):
        return rows.reshape(slots, n, unit * HD).transpose(1, 0, 2).reshape(n, slots * unit, HD)

    def stat_rows(rows):
        return rows.reshape(slots, n, unit).transpose(1, 0, 2).reshape(n, 1, slots * unit)

    back = swap(
        jnp.concatenate([by_piece(partial_out), stat_rows(top), stat_rows(total)], axis=1)
    )
    term_a = back_term(exponent, key_rows, value_rows, slot_grads)

    got_part = back[:, : slots * unit].reshape(all_slots, unit * HD)
    got_stat = back[:, slots * unit :].reshape(n, 2, slots, unit)
    got_stat = got_stat.transpose(0, 2, 1, 3).reshape(all_slots, 2 * unit)

    def pick(mask, rows):
        return jnp.einsum("cs,sw->cw", mask, rows, preferred_element_type=F32)

    part = [pick(m, got_part).reshape(all_spans, unit, HD) for m in (hit_a, hit_b)]
    stat = [pick(m, got_stat).reshape(all_spans, 2, unit) for m in (hit_a, hit_b)]
    tops = [s[:, 0] for s in stat]
    totals = [s[:, 1] for s in stat]
    highest = jnp.maximum(tops[0], tops[1])
    factor = [jnp.exp(t - highest) for t in tops]
    denominator = factor[0] * totals[0] + factor[1] * totals[1]
    low = [lax.optimization_barrier((f / denominator).astype(BF)) for f in factor]
    weight = [v.astype(F32) for v in low]
    attended = (weight[0][..., None] * part[0] + weight[1][..., None] * part[1]).astype(BF)
    grads = g_piece.reshape(all_spans, unit, HD).astype(F32)
    products = [jnp.sum(grads * p, axis=-1) for p in part]
    delta = (weight[0] * products[0] + weight[1] * products[1]).astype(BF)
    w_slot = jnp.einsum("cs,cw->sw", hit_a, low[0], preferred_element_type=F32) + jnp.einsum(
        "cs,cw->sw", hit_b, low[1], preferred_element_type=F32
    )
    d_slot = jnp.einsum("cs,cw->sw", hit, delta, preferred_element_type=F32)
    wd = jnp.stack(
        [w_slot.astype(BF).reshape(n, slots * unit), d_slot.astype(BF).reshape(n, slots * unit)],
        axis=1,
    )
    wd = swap(wd).reshape(n, 2, slots, unit).transpose(1, 2, 0, 3).reshape(2, slots, heads, SPAN)
    wd = wd.astype(F32)[..., None]
    terms = (
        wd[0] * (term_a.astype(F32) - wd[1] * term_b.astype(F32)) * scale_factor
    ).astype(BF)
    got_terms = swap(by_piece(terms)).reshape(all_slots, unit * HD)
    query_grad = pick(hit, got_terms).astype(BF)
    final = jnp.stack(
        [
            attended.reshape(n, spans * unit, HD),
            query_grad.reshape(n, spans * unit, HD),
        ],
        axis=1,
    )
    final = swap(final).reshape(heads, blocks, 2, spans, unit, HD)
    final = final.transpose(2, 3, 1, 4, 0, 5).reshape(2, spans * SPAN, width)
    return final[0], final[1]


def solution(mesh):
    in_specs = (P("seq", "head"), P("seq", "head"), P("seq", None, "head"), P("seq", None))
    out_specs = (P("seq", "head"), P("seq", "head"))
    return jax.shard_map(local, mesh=mesh, in_specs=in_specs, out_specs=out_specs, check_vma=False)
```

time: 618 us -> 473 us (0.77); the launches traced: 616 us -> 465 us
  waiting for transfers between devices: 381 us -> 125 us
  blocking collectives: 15 us -> 110 us
  local copies, waits for them, and re-layouts: 76.3 us -> 99.2 us
  starting transfers between devices: 71.5 us -> 57 us
    all_to_all x9 -> x6, waiting for transfers between devices: 381 us -> 125 us  [swap(): return lax.all_to_all(rows, 'seq', split_axis=0, concat_axis=0, tiled=True)]
    all_gather x0 -> x1, blocking collectives: none -> 61.2 us  [local(): pair = lax.all_gather(placement, 'seq', axis=0, tiled=True)]
    reshape x6 -> x17, local copies, waits for them, and re-layouts: 1.69 us -> 50.1 us  [the longest x6 31.2 us: by_piece(): rows.reshape(slots, n, unit * HD).transpose(1, 0, 2)]
    all_to_all x0 -> x1, blocking collectives: none -> 34.2 us  [swap(): return lax.all_to_all(rows, 'seq', split_axis=0, concat_axis=0, tiled=True)]
    gather x12 -> x0, local copies, waits for them, and re-layouts: 27.8 us -> none  [the longest x1 6.49 us: local(): slot_terms[back_index]]
    all_to_all x9 -> x6, starting transfers between devices: 71.5 us -> 57 us  [swap(): return lax.all_to_all(rows, 'seq', split_axis=0, concat_axis=0, tiled=True)]
    scatter x5 -> x0, local copies, waits for them, and re-layouts: 8.66 us -> none  [the longest x4 8.04 us: spread(): jnp.zeros((total_count,) + rows_in.shape[1:], rows_in.dtype).at[target]]
    dot_general x6 -> x15, matrix products: 41.2 us -> 44.9 us  [the longest x5 9.85 us: pick(): return jnp.einsum('cs,sw->cw', mask, rows, preferred_element_type=F32)]
  transfers between devices with their start and end apart: 9 -> 6, of which waited for: 8 -> 3; matrix products, arithmetic and copies ran while one was open for 20% -> 18% of each run, Pallas kernels for 0% -> 0%
where the time goes in v1:
time: 473 us; the launch traced here: 465 us
  waiting for transfers between devices  125 us (26%)
  blocking collectives  110 us (23%)
  local copies, waits for them, and re-layouts  99.2 us (21%)
  starting transfers between devices  57 us (12%)
  matrix products  44.9 us (9%)
  other arithmetic  26.5 us (6%)
    all_to_all x6, waiting for transfers between devices, swap(): return lax.all_to_all(rows, 'seq', split_axis=0, concat_axis=0, tiled=True)  125 us
    all_gather x1, blocking collectives, local(): pair = lax.all_gather(placement, 'seq', axis=0, tiled=True)  61.2 us
    all_to_all x6, starting transfers between devices, swap(): return lax.all_to_all(rows, 'seq', split_axis=0, concat_axis=0, tiled=True)  57 us
    all_to_all x1, blocking collectives, swap(): return lax.all_to_all(rows, 'seq', split_axis=0, concat_axis=0, tiled=True)  34.2 us
    reshape x6, local copies, waits for them, and re-layouts, by_piece(): rows.reshape(slots, n, unit * HD).transpose(1, 0, 2)  31.2 us
    unnamed x19, local copies, waits for them, and re-layouts  21.8 us
    psum x1, blocking collectives, local(): row_scale = lax.rsqrt(lax.psum(square_sums, 'head') / D + 1e-06)  14.9 us
    mul x1, other arithmetic, encode(): normed = stored.astype(F32) * row_scale[:, :, None]  11.2 us
  transfers between devices with their start and end apart: 6, of which 3 were waited for; matrix products, arithmetic and copies ran while one was open for 18% of the time, Pallas kernels for 0%

profile of v1, /device:TPU:1, one launch (start us, length us, event | category | flops | bytes accessed | tf_op | source)
XLA Modules:
  0.0 464.7 jit_solution(7035936152062735313)
XLA Ops:
  5.0 13.0 %all-to-all-start = ((bf16[64,2,32,128]{3,2,1,0:T(8,128)(2,1)}), bf16[64,2,32,128]{3,2,1,0:T(8,128)(2,1)S(1)}, u32[]{:S(2)}, u32[]{:S(2)}) async-start(bf16[64,2,32,128]{3,2,1,0:T(8,128)(2,1)} %copy.75), calls=%async_computation | async-start | bytes 2097152 | tf_op jit(solution)/shard_map/all_to_all | solution.py:17
  18.0 61.2 %all-gather = s32[64,8,2]{1,2,0:T(2,128)S(1)} all-gather(s32[1,8,2]{1,2,0:T(2,128)S(1)} %bitcast.218), channel_id=1, replica_groups=mesh['seq'=64,'head'=4] {'seq'}, dimensions={0}, use_global_device_ids=true | all-gather | bytes 4160 | tf_op jit(solution)/shard_map/all_gather | solution.py:78
  84.4 8.5 %all-to-all-start.1 = ((bf16[64,128,128]{2,1,0:T(8,128)(2,1)}), bf16[64,128,128]{2,1,0:T(8,128)(2,1)S(1)}, u32[]{:S(2)}, u32[]{:S(2)}) async-start(bf16[64,128,128]{2,1,0:T(8,128)(2,1)} %reshape.113), calls=%async_computation.1 | async-start | bytes 4194304 | tf_op jit(solution)/shard_map/all_to_all | solution.py:17
  92.9 12.0 %copy.77 = bf16[32,128,1024]{1,2,0:T(8,128)(2,1)} copy(bf16[32,128,1024]{2,1,0:T(8,128)(2,1)} %param.6) | data formatting | bytes 16777216 | tf_op args[2]
  104.8 5.0 %fusion.1 = f32[32,128]{1,0:T(8,128)S(1)} fusion(bf16[32,128,1024]{1,2,0:T(8,128)(2,1)} %copy.77), kind=kLoop, calls=%fused_computation.3 | loop fusion | flops 12578816 | bytes 8404992 | tf_op jit(solution)/shard_map/reduce_sum | solution.py:79
  109.8 14.9 %psum.7 = f32[32,128]{1,0:T(8,128)S(1)} all-reduce(f32[32,128]{1,0:T(8,128)S(1)} %fusion.1), channel_id=1, replica_groups=mesh['seq'=64,'head'=4] {'head'}, use_global_device_ids=true, to_apply=%region_1.0 | all-reduce | flops 4096 | bytes 32768 | tf_op jit(solution)/shard_map/psum | solution.py:80
  124.8 11.2 %convert_multiply_fusion = f32[32,128,1024]{1,2,0:T(8,128)} fusion(bf16[32,128,1024]{1,2,0:T(8,128)(2,1)} %copy.77, f32[32,128]{1,0:T(8,128)S(1)} %add_rsqrt_fusion), kind=kLoop, calls=%fused_computation.1 | loop fusion | flops 8388608 | bytes 25182208 | tf_op jit(solution)/shard_map/mul | solution.py:24
  135.9 6.4 %slice.74 = bf16[32,128,4,1,128]{1,4,3,2,0:T(8,128)(2,1)} slice(f32[32,128,4,2,128]{1,4,3,2,0:T(8,128)} %bitcast.175), slice={[0:32], [0:128], [0:4], [0:1], [0:128]} | slice | bytes 8388608 | tf_op jit(solution)/shard_map/slice | solution.py:26
  142.3 6.4 %copy.113 = bf16[32,128,4,1,128]{4,1,2,0,3:T(8,128)(2,1)} copy(bf16[32,128,4,1,128]{1,4,3,2,0:T(8,128)(2,1)} %slice.74) | data formatting | bytes 8388608
  152.9 5.0 %multiply_reduce_fusion = (bf16[32,4,64]{2,1,0:T(4,128)(2,1)S(1)}, f32[32,4,64,128]{3,2,1,0:T(8,128)}) fusion(bf16[32,4,64,128]{3,2,1,0:T(8,128)(2,1)S(1)} %bitcast.177, bf16[32,128,4,1,128]{4,1,2,0,3:T(8,128)(2,1)S(1)} %copy-done.1), kind=kOutput, calls=%fused_computation.38 | convolution fusion | flops 270524416 | bytes 10502144 | tf_op jit(solution)/shard_map/ihtd,irhd->ihtr/dot_general | solution.py:42
  158.0 4.8 %fusion.84 = (f32[32,128,4]{1,2,0:T(4,128)S(1)}, f32[32,128,4,64]{1,3,2,0:T(8,128)S(1)}) fusion(f32[32,4,64,128]{3,2,1,0:T(8,128)} %get-tuple-element.14), kind=kOutput, calls=%fused_computation.106 | output fusion | flops 4194367 | bytes 8454144 | tf_op jit(solution)/shard_map/sub | solution.py:31
  165.3 5.2 %fusion.3 = bf16[32,128,4,128]{1,3,2,0:T(8,128)(2,1)S(1)} fusion(f32[32,128,4,2,128]{1,4,3,2,0:T(8,128)} %bitcast.176, bf16[32,4,64,128]{3,2,1,0:T(8,128)(2,1)S(1)} %bitcast.178, f32[32,128,4,64]{1,3,2,0:T(8,128)S(1)} %get-tuple-element.16, f32[32,128,4]{1,2,0:T(4,128)S(1)} %get-tuple-element.15), kind=kOutput, calls=%fused_computation.6 | convolution fusion | flops 274726912 | bytes 18939904 | tf_op jit(solution)/shard_map/irht,ihtd->irhd/dot_general | solution.py:32
  175.7 14.1 %reshape.117 = bf16[32,64,512]{2,1,0:T(8,128)(2,1)} reshape(bf16[32,4,64,128]{3,2,1,0:T(8,128)(2,1)S(1)} %convolution_convert_fusion.3) | data formatting | bytes 4194304 | tf_op jit(solution)/shard_map/reshape | solution.py:104
  199.3 12.9 %all-to-all-start.2 = ((bf16[64,130,128]{2,1,0:T(8,128)(2,1)}), bf16[64,130,128]{2,1,0:T(8,128)(2,1)S(1)}, u32[]{:S(2)}, u32[]{:S(2)}) async-start(bf16[64,130,128]{2,1,0:T(8,128)(2,1)} %pad_maximum_fusion), calls=%async_computation.2 | async-start | bytes 4456448 | tf_op jit(solution)/shard_map/all_to_all | solution.py:17
  215.3 4.4 reshape.124
  219.7 46.3 %all-to-all-done.2 = bf16[64,130,128]{2,1,0:T(8,128)(2,1)S(1)} async-done(((bf16[64,130,128]{2,1,0:T(8,128)(2,1)}), bf16[64,130,128]{2,1,0:T(8,128)(2,1)S(1)}, u32[]{:S(2)}, u32[]{:S(2)}) %all-to-all-start.2) | async-done | bytes 2129952 | tf_op jit(solution)/shard_map/all_to_all | solution.py:17
  266.0 6.2 %all-to-all-start.4 = ((bf16[64,128,128]{2,1,0:T(8,128)(2,1)}), bf16[64,128,128]{2,1,0:T(8,128)(2,1)}, u32[]{:S(2)}, u32[]{:S(2)}) async-start(bf16[64,128,128]{2,1,0:T(8,128)(2,1)} %reshape.124), calls=%async_computation.4 | async-start | bytes 4194304 | tf_op jit(solution)/shard_map/all_to_all | solution.py:17
  295.2 28.2 %all-to-all-done.4 = bf16[64,128,128]{2,1,0:T(8,128)(2,1)} async-done(((bf16[64,128,128]{2,1,0:T(8,128)(2,1)}), bf16[64,128,128]{2,1,0:T(8,128)(2,1)}, u32[]{:S(2)}, u32[]{:S(2)}) %all-to-all-start.4) | async-done | bytes 2097184 | tf_op jit(solution)/shard_map/all_to_all | solution.py:17
  323.4 6.1 %all-to-all-start.3 = ((bf16[64,2,128]{2,1,0:T(2,128)(2,1)}), bf16[64,2,128]{2,1,0:T(2,128)(2,1)S(1)}, u32[]{:S(2)}, u32[]{:S(2)}) async-start(bf16[64,2,128]{2,1,0:T(2,128)(2,1)} %copy.96), calls=%async_computation.3 | async-start | bytes 65536 | tf_op jit(solution)/shard_map/all_to_all | solution.py:17
  329.5 5.4 %fusion.6 = bf16[32,4,64,128]{3,2,1,0:T(8,128)(2,1)S(1)} fusion(f32[32,4,64,128]{3,2,1,0:T(8,128)} %get-tuple-element.14, f32[32,4,64]{2,1,0:T(4,128)S(1)} %convert_element_type.116, bf16[32,128,4,1,128]{4,1,2,0,3:T(8,128)(2,1)} %copy.113), kind=kOutput, calls=%fused_computation.11 | convolution fusion | flops 271581184 | bytes 10518528 | tf_op jit(solution)/shard_map/ihtr,irhd->ihtd/dot_general | solution.py:52
  341.2 8.5 %multiply_convert_fusion = bf16[32,4,64,128]{3,2,1,0:T(8,128)(2,1)} fusion(bf16[32,4,64,128]{3,2,1,0:T(8,128)(2,1)S(1)} %fusion.6, f32[32,4,64]{2,1,0:T(4,128)S(1)} %copy.105, f32[32,4,64]{2,1,0:T(4,128)S(1)} %copy.99, f32[32,4,64,128]{3,2,1,0:T(8,128)} %get-tuple-element.14, bf16[32,128,4,128]{1,3,2,0:T(8,128)(2,1)} %copy-done.3, ...), kind=kOutput, calls=%fused_computation.17 | convolution fusion | flops 549453824 | bytes 18972672 | tf_op jit(solution)/shard_map/ihtr,irhd->ihtd/dot_general | solution.py:58
  359.6 10.3 %all-to-all-start.5 = ((bf16[64,128,128]{2,1,0:T(8,128)(2,1)}), bf16[64,128,128]{2,1,0:T(8,128)(2,1)S(1)}, u32[]{:S(2)}, u32[]{:S(2)}) async-start(bf16[64,128,128]{2,1,0:T(8,128)(2,1)} %reshape.128), calls=%async_computation.5 | async-start | bytes 4194304 | tf_op jit(solution)/shard_map/all_to_all | solution.py:17
  370.4 50.8 %all-to-all-done.5 = bf16[64,128,128]{2,1,0:T(8,128)(2,1)S(1)} async-done(((bf16[64,128,128]{2,1,0:T(8,128)(2,1)}), bf16[64,128,128]{2,1,0:T(8,128)(2,1)S(1)}, u32[]{:S(2)}, u32[]{:S(2)}) %all-to-all-start.5) | async-done | bytes 2097184 | tf_op jit(solution)/shard_map/all_to_all | solution.py:17
  427.2 34.2 %all_to_all.35 = bf16[64,2,32,128]{3,2,1,0:T(8,128)(2,1)S(1)} all-to-all(bf16[64,2,32,128]{3,2,1,0:T(8,128)(2,1)S(1)} %copy.107), channel_id=1, replica_groups=mesh['seq'=64,'head'=4] {'seq'}, dimensions={0} | all-to-all | bytes 2097152 | tf_op jit(solution)/shard_map/all_to_all | solution.py:17
  (94 shorter events, 82.3 us)
Async XLA Ops:
  1.9 16.1 %copy-start.7 = (s32[8,2]{0,1:T(2,128)S(1)}, s32[8,2]{0,1:T(2,128)}, u32[]{:S(2)}) copy-start(s32[8,2]{0,1:T(2,128)} %param.7) | copy-start | bytes 196
  5.0 74.3 %all-to-all-start = ((bf16[64,2,32,128]{3,2,1,0:T(8,128)(2,1)}), bf16[64,2,32,128]{3,2,1,0:T(8,128)(2,1)S(1)}, u32[]{:S(2)}, u32[]{:S(2)}) async-start(bf16[64,2,32,128]{3,2,1,0:T(8,128)(2,1)} %copy.75), calls=%async_computation | async-start | bytes 2097152 | tf_op jit(solution)/shard_map/all_to_all | solution.py:17
  80.0 132.2 %copy-start.4 = (bf16[64,2,8,512]{3,2,1,0:T(8,128)(2,1)}, bf16[64,2,8,512]{3,2,1,0:T(8,128)(2,1)S(1)}, u32[]{:S(2)}) copy-start(bf16[64,2,8,512]{3,2,1,0:T(8,128)(2,1)S(1)} %reshape.112) | copy-start | bytes 3145732
  84.4 64.4 %all-to-all-start.1 = ((bf16[64,128,128]{2,1,0:T(8,128)(2,1)}), bf16[64,128,128]{2,1,0:T(8,128)(2,1)S(1)}, u32[]{:S(2)}, u32[]{:S(2)}) async-start(bf16[64,128,128]{2,1,0:T(8,128)(2,1)} %reshape.113), calls=%async_computation.1 | async-start | bytes 4194304 | tf_op jit(solution)/shard_map/all_to_all | solution.py:17
  148.7 1.3 copy-start.2
  150.1 2.8 copy-start.1
  158.0 4.8 %copy-start = (f32[32,4,64,128]{3,2,1,0:T(8,128)S(1)}, f32[32,4,64,128]{3,2,1,0:T(8,128)}, u32[]{:S(2)}) copy-start(f32[32,4,64,128]{3,2,1,0:T(8,128)} %get-tuple-element.14) | copy-start | bytes 12582916
  170.5 1.9 copy-start.3
  199.3 66.7 %all-to-all-start.2 = ((bf16[64,130,128]{2,1,0:T(8,128)(2,1)}), bf16[64,130,128]{2,1,0:T(8,128)(2,1)S(1)}, u32[]{:S(2)}, u32[]{:S(2)}) async-start(bf16[64,130,128]{2,1,0:T(8,128)(2,1)} %pad_maximum_fusion), calls=%async_computation.2 | async-start | bytes 4456448 | tf_op jit(solution)/shard_map/all_to_all | solution.py:17
  266.0 57.4 %all-to-all-start.4 = ((bf16[64,128,128]{2,1,0:T(8,128)(2,1)}), bf16[64,128,128]{2,1,0:T(8,128)(2,1)}, u32[]{:S(2)}, u32[]{:S(2)}) async-start(bf16[64,128,128]{2,1,0:T(8,128)(2,1)} %reshape.124), calls=%async_computation.4 | async-start | bytes 4194304 | tf_op jit(solution)/shard_map/all_to_all | solution.py:17
  287.0 3.0 copy-start.5
  287.0 3.1 copy-start.6
  323.4 17.2 %all-to-all-start.3 = ((bf16[64,2,128]{2,1,0:T(2,128)(2,1)}), bf16[64,2,128]{2,1,0:T(2,128)(2,1)S(1)}, u32[]{:S(2)}, u32[]{:S(2)}) async-start(bf16[64,2,128]{2,1,0:T(2,128)(2,1)} %copy.96), calls=%async_computation.3 | async-start | bytes 65536 | tf_op jit(solution)/shard_map/all_to_all | solution.py:17
  359.6 61.6 %all-to-all-start.5 = ((bf16[64,128,128]{2,1,0:T(8,128)(2,1)}), bf16[64,128,128]{2,1,0:T(8,128)(2,1)S(1)}, u32[]{:S(2)}, u32[]{:S(2)}) async-start(bf16[64,128,128]{2,1,0:T(8,128)(2,1)} %reshape.128), calls=%async_computation.5 | async-start | bytes 4194304 | tf_op jit(solution)/shard_map/all_to_all | solution.py:17

commit v2 on v1

v2 whole, which is shorter than its diff:
```python
import functools
import math

import jax
import jax.numpy as jnp
from jax import lax
from jax.experimental import pallas as pl
from jax.experimental.pallas import tpu as pltpu
from jax.sharding import PartitionSpec as P

D = 4096
HD = 128
SPAN = 64
R = 128
N = 64
C = 8
S = 32
H = 4
U = 4
TB = SPAN // U
W = U * HD
SPANS = N * C
SLOTS = N * S
HALF = S // 2
SCALE = 1.0 / math.sqrt(HD)
BF = jnp.bfloat16
F32 = jnp.float32
MIB = 1 << 20


def iota(shape, dim):
    return lax.broadcasted_iota(jnp.int32, shape, dim)


def hot(mask):
    return jnp.where(mask, 1.0, 0.0).astype(BF)


def mm(a, b):
    return jnp.dot(a, b, preferred_element_type=F32)


def mm_t(a, b):
    return lax.dot_general(a, b, (((1,), (1,)), ((), ())), preferred_element_type=F32)


def t_mm(a, b):
    return lax.dot_general(a, b, (((0,), (0,)), ((), ())), preferred_element_type=F32)


def call(body, out_shape, flops=1e8, nbytes=4e6, vmem=40, **kw):
    return pl.pallas_call(
        body,
        out_shape=out_shape,
        compiler_params=pltpu.CompilerParams(vmem_limit_bytes=vmem * MIB),
        cost_estimate=pl.CostEstimate(
            flops=int(flops), bytes_accessed=int(nbytes), transcendentals=0
        ),
        **kw,
    )


def sds(shape, dtype):
    return jax.ShapeDtypeStruct(shape, dtype)


def token_row(piece_row):
    return (piece_row % C) * SPAN + ((piece_row // C) % U) * TB + piece_row // (U * C)


def prep_body(q_ref, g_ref, digits_ref, out_ref):
    size = C * SPAN
    order = hot(iota((size, size), 1) == token_row(iota((size, size), 0)))
    for base, ref in ((0, q_ref), (U * C, g_ref)):
        rows = mm(order, ref[...]).astype(BF)
        for h in range(H):
            out_ref[h * TB : (h + 1) * TB, base : base + U * C, :] = rows[
                :, h * HD : (h + 1) * HD
            ].reshape(TB, U * C, HD)
    out_ref[:, 2 * U * C :, :] = jnp.broadcast_to(digits_ref[...][None], (N, C, HD))


def final_body(in_ref, att_ref, qg_ref):
    size = C * SPAN
    order = hot(iota((size, size), 0) == token_row(iota((size, size), 1)))
    for base, ref in ((0, att_ref), (U * C, qg_ref)):
        cat = jnp.concatenate(
            [
                in_ref[h * TB : (h + 1) * TB, base : base + U * C, :].reshape(size, HD)
                for h in range(H)
            ],
            axis=1,
        )
        ref[...] = mm(order, cat).astype(BF)


def span_rows(block):
    wide = block.astype(F32)
    return [wide[:, u * C : (u + 1) * C, :].reshape(SPANS, HD) for u in range(U)]


def route_body(base, first_ref, out_ref, row_ref, col_ref, x_ref):
    digits = first_ref[:, 2 * U * C :, :].astype(F32).reshape(SPANS, HD)
    lane = iota((SPANS, HD), 1)
    slot_part = pltpu.roll(digits, HD - 2, 1)
    cols = jnp.where(lane < 2, digits * float(S) + slot_part, 0.0)
    cols = cols + jnp.where((lane >= 2) & (lane < 6), pltpu.roll(digits, 2, 1), 0.0)
    col_ref[...] = cols
    rows = jnp.transpose(cols)[:8]
    row_ref[...] = rows
    for u, part in enumerate(span_rows(first_ref[:, base : base + U * C, :])):
        x_ref[:, u * HD : (u + 1) * HD] = part.astype(BF)
    per = 8
    slot_a = rows[0:1]
    slot_b = rows[1:2]

    def step(j, _):
        ids = (iota((per * S, SPANS), 0) + j * (per * S)).astype(F32)
        hit = hot((ids == slot_a) | (ids == slot_b))
        got = mm(hit, x_ref[...]).astype(BF)
        at = pl.ds(pl.multiple_of(j * per, per), per)
        for u in range(U):
            out_ref[at, u * S : (u + 1) * S, :] = got[:, u * HD : (u + 1) * HD].reshape(
                per, S, HD
            )
        return 0

    lax.fori_loop(0, N // per, step, 0)


def swap_order():
    size = TB * HALF
    a, b = iota((size, size), 0), iota((size, size), 1)
    return hot((a // TB == b % TB) & (a % TB == b // TB))


def to_slots(order, src_ref, dst_ref):
    for h in range(H):
        pair, i = h // 2, h % 2
        for u in range(0, U, 2):
            block = jnp.concatenate(
                [
                    src_ref[h * TB : (h + 1) * TB, v, :, :].reshape(TB * HALF, HD)
                    for v in (u, u + 1)
                ],
                axis=1,
            )
            rows = mm(order, block).astype(BF)
            for j in range(2):
                lo = i * SPAN + (u + j) * TB
                dst_ref[:, pair, lo : lo + TB, i * HD : (i + 1) * HD] = rows[
                    :, j * HD : (j + 1) * HD
                ].reshape(HALF, TB, HD)


def forward_body(
    q_ref, nb_ref, rs_ref, e_ref, k_ref, v_ref, p_ref, b_ref, stat_ref, qs, pbs, tops, totals
):
    step = pl.program_id(0)
    order = swap_order()

    @pl.when(step == 0)
    def _():
        tops[...] = jnp.zeros_like(tops)
        totals[...] = jnp.zeros_like(totals)
        qs[...] = jnp.zeros_like(qs)

    to_slots(order, q_ref, qs)
    row = iota((2 * SPAN, HD), 0) % SPAN

    def slot(s, _):
        at = step * HALF + s
        scale = jnp.sum(
            jnp.where(iota((R, HD), 1) == at, rs_ref[...], 0.0), axis=1, keepdims=True
        )
        mark = iota((2 * SPAN, HD), 1) == (row // TB) * S + at
        for pair in range(H // 2):
            lo = 4 * pair * HD
            part = [
                nb_ref[s, :, lo + i * HD : lo + (i + 1) * HD].astype(F32) * scale
                for i in range(4)
            ]
            keys = [part[0].astype(BF), part[2].astype(BF)]
            key2 = jnp.concatenate(keys, axis=1)
            q2 = qs[s, pair]
            scores = mm_t(q2, key2) * SCALE
            split = scores.reshape(2, SPAN, R)
            cond = jnp.exp(split - jnp.max(split, axis=1, keepdims=True))
            cond = cond / jnp.sum(cond, axis=1, keepdims=True)
            cond = t_mm(cond.reshape(2 * SPAN, R).astype(BF), q2)
            values = [
                (part[2 * i + 1] + cond[:, i * HD : (i + 1) * HD]).astype(BF) for i in range(2)
            ]
            top = jnp.max(scores, axis=1, keepdims=True).astype(BF).astype(F32)
            expo = jnp.exp(scores - top)
            total = jnp.sum(expo, axis=1, keepdims=True)
            low = expo.astype(BF)
            e_ref[s, pair] = expo
            k_ref[s, pair] = key2
            v_ref[s, pair] = jnp.concatenate(values, axis=1)
            for i in range(2):
                pbs[s, 2 * pair + i] = mm(
                    low[i * SPAN : (i + 1) * SPAN], jnp.concatenate([values[i], keys[i]], axis=1)
                ).astype(BF)
            tops[pair] = jnp.where(mark, top, tops[pair])
            totals[pair] = jnp.where(mark, total, totals[pair])
        return 0

    lax.fori_loop(0, HALF, slot, 0, unroll=2)
    for h in range(H):
        for u in range(U):
            block = pbs[:, h, u * TB : (u + 1) * TB, :].reshape(HALF * TB, 2 * HD)
            rows = mm(order, block).astype(BF)
            for i, dst_ref in enumerate((p_ref, b_ref)):
                dst_ref[h * TB : (h + 1) * TB, u, :, :] = rows[
                    :, i * HD : (i + 1) * HD
                ].reshape(TB, HALF, HD)

    @pl.when(step == 1)
    def _():
        for h in range(H):
            lo = (h % 2) * SPAN
            for i, acc in enumerate((tops, totals)):
                rows = acc[h // 2, lo : lo + TB]
                for u in range(1, U):
                    rows = rows + acc[h // 2, lo + u * TB : lo + (u + 1) * TB]
                stat_ref[i, h * TB : (h + 1) * TB, :] = rows.astype(BF)


def backward_body(g_ref, e_ref, k_ref, v_ref, a_ref, gs, as_):
    order = swap_order()

    @pl.when(pl.program_id(0) == 0)
    def _():
        gs[...] = jnp.zeros_like(gs)

    to_slots(order, g_ref, gs)

    def slot(s, _):
        for pair in range(H // 2):
            grad = mm_t(gs[s, pair], v_ref[s, pair])
            both = mm((e_ref[s, pair] * grad).astype(BF), k_ref[s, pair]).astype(BF)
            for i in range(2):
                as_[s, 2 * pair + i] = both[i * SPAN : (i + 1) * SPAN, i * HD : (i + 1) * HD]
        return 0

    lax.fori_loop(0, HALF, slot, 0, unroll=2)
    for h in range(H):
        for u in range(0, U, 2):
            block = jnp.concatenate(
                [
                    as_[:, h, v * TB : (v + 1) * TB, :].reshape(HALF * TB, HD)
                    for v in (u, u + 1)
                ],
                axis=1,
            )
            rows = mm(order, block).astype(BF)
            for j in range(2):
                a_ref[h * TB : (h + 1) * TB, u + j, :, :] = rows[
                    :, j * HD : (j + 1) * HD
                ].reshape(TB, HALF, HD)


def choose_rows(in_ref, picks, out_refs, cat_ref):
    for u in range(U):
        cat_ref[:, u * HD : (u + 1) * HD] = in_ref[:, u * S : (u + 1) * S, :].reshape(SLOTS, HD)
    size = 128
    for cols, out_ref in zip(picks, out_refs):

        def step(i, _, cols=cols, out_ref=out_ref):
            at = pl.ds(pl.multiple_of(i * size, size), size)
            ids = iota((size, SLOTS), 1).astype(F32)
            mask = ids == cols[0][at, :]
            for col in cols[1:]:
                mask = mask | (ids == col[at, :])
            out_ref[at, :] = mm(hot(mask), cat_ref[...])
            return 0

        lax.fori_loop(0, SPANS // size, step, 0)


def combine_body(back_ref, first_ref, row_ref, col_ref, att_ref, wd_ref, cat, pa, pb, ca, cb):
    cols = col_ref[...]
    ca[...] = cols[:, 0:1]
    cb[...] = cols[:, 1:2]
    choose_rows(back_ref, ((ca,), (cb,)), (pa, pb), cat)
    lane = iota((SPANS, HD), 1)
    group = hot(iota((HD, HD), 0) // S == iota((HD, HD), 1))
    ungroup = hot(iota((HD, HD), 0) == iota((HD, HD), 1) // S)
    wide = hot(iota((HD, W), 0) == iota((HD, W), 1) // HD)
    stats = back_ref[:, U * S :, :].astype(F32).reshape(N * C, HD).astype(BF)

    def owner_stat(n, which):
        at = cols[:, 2 + n : 3 + n] * float(C) + float(which)
        rows = mm(hot(iota((SPANS, N * C), 1).astype(F32) == at), stats)
        rows = jnp.where((lane % S).astype(F32) == cols[:, 4 + n : 5 + n], rows, 0.0)
        return mm(rows.astype(BF), group)

    tops = [owner_stat(n, 0) for n in range(2)]
    totals = [owner_stat(n, 1) + jnp.where(lane >= U, 1.0, 0.0) for n in range(2)]
    highest = jnp.maximum(tops[0], tops[1])
    factor = [jnp.exp(t - highest) for t in tops]
    denominator = factor[0] * totals[0] + factor[1] * totals[1]
    low = [(f / denominator).astype(BF) for f in factor]
    attended = mm(low[0], wide) * pa[...] + mm(low[1], wide) * pb[...]
    grads = span_rows(first_ref[:, U * C : 2 * U * C, :])
    delta = jnp.zeros((SPANS, HD), F32)
    for u in range(U):
        part = jnp.sum(grads[u] * attended[:, u * HD : (u + 1) * HD], axis=1, keepdims=True)
        delta = jnp.where(lane == u, part, delta)
    delta = delta.astype(BF)
    for u in range(0, U, 2):
        att_ref[:, u * C : (u + 2) * C, :] = jnp.concatenate(
            [
                attended[:, v * HD : (v + 1) * HD].reshape(N, C, HD)
                for v in (u, u + 1)
            ],
            axis=1,
        ).astype(BF)

    sent = []
    for values in (low, [delta, delta]):
        rows = jnp.zeros((N, HD), F32)
        for n in range(2):
            spread = mm(values[n], ungroup)
            spread = jnp.where((lane % S).astype(F32) == cols[:, 4 + n : 5 + n], spread, 0.0)
            owners = hot(iota((N, SPANS), 0).astype(F32) == row_ref[2 + n : 3 + n, :])
            rows = rows + mm(owners, spread.astype(BF))
        sent.append(rows[:, None, :])
    place = iota((N, C, HD), 1)
    wd_ref[...] = jnp.where(
        place == 0, sent[0], jnp.where(place == 1, sent[1], 0.0)
    ).astype(BF)


def scale_body(wd_ref, a_ref, b_ref, out_ref):
    count = wd_ref.shape[0]
    flat = wd_ref[...].astype(F32).reshape(count * C, HD)
    cols = jnp.transpose(flat)
    for k in range(count):
        w = cols[:, k * C : k * C + 1]
        delta = cols[:, k * C + 1 : k * C + 2]
        out_ref[k] = (
            w * (a_ref[k].astype(F32) - delta * b_ref[k].astype(F32)) * SCALE
        ).astype(BF)


def sum_body(terms_ref, att_ref, col_ref, out_ref, cat, acc, ca, cb):
    cols = col_ref[...]
    ca[...] = cols[:, 0:1]
    cb[...] = cols[:, 1:2]
    choose_rows(terms_ref, ((ca, cb),), (acc,), cat)
    out_ref[:, : U * C, :] = att_ref[...]
    for u in range(0, U, 2):
        base = U * C + u * C
        out_ref[:, base : base + 2 * C, :] = jnp.concatenate(
            [acc[:, v * HD : (v + 1) * HD].reshape(N, C, HD) for v in (u, u + 1)], axis=1
        ).astype(BF)


def swap(rows):
    return lax.all_to_all(rows, "seq", split_axis=0, concat_axis=0, tiled=True)


def route(first, base):
    return call(
        functools.partial(route_body, base),
        (sds((N, U * S, HD), BF), sds((8, SPANS), F32), sds((SPANS, HD), F32)),
        scratch_shapes=[pltpu.VMEM((SPANS, W), BF)],
        flops=1.1e9,
    )(first)


def local(queries, out_grad, neighbours, placement):
    owner, place = placement // S, placement % S
    digits = jnp.concatenate([owner, place], axis=1).astype(BF)
    digits = jnp.pad(digits, ((0, 0), (0, HD - 4)))
    rows_in = 2 * U * C + C
    first = swap(
        call(prep_body, sds((N, rows_in, HD), BF), flops=5e8)(queries, out_grad, digits)
    )
    square_sums = jnp.sum(jnp.square(neighbours.astype(F32)), axis=-1)
    row_scale = lax.rsqrt(lax.psum(square_sums, "head") / D + 1e-06)
    row_scale = jnp.pad(row_scale.T, ((0, 0), (0, HD - S)))

    first, row_scale = lax.optimization_barrier((first, row_scale))
    q_send, rowv, colv = route(first, 0)
    got_q = swap(q_send)
    g_send = route(first, U * C)[0]
    g_send, got_q = lax.optimization_barrier((g_send, got_q))
    got_g = swap(g_send)

    def cut(rows):
        return rows.reshape(N, U, S, HD)

    half_piece = pl.BlockSpec((N, U, HALF, HD), lambda i: (0, 0, i, 0))
    by_slot = lambda *tail: pl.BlockSpec((HALF, H // 2) + tail, lambda i: (i, 0, 0, 0))
    whole = lambda *shape: pl.BlockSpec(shape, lambda i: (0,) * len(shape))
    diagonal = pltpu.VMEM((HALF, H // 2, 2 * SPAN, 2 * HD), BF)
    stat_acc = pltpu.VMEM((H // 2, 2 * SPAN, HD), F32)
    expo, keys, values, p_send, b_rows, stats = call(
        forward_body,
        (
            sds((S, H // 2, 2 * SPAN, R), F32),
            sds((S, H // 2, R, 2 * HD), BF),
            sds((S, H // 2, R, 2 * HD), BF),
            sds((N, U, S, HD), BF),
            sds((N, U, S, HD), BF),
            sds((2, N, HD), BF),
        ),
        grid=(2,),
        in_specs=[
            half_piece,
            pl.BlockSpec((HALF, R, 2 * H * HD), lambda i: (i, 0, 0)),
            whole(R, HD),
        ],
        out_specs=(
            by_slot(2 * SPAN, R),
            by_slot(R, 2 * HD),
            by_slot(R, 2 * HD),
            half_piece,
            half_piece,
            whole(2, N, HD),
        ),
        scratch_shapes=[
            diagonal,
            pltpu.VMEM((HALF, H, SPAN, 2 * HD), BF),
            stat_acc,
            stat_acc,
        ],
        flops=2e9,
        nbytes=3e7,
        vmem=56,
    )(cut(got_q), neighbours, row_scale)
    stats = jnp.pad(jnp.transpose(stats, (1, 0, 2)), ((0, 0), (0, C - 2), (0, 0)))
    back_send = jnp.concatenate([p_send.reshape(N, U * S, HD), stats], axis=1)
    back_send, got_g = lax.optimization_barrier((back_send, got_g))
    back = swap(back_send)
    a_rows = call(
        backward_body,
        sds((N, U, S, HD), BF),
        grid=(2,),
        in_specs=[half_piece, by_slot(2 * SPAN, R), by_slot(R, 2 * HD), by_slot(R, 2 * HD)],
        out_specs=half_piece,
        scratch_shapes=[diagonal, pltpu.VMEM((HALF, H, SPAN, HD), BF)],
        flops=1e9,
        nbytes=2e7,
        vmem=48,
    )(cut(got_g), expo, keys, values)

    back, a_rows = lax.optimization_barrier((back, a_rows))
    span_table = pltpu.VMEM((SPANS, W), F32)
    column = pltpu.VMEM((SPANS, 1), F32)
    cat = pltpu.VMEM((SLOTS, W), BF)
    attended, wd_send = call(
        combine_body,
        (sds((N, U * C, HD), BF), sds((N, C, HD), BF)),
        scratch_shapes=[cat, span_table, span_table, column, column],
        flops=2.2e9,
        vmem=48,
    )(back, first, rowv, colv)
    wd = swap(wd_send)
    group = 16
    k_block = lambda rows: pl.BlockSpec((group, rows, HD), lambda i: (i, 0, 0))
    terms = call(
        scale_body,
        sds((N, U * S, HD), BF),
        grid=(N // group,),
        in_specs=[k_block(C), k_block(U * S), k_block(U * S)],
        out_specs=k_block(U * S),
    )(wd, a_rows.reshape(N, U * S, HD), b_rows.reshape(N, U * S, HD))
    last = call(
        sum_body,
        sds((N, 2 * U * C, HD), BF),
        scratch_shapes=[cat, span_table, column, column],
        flops=1.1e9,
        vmem=48,
    )(swap(terms), attended, colv)
    return call(
        final_body, (sds(queries.shape, BF), sds(queries.shape, BF)), flops=5e8
    )(swap(last))


def solution(mesh):
    in_specs = (P("seq", "head"), P("seq", "head"), P("seq", None, "head"), P("seq", None))
    out_specs = (P("seq", "head"), P("seq", "head"))
    return jax.shard_map(local, mesh=mesh, in_specs=in_specs, out_specs=out_specs, check_vma=False)
```

time: 473 us -> 353 us (0.75); the launches traced: 465 us -> 352 us
  local copies, waits for them, and re-layouts: 99.2 us -> 9.88 us
  Pallas kernels: 0 us -> 76.5 us
  matrix products: 44.9 us -> 0 us
  starting transfers between devices: 57 us -> 31 us
  waiting for transfers between devices: 125 us -> 104 us
  other arithmetic: 26.5 us -> 8.38 us
  blocking collectives: 110 us -> 121 us
    pallas_call x0 -> x9, Pallas kernels: none -> 76.5 us  [the longest x1 39.3 us: local(): call(forward_body, (sds((S, H // 2, 2 * SPAN, R), F32), sds((S, H // 2, R...]
    all_to_all x1 -> x3, blocking collectives: 34.2 us -> 106 us  [swap(): return lax.all_to_all(rows, 'seq', split_axis=0, concat_axis=0, tiled=True)]
    all_gather x1 -> x0, blocking collectives: 61.2 us -> none  [local(): pair = lax.all_gather(placement, 'seq', axis=0, tiled=True)]
    reshape x17 -> x0, local copies, waits for them, and re-layouts: 50.1 us -> none  [the longest x6 31.2 us: by_piece(): rows.reshape(slots, n, unit * HD).transpose(1, 0, 2)]
    dot_general x15 -> x0, matrix products: 44.9 us -> none  [the longest x5 9.85 us: pick(): return jnp.einsum('cs,sw->cw', mask, rows, preferred_element_type=F32)]
    all_to_all x6 -> x4, starting transfers between devices: 57 us -> 31 us  [swap(): return lax.all_to_all(rows, 'seq', split_axis=0, concat_axis=0, tiled=True)]
    all_to_all x6 -> x4, waiting for transfers between devices: 125 us -> 104 us  [swap(): return lax.all_to_all(rows, 'seq', split_axis=0, concat_axis=0, tiled=True)]
    unnamed x19 -> x15, local copies, waits for them, and re-layouts: 21.8 us -> 8.36 us
  transfers between devices with their start and end apart: 6 -> 4, of which waited for: 3 -> 4; matrix products, arithmetic and copies ran while one was open for 18% -> 3% of each run, Pallas kernels for 0% -> 16%
where the time goes in v2:
time: 353 us; the launch traced here: 352 us
  blocking collectives  121 us (34%)
  waiting for transfers between devices  104 us (29%)
  Pallas kernels  76.5 us (22%)
  starting transfers between devices  31 us (9%)
  local copies, waits for them, and re-layouts  9.88 us (3%)
  other arithmetic  8.38 us (2%)
    all_to_all x3, blocking collectives, swap(): return lax.all_to_all(rows, 'seq', split_axis=0, concat_axis=0, tiled=True)  106 us
    all_to_all x4, waiting for transfers between devices, swap(): return lax.all_to_all(rows, 'seq', split_axis=0, concat_axis=0, tiled=True)  104 us
    pallas_call x1, Pallas kernels, local(): call(forward_body, (sds((S, H // 2, 2 * SPAN, R), F32), sds((S, H // 2, R...  39.3 us
    all_to_all x4, starting transfers between devices, swap(): return lax.all_to_all(rows, 'seq', split_axis=0, concat_axis=0, tiled=True)  31 us
    psum x1, blocking collectives, local(): row_scale = lax.rsqrt(lax.psum(square_sums, 'head') / D + 1e-06)  15.2 us
    pallas_call x1, Pallas kernels, local(): call(backward_body, sds((N, U, S, HD), BF), grid=(2,), in_specs=[half_pie...  13.4 us
    pallas_call x1, Pallas kernels, local(): call(combine_body, (sds((N, U * C, HD), BF), sds((N, C, HD), BF)), scratc...  8.68 us
    unnamed x15, local copies, waits for them, and re-layouts  8.36 us
  transfers between devices with their start and end apart: 4, of which 4 were waited for; matrix products, arithmetic and copies ran while one was open for 3% of the time, Pallas kernels for 16%

profile of v2, /device:TPU:1, one launch (start us, length us, event | category | flops | bytes accessed | tf_op | source)
XLA Modules:
  0.0 351.7 jit_solution(1220353106785581460)
XLA Ops:
  3.6 1.8 shard_map.59
  5.3 13.0 %all-to-all-start = ((bf16[64,72,128]{2,1,0:T(8,128)(2,1)}), bf16[64,72,128]{2,1,0:T(8,128)(2,1)S(1)}, u32[]{:S(2)}, u32[]{:S(2)}) async-start(bf16[64,72,128]{2,1,0:T(8,128)(2,1)} %shard_map.59), calls=%async_computation | async-start | bytes 2359296 | tf_op jit(solution)/shard_map/all_to_all | solution.py:362
  18.3 5.1 %multiply_reduce_fusion = f32[32,128]{1,0:T(8,128)S(1)} fusion(bf16[32,128,1024]{2,1,0:T(8,128)(2,1)} %nb_ref.1), kind=kLoop, calls=%fused_computation | loop fusion | flops 12578816 | bytes 8404992 | tf_op jit(solution)/shard_map/reduce_sum | solution.py:382
  23.5 15.2 %psum.7 = f32[32,128]{0,1:T(8,128)S(1)} all-reduce(f32[32,128]{0,1:T(8,128)S(1)} %copy.15), channel_id=1, replica_groups=mesh['seq'=64,'head'=4] {'head'}, use_global_device_ids=true, to_apply=%region_1.2 | all-reduce | flops 4096 | bytes 32768 | tf_op jit(solution)/shard_map/psum | solution.py:383
  39.4 10.3 %all-to-all-done.first_ref = bf16[64,72,128]{2,1,0:T(8,128)(2,1)S(1)} async-done(((bf16[64,72,128]{2,1,0:T(8,128)(2,1)}), bf16[64,72,128]{2,1,0:T(8,128)(2,1)S(1)}, u32[]{:S(2)}, u32[]{:S(2)}) %all-to-all-start) | async-done | bytes 1179680 | tf_op jit(solution)/shard_map/all_to_all | solution.py:362
  49.7 4.2 %shard_map.61 = (bf16[64,128,128]{2,1,0:T(8,128)(2,1)}, f32[8,512]{1,0:T(8,128)S(1)}, f32[512,128]{1,0:T(8,128)S(1)}) custom-call(bf16[64,72,128]{2,1,0:T(8,128)(2,1)S(1)} %all-to-all-done.first_ref), custom_call_target="tpu_custom_call" | custom-call | flops 1100000000 | bytes 4000000 | tf_op jit(solution)/shard_map/pallas_call | solution.py:366
  53.8 6.2 %all-to-all-start.1 = ((bf16[64,128,128]{2,1,0:T(8,128)(2,1)}), bf16[64,128,128]{2,1,0:T(8,128)(2,1)S(1)}, u32[]{:S(2)}, u32[]{:S(2)}) async-start(bf16[64,128,128]{2,1,0:T(8,128)(2,1)} %get-tuple-element.24), calls=%async_computation.1 | async-start | bytes 4194304 | tf_op jit(solution)/shard_map/all_to_all | solution.py:362
  60.0 3.2 shard_map.60
  64.5 46.7 %all-to-all-done.1 = bf16[64,128,128]{2,1,0:T(8,128)(2,1)S(1)} async-done(((bf16[64,128,128]{2,1,0:T(8,128)(2,1)}), bf16[64,128,128]{2,1,0:T(8,128)(2,1)S(1)}, u32[]{:S(2)}, u32[]{:S(2)}) %all-to-all-start.1) | async-done | bytes 2097184 | tf_op jit(solution)/shard_map/all_to_all | solution.py:362
  112.6 5.8 %all-to-all-start.2 = ((bf16[64,128,128]{2,1,0:T(8,128)(2,1)}), bf16[64,128,128]{2,1,0:T(8,128)(2,1)S(1)}, u32[]{:S(2)}, u32[]{:S(2)}) async-start(bf16[64,128,128]{2,1,0:T(8,128)(2,1)} %copy-done.3), calls=%async_computation.2 | async-start | bytes 4194304 | tf_op jit(solution)/shard_map/all_to_all | solution.py:362
  118.4 39.3 %shard_map.62 = (f32[32,2,128,128]{3,2,1,0:T(8,128)}, bf16[32,2,128,256]{3,2,1,0:T(8,128)(2,1)}, bf16[32,2,128,256]{3,2,1,0:T(8,128)(2,1)}, bf16[64,4,32,128]{3,...) custom-call(bf16[64,4,32,128]{3,2,1,0:T(8,128)(2,1)} %bitcast.13, ...), custom_call_target="tpu_custom_call" | custom-call | flops 2000000000 | bytes 30000000 | tf_op jit(solution)/shard_map/pallas_call | solution.py:401
  158.5 3.2 fusion.1
  161.7 8.0 %all-to-all-done.2 = bf16[64,128,128]{2,1,0:T(8,128)(2,1)S(1)} async-done(((bf16[64,128,128]{2,1,0:T(8,128)(2,1)}), bf16[64,128,128]{2,1,0:T(8,128)(2,1)S(1)}, u32[]{:S(2)}, u32[]{:S(2)}) %all-to-all-start.2) | async-done | bytes 2097184 | tf_op jit(solution)/shard_map/all_to_all | solution.py:362
  171.0 6.0 %all-to-all-start.3 = ((bf16[64,136,128]{2,1,0:T(8,128)(2,1)}), bf16[64,136,128]{2,1,0:T(8,128)(2,1)}, u32[]{:S(2)}, u32[]{:S(2)}) async-start(bf16[64,136,128]{2,1,0:T(8,128)(2,1)} %fusion.1), calls=%async_computation.3 | async-start | bytes 4456448 | tf_op jit(solution)/shard_map/all_to_all | solution.py:362
  177.0 1.6 copy-done.1
  178.6 13.4 %shard_map.63 = bf16[64,4,32,128]{3,2,1,0:T(8,128)(2,1)S(1)} custom-call(bf16[64,4,32,128]{3,2,1,0:T(8,128)(2,1)S(1)} %bitcast.11, f32[32,2,128,128]{3,2,1,0:T(8,128)} %get-tuple-element.32.e_ref, bf16[32,2,128,256]{3,2,1,0:T(8,128)(2,1)} %get-tuple-element.33.k_ref, bf16[32,2,128,256]{3,2,1,0:T(8,128)(2,1)} %get-tuple-element.34.v_ref), custom_call_target="tpu_custom_call" | custom-call | flops 1000000000 | bytes 20000000 | tf_op jit(solution)/shard_map/pallas_call | solution.py:439
  192.0 38.8 %all-to-all-done.3.back_ref = bf16[64,136,128]{2,1,0:T(8,128)(2,1)} async-done(((bf16[64,136,128]{2,1,0:T(8,128)(2,1)}), bf16[64,136,128]{2,1,0:T(8,128)(2,1)}, u32[]{:S(2)}, u32[]{:S(2)}) %all-to-all-start.3) | async-done | bytes 2228256 | tf_op jit(solution)/shard_map/all_to_all | solution.py:362
  230.7 8.7 %shard_map.64 = (bf16[64,32,128]{2,1,0:T(8,128)(2,1)S(1)}, bf16[64,8,128]{2,1,0:T(8,128)(2,1)S(1)}) custom-call(bf16[64,136,128]{2,1,0:T(8,128)(2,1)} %all-to-all-done.3.back_ref, bf16[64,72,128]{2,1,0:T(8,128)(2,1)S(1)} %all-to-all-done.first_ref, f32[8,512]{1,0:T(8,128)S(1)} %get-tuple-element.36.row_ref, f32[512,128]{1,0:T(8,128)S(1)} %get-tuple-element.37.col_ref), custom_call_target="tpu_custom_call" | custom-call | flops 2200000000 | bytes 4000000 | tf_op jit(solution)/shard_map/pallas_call | solution.py:455
  239.4 16.2 %all_to_all.35.wd_ref = bf16[64,8,128]{2,1,0:T(8,128)(2,1)S(1)} all-to-all(bf16[64,8,128]{2,1,0:T(8,128)(2,1)S(1)} %get-tuple-element.38), channel_id=1, replica_groups=mesh['seq'=64,'head'=4] {'seq'}, dimensions={0} | all-to-all | bytes 262144 | tf_op jit(solution)/shard_map/all_to_all | solution.py:362
  255.6 2.1 shard_map.65
  257.7 55.9 %all_to_all.36.terms_ref = bf16[64,128,128]{2,1,0:T(8,128)(2,1)S(1)} all-to-all(bf16[64,128,128]{2,1,0:T(8,128)(2,1)S(1)} %shard_map.65), channel_id=1, replica_groups=mesh['seq'=64,'head'=4] {'seq'}, dimensions={0} | all-to-all | bytes 4194304 | tf_op jit(solution)/shard_map/all_to_all | solution.py:362
  313.6 2.4 shard_map.66
  316.0 34.2 %all_to_all.37.in_ref = bf16[64,64,128]{2,1,0:T(8,128)(2,1)S(1)} all-to-all(bf16[64,64,128]{2,1,0:T(8,128)(2,1)S(1)} %shard_map.66), channel_id=1, replica_groups=mesh['seq'=64,'head'=4] {'seq'}, dimensions={0} | all-to-all | bytes 2097152 | tf_op jit(solution)/shard_map/all_to_all | solution.py:362
  350.2 1.5 shard_map.67
  (20 shorter events, 8.4 us)
Async XLA Ops:
  1.5 1.0 copy-start.4
  2.5 1.0 copy-start.5
  5.3 44.3 %all-to-all-start = ((bf16[64,72,128]{2,1,0:T(8,128)(2,1)}), bf16[64,72,128]{2,1,0:T(8,128)(2,1)S(1)}, u32[]{:S(2)}, u32[]{:S(2)}) async-start(bf16[64,72,128]{2,1,0:T(8,128)(2,1)} %shard_map.59), calls=%async_computation | async-start | bytes 2359296 | tf_op jit(solution)/shard_map/all_to_all | solution.py:362
  53.8 57.4 %all-to-all-start.1 = ((bf16[64,128,128]{2,1,0:T(8,128)(2,1)}), bf16[64,128,128]{2,1,0:T(8,128)(2,1)S(1)}, u32[]{:S(2)}, u32[]{:S(2)}) async-start(bf16[64,128,128]{2,1,0:T(8,128)(2,1)} %get-tuple-element.24), calls=%async_computation.1 | async-start | bytes 4194304 | tf_op jit(solution)/shard_map/all_to_all | solution.py:362
  63.2 1.3 copy-start.3
  111.3 1.3 copy-start.6
  112.6 57.1 %all-to-all-start.2 = ((bf16[64,128,128]{2,1,0:T(8,128)(2,1)}), bf16[64,128,128]{2,1,0:T(8,128)(2,1)S(1)}, u32[]{:S(2)}, u32[]{:S(2)}) async-start(bf16[64,128,128]{2,1,0:T(8,128)(2,1)} %copy-done.3), calls=%async_computation.2 | async-start | bytes 4194304 | tf_op jit(solution)/shard_map/all_to_all | solution.py:362
  169.7 1.3 copy-start
  171.0 59.8 %all-to-all-start.3 = ((bf16[64,136,128]{2,1,0:T(8,128)(2,1)}), bf16[64,136,128]{2,1,0:T(8,128)(2,1)}, u32[]{:S(2)}, u32[]{:S(2)}) async-start(bf16[64,136,128]{2,1,0:T(8,128)(2,1)} %fusion.1), calls=%async_computation.3 | async-start | bytes 4456448 | tf_op jit(solution)/shard_map/all_to_all | solution.py:362
  177.0 1.6 copy-start.1
  230.7 24.8 %copy-start.2 = (bf16[64,4,32,128]{3,2,1,0:T(8,128)(2,1)S(1)}, bf16[64,4,32,128]{3,2,1,0:T(8,128)(2,1)}, u32[]{:S(2)}) copy-start(bf16[64,4,32,128]{3,2,1,0:T(8,128)(2,1)} %get-tuple-element.40) | copy-start | bytes 6291460

commit v3 on v2

--- a/solution.py
+++ b/solution.py
@@ -48,7 +48,7 @@
     return lax.dot_general(a, b, (((0,), (0,)), ((), ())), preferred_element_type=F32)
 
 
-def call(body, out_shape, flops=1e8, nbytes=4e6, vmem=40, **kw):
+def call(body, out_shape, flops=1e8, nbytes=4e6, vmem=20, **kw):
     return pl.pallas_call(
         body,
         out_shape=out_shape,
@@ -279,36 +279,65 @@
         lax.fori_loop(0, SPANS // size, step, 0)
 
 
-def combine_body(back_ref, first_ref, row_ref, col_ref, att_ref, wd_ref, cat, pa, pb, ca, cb):
+def product_body(back_ref, g_ref, out_ref):
+    ones = jnp.ones((C, HD), BF)
+    for k in range(back_ref.shape[0]):
+        prod = back_ref[k, : U * S, :].astype(F32) * g_ref[k].astype(F32)
+        high = prod.astype(BF)
+        rest = (prod - high.astype(F32)).astype(BF)
+        rows = mm_t(ones, high) + mm_t(ones, rest)
+        part = rows.astype(BF).astype(F32)
+        stats = back_ref[k, U * S :, :].astype(F32)
+        row = iota((C, HD), 0)
+        out_ref[k] = jnp.where(row == 2, part, jnp.where(row == 3, rows - part, stats)).astype(BF)
+
+
+def weight_body(stat_ref, row_ref, col_ref, wd_ref, wts_ref, flat):
+    cols = col_ref[...]
+    lane = iota((SPANS, HD), 1)
+    flat[...] = stat_ref[...].astype(F32).reshape(N * C, HD)
+    stats = jnp.concatenate(
+        [flat[pl.ds(i, N, stride=C), :].astype(BF) for i in range(4)], axis=1
+    )
+    row, col = iota((4 * HD, HD), 0), iota((4 * HD, HD), 1)
+    stat = jnp.minimum(row // HD, 2)
+    group = hot(stat * U + row % HD // S == col)
+    slot_lane = (iota((SPANS, 4 * HD), 1) % S).astype(F32)
+    tops, totals, products = [], [], []
+    for n in range(2):
+        owner = hot(iota((SPANS, N), 1).astype(F32) == cols[:, 2 + n : 3 + n])
+        rows = mm(owner, stats)
+        rows = jnp.where(slot_lane == cols[:, 4 + n : 5 + n], rows, 0.0).astype(BF)
+        rows = mm(rows, group)
+        tops.append(rows)
+        totals.append(pltpu.roll(rows, HD - U, 1))
+        products.append(pltpu.roll(rows, HD - 2 * U, 1))
+    highest = jnp.maximum(tops[0], tops[1])
+    factor = [jnp.exp(t - highest) for t in tops]
+    denominator = factor[0] * totals[0] + factor[1] * totals[1]
+    low = [jnp.where(lane < U, f / denominator, 0.0).astype(BF).astype(F32) for f in factor]
+    delta = jnp.where(lane < U, low[0] * products[0] + low[1] * products[1], 0.0)
+    wts_ref[...] = (low[0] + pltpu.roll(low[1], U, 1)).astype(BF)
+    delta = pltpu.roll(delta, U, 1)
+    spread = hot(iota((HD, 2 * HD), 0) == iota((HD, 2 * HD), 1) // S)
+    out = jnp.zeros((N, 2 * HD), F32)
+    for n in range(2):
+        rows = mm((low[n] + delta).astype(BF), spread)
+        rows = jnp.where(slot_lane[:, : 2 * HD] == cols[:, 4 + n : 5 + n], rows, 0.0)
+        owners = hot(iota((N, SPANS), 0).astype(F32) == row_ref[2 + n : 3 + n, :])
+        out = out + mm(owners, rows.astype(BF))
+    place = iota((N, 2, HD), 1)
+    wd_ref[...] = jnp.where(place == 0, out[:, None, :HD], out[:, None, HD:]).astype(BF)
+
+
+def attended_body(back_ref, col_ref, wts_ref, att_ref, cat, pa, pb, ca, cb):
     cols = col_ref[...]
     ca[...] = cols[:, 0:1]
     cb[...] = cols[:, 1:2]
     choose_rows(back_ref, ((ca,), (cb,)), (pa, pb), cat)
-    lane = iota((SPANS, HD), 1)
-    group = hot(iota((HD, HD), 0) // S == iota((HD, HD), 1))
-    ungroup = hot(iota((HD, HD), 0) == iota((HD, HD), 1) // S)
-    wide = hot(iota((HD, W), 0) == iota((HD, W), 1) // HD)
-    stats = back_ref[:, U * S :, :].astype(F32).reshape(N * C, HD).astype(BF)
-
-    def owner_stat(n, which):
-        at = cols[:, 2 + n : 3 + n] * float(C) + float(which)
-        rows = mm(hot(iota((SPANS, N * C), 1).astype(F32) == at), stats)
-        rows = jnp.where((lane % S).astype(F32) == cols[:, 4 + n : 5 + n], rows, 0.0)
-        return mm(rows.astype(BF), group)
-
-    tops = [owner_stat(n, 0) for n in range(2)]
-    totals = [owner_stat(n, 1) + jnp.where(lane >= U, 1.0, 0.0) for n in range(2)]
-    highest = jnp.maximum(tops[0], tops[1])
-    factor = [jnp.exp(t - highest) for t in tops]
-    denominator = factor[0] * totals[0] + factor[1] * totals[1]
-    low = [(f / denominator).astype(BF) for f in factor]
-    attended = mm(low[0], wide) * pa[...] + mm(low[1], wide) * pb[...]
-    grads = span_rows(first_ref[:, U * C : 2 * U * C, :])
-    delta = jnp.zeros((SPANS, HD), F32)
-    for u in range(U):
-        part = jnp.sum(grads[u] * attended[:, u * HD : (u + 1) * HD], axis=1, keepdims=True)
-        delta = jnp.where(lane == u, part, delta)
-    delta = delta.astype(BF)
+    wide = hot(iota((HD, 2 * W), 0) == iota((HD, 2 * W), 1) // HD)
+    weight = mm(wts_ref[...], wide)
+    attended = weight[:, :W] * pa[...] + weight[:, W:] * pb[...]
     for u in range(0, U, 2):
         att_ref[:, u * C : (u + 2) * C, :] = jnp.concatenate(
             [
@@ -318,28 +347,14 @@
             axis=1,
         ).astype(BF)
 
-    sent = []
-    for values in (low, [delta, delta]):
-        rows = jnp.zeros((N, HD), F32)
-        for n in range(2):
-            spread = mm(values[n], ungroup)
-            spread = jnp.where((lane % S).astype(F32) == cols[:, 4 + n : 5 + n], spread, 0.0)
-            owners = hot(iota((N, SPANS), 0).astype(F32) == row_ref[2 + n : 3 + n, :])
-            rows = rows + mm(owners, spread.astype(BF))
-        sent.append(rows[:, None, :])
-    place = iota((N, C, HD), 1)
-    wd_ref[...] = jnp.where(
-        place == 0, sent[0], jnp.where(place == 1, sent[1], 0.0)
-    ).astype(BF)
-
 
 def scale_body(wd_ref, a_ref, b_ref, out_ref):
     count = wd_ref.shape[0]
-    flat = wd_ref[...].astype(F32).reshape(count * C, HD)
+    flat = wd_ref[...].astype(F32).reshape(2 * count, HD)
     cols = jnp.transpose(flat)
     for k in range(count):
-        w = cols[:, k * C : k * C + 1]
-        delta = cols[:, k * C + 1 : k * C + 2]
+        w = cols[:, 2 * k : 2 * k + 1]
+        delta = cols[:, 2 * k + 1 : 2 * k + 2]
         out_ref[k] = (
             w * (a_ref[k].astype(F32) - delta * b_ref[k].astype(F32)) * SCALE
         ).astype(BF)
@@ -430,11 +445,22 @@
         ],
         flops=2e9,
         nbytes=3e7,
-        vmem=56,
+        vmem=36,
     )(cut(got_q), neighbours, row_scale)
     stats = jnp.pad(jnp.transpose(stats, (1, 0, 2)), ((0, 0), (0, C - 2), (0, 0)))
     back_send = jnp.concatenate([p_send.reshape(N, U * S, HD), stats], axis=1)
-    back_send, got_g = lax.optimization_barrier((back_send, got_g))
+    group = 16
+    k_block = lambda rows: pl.BlockSpec((group, rows, HD), lambda i: (i, 0, 0))
+    stat_block = pl.BlockSpec((group, C, HD), lambda i: (i, U * S // C, 0))
+    back_send = call(
+        product_body,
+        sds((N, U * S + C, HD), BF),
+        grid=(N // group,),
+        in_specs=[k_block(U * S + C), k_block(U * S)],
+        out_specs=stat_block,
+        input_output_aliases={0: 0},
+        vmem=16,
+    )(back_send, got_g)
     back = swap(back_send)
     a_rows = call(
         backward_body,
@@ -445,36 +471,48 @@
         scratch_shapes=[diagonal, pltpu.VMEM((HALF, H, SPAN, HD), BF)],
         flops=1e9,
         nbytes=2e7,
-        vmem=48,
+        vmem=26,
     )(cut(got_g), expo, keys, values)
 
     back, a_rows = lax.optimization_barrier((back, a_rows))
     span_table = pltpu.VMEM((SPANS, W), F32)
     column = pltpu.VMEM((SPANS, 1), F32)
     cat = pltpu.VMEM((SLOTS, W), BF)
-    attended, wd_send = call(
-        combine_body,
-        (sds((N, U * C, HD), BF), sds((N, C, HD), BF)),
+    wd_send, wts = call(
+        weight_body,
+        (sds((N, 2, HD), BF), sds((SPANS, HD), BF)),
+        grid=(1,),
+        in_specs=[
+            pl.BlockSpec((N, C, HD), lambda i: (0, U * S // C, 0)),
+            whole(8, SPANS),
+            whole(SPANS, HD),
+        ],
+        out_specs=(whole(N, 2, HD), whole(SPANS, HD)),
+        scratch_shapes=[pltpu.VMEM((N * C, HD), F32)],
+        vmem=20,
+    )(back, rowv, colv)
+    wd = swap(wd_send)
+    attended = call(
+        attended_body,
+        sds((N, U * C, HD), BF),
         scratch_shapes=[cat, span_table, span_table, column, column],
         flops=2.2e9,
-        vmem=48,
-    )(back, first, rowv, colv)
-    wd = swap(wd_send)
-    group = 16
-    k_block = lambda rows: pl.BlockSpec((group, rows, HD), lambda i: (i, 0, 0))
+        vmem=24,
+    )(back, colv, wts)
     terms = call(
         scale_body,
         sds((N, U * S, HD), BF),
         grid=(N // group,),
-        in_specs=[k_block(C), k_block(U * S), k_block(U * S)],
+        in_specs=[pl.BlockSpec((group, 2, HD), lambda i: (i, 0, 0)), k_block(U * S), k_block(U * S)],
         out_specs=k_block(U * S),
+        vmem=16,
     )(wd, a_rows.reshape(N, U * S, HD), b_rows.reshape(N, U * S, HD))
     last = call(
         sum_body,
         sds((N, 2 * U * C, HD), BF),
         scratch_shapes=[cat, span_table, column, column],
         flops=1.1e9,
-        vmem=48,
+        vmem=20,
     )(swap(terms), attended, colv)
     return call(
         final_body, (sds(queries.shape, BF), sds(queries.shape, BF)), flops=5e8

time: 353 us -> 354 us (level)
  blocking collectives: 121 us -> 64.5 us
  waiting for transfers between devices: 104 us -> 143 us
  local copies, waits for them, and re-layouts: 9.88 us -> 24.1 us
  starting transfers between devices: 31 us -> 35.8 us
    all_to_all x3 -> x2, blocking collectives: 106 us -> 49.3 us  [swap(): return lax.all_to_all(rows, 'seq', split_axis=0, concat_axis=0, tiled=True)]
    all_to_all x4 -> x5, waiting for transfers between devices: 104 us -> 143 us  [swap(): return lax.all_to_all(rows, 'seq', split_axis=0, concat_axis=0, tiled=True)]
    unnamed x15 -> x35, local copies, waits for them, and re-layouts: 8.36 us -> 23.9 us
    pallas_call x2 -> x4, Pallas kernels: 10.7 us -> 17.8 us  [the longest x1 6.37 us: local(): call(attended_body, sds((N, U * C, HD), BF), scratch_shapes=[cat, span_ta...]
    all_to_all x4 -> x5, starting transfers between devices: 31 us -> 35.8 us  [swap(): return lax.all_to_all(rows, 'seq', split_axis=0, concat_axis=0, tiled=True)]
  transfers between devices with their start and end apart: 4 -> 5, of which waited for: 4 -> 5; matrix products, arithmetic and copies ran while one was open for 3% -> 2% of each run, Pallas kernels for 16% -> 16%
where the time goes in v3:
time: 354 us; the launch traced here: 353 us
  waiting for transfers between devices  143 us (40%)
  Pallas kernels  77.3 us (22%)
  blocking collectives  64.5 us (18%)
  starting transfers between devices  35.8 us (10%)
  local copies, waits for them, and re-layouts  24.1 us (7%)
  other arithmetic  6.74 us (2%)
    all_to_all x5, waiting for transfers between devices, swap(): return lax.all_to_all(rows, 'seq', split_axis=0, concat_axis=0, tiled=True)  143 us
    all_to_all x2, blocking collectives, swap(): return lax.all_to_all(rows, 'seq', split_axis=0, concat_axis=0, tiled=True)  49.3 us
    pallas_call x1, Pallas kernels, local(): call(forward_body, (sds((S, H // 2, 2 * SPAN, R), F32), sds((S, H // 2, R...  37.1 us
    all_to_all x5, starting transfers between devices, swap(): return lax.all_to_all(rows, 'seq', split_axis=0, concat_axis=0, tiled=True)  35.8 us
    unnamed x35, local copies, waits for them, and re-layouts  23.9 us
    psum x1, blocking collectives, local(): row_scale = lax.rsqrt(lax.psum(square_sums, 'head') / D + 1e-06)  15.2 us
    pallas_call x1, Pallas kernels, local(): call(backward_body, sds((N, U, S, HD), BF), grid=(2,), in_specs=[half_pie...  10.6 us
  transfers between devices with their start and end apart: 5, of which 5 were waited for; matrix products, arithmetic and copies ran while one was open for 2% of the time, Pallas kernels for 16%

profile of v3, /device:TPU:1, one launch (start us, length us, event | category | flops | bytes accessed | tf_op | source)
XLA Modules:
  0.0 352.5 jit_solution(5268293204078420226)
XLA Ops:
  5.3 13.0 %all-to-all-start = ((bf16[64,72,128]{2,1,0:T(8,128)(2,1)}), bf16[64,72,128]{2,1,0:T(8,128)(2,1)S(1)}, u32[]{:S(2)}, u32[]{:S(2)}) async-start(bf16[64,72,128]{2,1,0:T(8,128)(2,1)} %shard_map.59), calls=%async_computation | async-start | bytes 2359296 | tf_op jit(solution)/shard_map/all_to_all | solution.py:377
  18.3 5.1 %multiply_reduce_fusion = f32[32,128]{1,0:T(8,128)S(1)} fusion(bf16[32,128,1024]{2,1,0:T(8,128)(2,1)} %nb_ref.1), kind=kLoop, calls=%fused_computation | loop fusion | flops 12578816 | bytes 8404992 | tf_op jit(solution)/shard_map/reduce_sum | solution.py:397
  23.5 15.2 %psum.7 = f32[32,128]{0,1:T(8,128)S(1)} all-reduce(f32[32,128]{0,1:T(8,128)S(1)} %copy.16), channel_id=1, replica_groups=mesh['seq'=64,'head'=4] {'head'}, use_global_device_ids=true, to_apply=%region_1.2 | all-reduce | flops 4096 | bytes 32768 | tf_op jit(solution)/shard_map/psum | solution.py:398
  38.8 10.9 %all-to-all-done.first_ref = bf16[64,72,128]{2,1,0:T(8,128)(2,1)S(1)} async-done(((bf16[64,72,128]{2,1,0:T(8,128)(2,1)}), bf16[64,72,128]{2,1,0:T(8,128)(2,1)S(1)}, u32[]{:S(2)}, u32[]{:S(2)}) %all-to-all-start) | async-done | bytes 1179680 | tf_op jit(solution)/shard_map/all_to_all | solution.py:377
  49.7 2.8 shard_map.61
  54.5 6.2 %all-to-all-start.1 = ((bf16[64,128,128]{2,1,0:T(8,128)(2,1)}), bf16[64,128,128]{2,1,0:T(8,128)(2,1)S(1)}, u32[]{:S(2)}, u32[]{:S(2)}) async-start(bf16[64,128,128]{2,1,0:T(8,128)(2,1)} %copy-done.12), calls=%async_computation.1 | async-start | bytes 4194304 | tf_op jit(solution)/shard_map/all_to_all | solution.py:377
  60.7 3.2 shard_map.60
  65.2 46.7 %all-to-all-done.1 = bf16[64,128,128]{2,1,0:T(8,128)(2,1)S(1)} async-done(((bf16[64,128,128]{2,1,0:T(8,128)(2,1)}), bf16[64,128,128]{2,1,0:T(8,128)(2,1)S(1)}, u32[]{:S(2)}, u32[]{:S(2)}) %all-to-all-start.1) | async-done | bytes 2097184 | tf_op jit(solution)/shard_map/all_to_all | solution.py:377
  113.3 5.8 %all-to-all-start.2 = ((bf16[64,128,128]{2,1,0:T(8,128)(2,1)}), bf16[64,128,128]{2,1,0:T(8,128)(2,1)S(1)}, u32[]{:S(2)}, u32[]{:S(2)}) async-start(bf16[64,128,128]{2,1,0:T(8,128)(2,1)} %copy-done.11), calls=%async_computation.2 | async-start | bytes 4194304 | tf_op jit(solution)/shard_map/all_to_all | solution.py:377
  120.7 37.1 %shard_map.62 = (f32[32,2,128,128]{3,2,1,0:T(8,128)S(1)}, bf16[32,2,128,256]{3,2,1,0:T(8,128)(2,1)S(1)}, bf16[32,2,128,256]{3,2,1,0:T(8,128)(2,1)}, bf16[64,4,32...) custom-call(bf16[64,4,32,128]{3,2,1,0:T(8,128)(2,1)S(1)} %bitcast.11, ...), custom_call_target="tpu_custom_call" | custom-call | flops 2000000000 | bytes 30000000 | tf_op jit(solution)/shard_map/pallas_call | solution.py:416
  164.8 5.6 %all-to-all-done.2.g_ref = bf16[64,128,128]{2,1,0:T(8,128)(2,1)S(1)} async-done(((bf16[64,128,128]{2,1,0:T(8,128)(2,1)}), bf16[64,128,128]{2,1,0:T(8,128)(2,1)S(1)}, u32[]{:S(2)}, u32[]{:S(2)}) %all-to-all-start.2) | async-done | bytes 2097184 | tf_op jit(solution)/shard_map/all_to_all | solution.py:377
  170.4 4.8 %shard_map.63 = bf16[64,136,128]{2,1,0:T(8,128)(2,1)} custom-call(bf16[64,136,128]{2,1,0:T(8,128)(2,1)} %fusion.1.back_ref, bf16[64,128,128]{2,1,0:T(8,128)(2,1)S(1)} %all-to-all-done.2.g_ref), custom_call_target="tpu_custom_call", output_to_operand_aliasing={{}: (0, {})} | custom-call | flops 100000000 | bytes 4000000 | tf_op jit(solution)/shard_map/pallas_call | solution.py:455
  175.2 6.0 %all-to-all-start.3 = ((bf16[64,136,128]{2,1,0:T(8,128)(2,1)}), bf16[64,136,128]{2,1,0:T(8,128)(2,1)}, u32[]{:S(2)}, u32[]{:S(2)}) async-start(bf16[64,136,128]{2,1,0:T(8,128)(2,1)} %shard_map.63), calls=%async_computation.3 | async-start | bytes 4456448 | tf_op jit(solution)/shard_map/all_to_all | solution.py:377
  183.3 2.2 copy-done.7
  187.7 10.6 %shard_map.64 = bf16[64,4,32,128]{3,2,1,0:T(8,128)(2,1)S(1)} custom-call(bf16[64,4,32,128]{3,2,1,0:T(8,128)(2,1)S(1)} %bitcast.10, f32[32,2,128,128]{3,2,1,0:T(8,128)S(1)} %copy-done.5, bf16[32,2,128,256]{3,2,1,0:T(8,128)(2,1)S(1)} %copy-done.7, bf16[32,2,128,256]{3,2,1,0:T(8,128)(2,1)S(1)} %copy-done.8), custom_call_target="tpu_custom_call" | custom-call | flops 1000000000 | bytes 20000000 | tf_op jit(solution)/shard_map/pallas_call | solution.py:465
  199.7 35.2 %all-to-all-done.3.stat_ref.back_ref = bf16[64,136,128]{2,1,0:T(8,128)(2,1)} async-done(((bf16[64,136,128]{2,1,0:T(8,128)(2,1)}), bf16[64,136,128]{2,1,0:T(8,128)(2,1)}, u32[]{:S(2)}, u32[]{:S(2)}) %all-to-all-start.3) | async-done | bytes 2228256 | tf_op jit(solution)/shard_map/all_to_all | solution.py:377
  234.9 2.7 shard_map.65
  237.6 15.1 %all_to_all.35.wd_ref = bf16[64,2,128]{2,1,0:T(2,128)(2,1)S(1)} all-to-all(bf16[64,2,128]{2,1,0:T(2,128)(2,1)S(1)} %get-tuple-element.34), channel_id=1, replica_groups=mesh['seq'=64,'head'=4] {'seq'}, dimensions={0} | all-to-all | bytes 65536 | tf_op jit(solution)/shard_map/all_to_all | solution.py:377
  254.3 3.9 %shard_map.66 = bf16[64,128,128]{2,1,0:T(8,128)(2,1)} custom-call(bf16[64,2,128]{2,1,0:T(2,128)(2,1)S(1)} %all_to_all.35.wd_ref, bf16[64,128,128]{2,1,0:T(8,128)(2,1)S(1)} %bitcast.12, bf16[64,128,128]{2,1,0:T(8,128)(2,1)S(1)} %bitcast.13), custom_call_target="tpu_custom_call" | custom-call | flops 100000000 | bytes 4000000 | tf_op jit(solution)/shard_map/pallas_call | solution.py:502
  258.2 4.8 %all-to-all-start.5 = ((bf16[64,128,128]{2,1,0:T(8,128)(2,1)}), bf16[64,128,128]{2,1,0:T(8,128)(2,1)S(1)}, u32[]{:S(2)}, u32[]{:S(2)}) async-start(bf16[64,128,128]{2,1,0:T(8,128)(2,1)} %shard_map.66), calls=%async_computation.5 | async-start | bytes 4194304 | tf_op jit(solution)/shard_map/all_to_all | solution.py:377
  263.0 6.4 %shard_map.67.att_ref = bf16[64,32,128]{2,1,0:T(8,128)(2,1)S(1)} custom-call(bf16[64,136,128]{2,1,0:T(8,128)(2,1)} %all-to-all-done.3.stat_ref.back_ref, f32[512,128]{1,0:T(8,128)S(1)} %copy-done.16, bf16[512,128]{1,0:T(8,128)(2,1)S(1)} %get-tuple-element.37.wts_ref), custom_call_target="tpu_custom_call" | custom-call | flops 2200000000 | bytes 4000000 | tf_op jit(solution)/shard_map/pallas_call | solution.py:495
  269.4 45.0 %all-to-all-done.5.terms_ref = bf16[64,128,128]{2,1,0:T(8,128)(2,1)S(1)} async-done(((bf16[64,128,128]{2,1,0:T(8,128)(2,1)}), bf16[64,128,128]{2,1,0:T(8,128)(2,1)S(1)}, u32[]{:S(2)}, u32[]{:S(2)}) %all-to-all-start.5) | async-done | bytes 2097184 | tf_op jit(solution)/shard_map/all_to_all | solution.py:377
  314.4 2.4 shard_map.68
  316.8 34.2 %all_to_all.36.in_ref = bf16[64,64,128]{2,1,0:T(8,128)(2,1)S(1)} all-to-all(bf16[64,64,128]{2,1,0:T(8,128)(2,1)S(1)} %shard_map.68), channel_id=1, replica_groups=mesh['seq'=64,'head'=4] {'seq'}, dimensions={0} | all-to-all | bytes 2097152 | tf_op jit(solution)/shard_map/all_to_all | solution.py:377
  (43 shorter events, 26.8 us)
Async XLA Ops:
  1.5 1.0 copy-start.13
  2.5 1.0 copy-start.14
  5.3 44.3 %all-to-all-start = ((bf16[64,72,128]{2,1,0:T(8,128)(2,1)}), bf16[64,72,128]{2,1,0:T(8,128)(2,1)S(1)}, u32[]{:S(2)}, u32[]{:S(2)}) async-start(bf16[64,72,128]{2,1,0:T(8,128)(2,1)} %shard_map.59), calls=%async_computation | async-start | bytes 2359296 | tf_op jit(solution)/shard_map/all_to_all | solution.py:377
  52.5 1.3 copy-start.12
  53.8 0.7 copy-start.15
  54.5 57.4 %all-to-all-start.1 = ((bf16[64,128,128]{2,1,0:T(8,128)(2,1)}), bf16[64,128,128]{2,1,0:T(8,128)(2,1)S(1)}, u32[]{:S(2)}, u32[]{:S(2)}) async-start(bf16[64,128,128]{2,1,0:T(8,128)(2,1)} %copy-done.12), calls=%async_computation.1 | async-start | bytes 4194304 | tf_op jit(solution)/shard_map/all_to_all | solution.py:377
  63.9 1.3 copy-start.11
  112.0 1.3 copy-start
  113.3 57.1 %all-to-all-start.2 = ((bf16[64,128,128]{2,1,0:T(8,128)(2,1)}), bf16[64,128,128]{2,1,0:T(8,128)(2,1)S(1)}, u32[]{:S(2)}, u32[]{:S(2)}) async-start(bf16[64,128,128]{2,1,0:T(8,128)(2,1)} %copy-done.11), calls=%async_computation.2 | async-start | bytes 4194304 | tf_op jit(solution)/shard_map/all_to_all | solution.py:377
  119.1 1.6 copy-start.1
  157.9 2.0 copy-start.4
  159.9 2.0 copy-start.6
  161.9 1.4 copy-start.9
  175.2 59.8 %all-to-all-start.3 = ((bf16[64,136,128]{2,1,0:T(8,128)(2,1)}), bf16[64,136,128]{2,1,0:T(8,128)(2,1)}, u32[]{:S(2)}, u32[]{:S(2)}) async-start(bf16[64,136,128]{2,1,0:T(8,128)(2,1)} %shard_map.63), calls=%async_computation.3 | async-start | bytes 4456448 | tf_op jit(solution)/shard_map/all_to_all | solution.py:377
  181.2 2.2 copy-start.5
  183.3 2.2 copy-start.7
  185.5 2.2 copy-start.8
  187.7 47.2 %copy-start.16 = (f32[512,128]{1,0:T(8,128)S(1)}, f32[512,128]{1,0:T(8,128)}, u32[]{:S(2)}) copy-start(f32[512,128]{1,0:T(8,128)} %copy-done.15) | copy-start | bytes 786436
  198.3 1.3 copy-start.2
  234.9 17.8 %copy-start.3 = (bf16[64,4,32,128]{3,2,1,0:T(8,128)(2,1)S(1)}, bf16[64,4,32,128]{3,2,1,0:T(8,128)(2,1)}, u32[]{:S(2)}) copy-start(bf16[64,4,32,128]{3,2,1,0:T(8,128)(2,1)} %copy-done.2) | copy-start | bytes 6291460
  252.7 1.6 copy-start.10
  258.2 56.2 %all-to-all-start.5 = ((bf16[64,128,128]{2,1,0:T(8,128)(2,1)}), bf16[64,128,128]{2,1,0:T(8,128)(2,1)S(1)}, u32[]{:S(2)}, u32[]{:S(2)}) async-start(bf16[64,128,128]{2,1,0:T(8,128)(2,1)} %shard_map.66), calls=%async_computation.5 | async-start | bytes 4194304 | tf_op jit(solution)/shard_map/all_to_all | solution.py:377

commit v4 on v3

--- a/solution.py
+++ b/solution.py
@@ -68,30 +68,34 @@
     return (piece_row % C) * SPAN + ((piece_row // C) % U) * TB + piece_row // (U * C)
 
 
-def prep_body(q_ref, g_ref, digits_ref, out_ref):
+def prep_body(q_ref, g_ref, digits_ref, out_ref, order):
     size = C * SPAN
-    order = hot(iota((size, size), 1) == token_row(iota((size, size), 0)))
-    for base, ref in ((0, q_ref), (U * C, g_ref)):
-        rows = mm(order, ref[...]).astype(BF)
-        for h in range(H):
-            out_ref[h * TB : (h + 1) * TB, base : base + U * C, :] = rows[
-                :, h * HD : (h + 1) * HD
-            ].reshape(TB, U * C, HD)
-    out_ref[:, 2 * U * C :, :] = jnp.broadcast_to(digits_ref[...][None], (N, C, HD))
-
-
-def final_body(in_ref, att_ref, qg_ref):
+
+    @pl.when(pl.program_id(0) == 0)
+    def _():
+        order[...] = hot(iota((size, size), 1) == token_row(iota((size, size), 0)))
+
+    rows = mm(order[...], jnp.concatenate([q_ref[...], g_ref[...]], axis=1)).astype(BF)
+    for i in range(2):
+        out_ref[:, i * U * C : (i + 1) * U * C, :] = rows[:, i * HD : (i + 1) * HD].reshape(
+            TB, U * C, HD
+        )
+    out_ref[:, 2 * U * C :, :] = jnp.broadcast_to(digits_ref[...][None], (TB, C, HD))
+
+
+def final_body(in_ref, att_ref, qg_ref, order):
     size = C * SPAN
-    order = hot(iota((size, size), 0) == token_row(iota((size, size), 1)))
-    for base, ref in ((0, att_ref), (U * C, qg_ref)):
-        cat = jnp.concatenate(
-            [
-                in_ref[h * TB : (h + 1) * TB, base : base + U * C, :].reshape(size, HD)
-                for h in range(H)
-            ],
-            axis=1,
-        )
-        ref[...] = mm(order, cat).astype(BF)
+
+    @pl.when(pl.program_id(0) == 0)
+    def _():
+        order[...] = hot(iota((size, size), 0) == token_row(iota((size, size), 1)))
+
+    both = jnp.concatenate(
+        [in_ref[:, i * U * C : (i + 1) * U * C, :].reshape(size, HD) for i in range(2)], axis=1
+    )
+    both = mm(order[...], both).astype(BF)
+    att_ref[...] = both[:, :HD]
+    qg_ref[...] = both[:, HD:]
 
 
 def span_rows(block):
@@ -100,32 +104,25 @@
 
 
 def route_body(base, first_ref, out_ref, row_ref, col_ref, x_ref):
-    digits = first_ref[:, 2 * U * C :, :].astype(F32).reshape(SPANS, HD)
-    lane = iota((SPANS, HD), 1)
-    slot_part = pltpu.roll(digits, HD - 2, 1)
-    cols = jnp.where(lane < 2, digits * float(S) + slot_part, 0.0)
-    cols = cols + jnp.where((lane >= 2) & (lane < 6), pltpu.roll(digits, 2, 1), 0.0)
-    col_ref[...] = cols
-    rows = jnp.transpose(cols)[:8]
-    row_ref[...] = rows
-    for u, part in enumerate(span_rows(first_ref[:, base : base + U * C, :])):
-        x_ref[:, u * HD : (u + 1) * HD] = part.astype(BF)
-    per = 8
-    slot_a = rows[0:1]
-    slot_b = rows[1:2]
-
-    def step(j, _):
-        ids = (iota((per * S, SPANS), 0) + j * (per * S)).astype(F32)
-        hit = hot((ids == slot_a) | (ids == slot_b))
-        got = mm(hit, x_ref[...]).astype(BF)
-        at = pl.ds(pl.multiple_of(j * per, per), per)
-        for u in range(U):
-            out_ref[at, u * S : (u + 1) * S, :] = got[:, u * HD : (u + 1) * HD].reshape(
-                per, S, HD
-            )
-        return 0
-
-    lax.fori_loop(0, N // per, step, 0)
+    per = out_ref.shape[0]
+
+    @pl.when(pl.program_id(0) == 0)
+    def _():
+        digits = first_ref[:, 2 * U * C :, :].astype(F32).reshape(SPANS, HD)
+        lane = iota((SPANS, HD), 1)
+        slot_part = pltpu.roll(digits, HD - 2, 1)
+        cols = jnp.where(lane < 2, digits * float(S) + slot_part, 0.0)
+        cols = cols + jnp.where((lane >= 2) & (lane < 6), pltpu.roll(digits, 2, 1), 0.0)
+        col_ref[...] = cols
+        row_ref[...] = jnp.transpose(cols)[:8]
+        for u, part in enumerate(span_rows(first_ref[:, base : base + U * C, :])):
+            x_ref[:, u * HD : (u + 1) * HD] = part.astype(BF)
+
+    ids = (iota((per * S, SPANS), 0) + pl.program_id(0) * (per * S)).astype(F32)
+    hit = hot((ids == row_ref[0:1, :]) | (ids == row_ref[1:2, :]))
+    got = mm(hit, x_ref[...]).astype(BF)
+    for u in range(U):
+        out_ref[:, u * S : (u + 1) * S, :] = got[:, u * HD : (u + 1) * HD].reshape(per, S, HD)
 
 
 def swap_order():
@@ -154,7 +151,7 @@
 
 
 def forward_body(
-    q_ref, nb_ref, rs_ref, e_ref, k_ref, v_ref, p_ref, b_ref, stat_ref, qs, pbs, tops, totals
+    q_ref, nb_ref, rs_ref, e_ref, k_ref, v_ref, pay_ref, b_ref, qs, pbs, tops, totals
 ):
     step = pl.program_id(0)
     order = swap_order()
@@ -211,20 +208,24 @@
         for u in range(U):
             block = pbs[:, h, u * TB : (u + 1) * TB, :].reshape(HALF * TB, 2 * HD)
             rows = mm(order, block).astype(BF)
-            for i, dst_ref in enumerate((p_ref, b_ref)):
-                dst_ref[h * TB : (h + 1) * TB, u, :, :] = rows[
-                    :, i * HD : (i + 1) * HD
-                ].reshape(TB, HALF, HD)
+            at = pl.ds(pl.multiple_of(u * S + step * HALF, HALF), HALF)
+            pay_ref[h * TB : (h + 1) * TB, at, :] = rows[:, :HD].reshape(TB, HALF, HD)
+            b_ref[h * TB : (h + 1) * TB, u, :, :] = rows[:, HD:].reshape(TB, HALF, HD)
 
     @pl.when(step == 1)
     def _():
+        place = iota((TB, C, HD), 1)
         for h in range(H):
             lo = (h % 2) * SPAN
-            for i, acc in enumerate((tops, totals)):
-                rows = acc[h // 2, lo : lo + TB]
+            rows = []
+            for acc in (tops, totals):
+                total = acc[h // 2, lo : lo + TB]
                 for u in range(1, U):
-                    rows = rows + acc[h // 2, lo + u * TB : lo + (u + 1) * TB]
-                stat_ref[i, h * TB : (h + 1) * TB, :] = rows.astype(BF)
+                    total = total + acc[h // 2, lo + u * TB : lo + (u + 1) * TB]
+                rows.append(total[:, None, :])
+            pay_ref[h * TB : (h + 1) * TB, U * S :, :] = jnp.where(
+                place == 0, rows[0], jnp.where(place == 1, rows[1], 0.0)
+            ).astype(BF)
 
 
 def backward_body(g_ref, e_ref, k_ref, v_ref, a_ref, gs, as_):
@@ -280,15 +281,15 @@
 
 
 def product_body(back_ref, g_ref, out_ref):
-    ones = jnp.ones((C, HD), BF)
+    size = U * S
+    diagonal = iota((size, HD), 0) == iota((size, HD), 1)
+    row = iota((C, HD), 0)
     for k in range(back_ref.shape[0]):
-        prod = back_ref[k, : U * S, :].astype(F32) * g_ref[k].astype(F32)
-        high = prod.astype(BF)
-        rest = (prod - high.astype(F32)).astype(BF)
-        rows = mm_t(ones, high) + mm_t(ones, rest)
+        prod = back_ref[k, :size, :].astype(F32) * g_ref[k].astype(F32)
+        prod = jnp.where(diagonal, jnp.sum(prod, axis=1, keepdims=True), 0.0)
+        rows = jnp.sum(prod, axis=0, keepdims=True)
         part = rows.astype(BF).astype(F32)
-        stats = back_ref[k, U * S :, :].astype(F32)
-        row = iota((C, HD), 0)
+        stats = back_ref[k, size:, :].astype(F32)
         out_ref[k] = jnp.where(row == 2, part, jnp.where(row == 3, rows - part, stats)).astype(BF)
 
 
@@ -326,8 +327,10 @@
         rows = jnp.where(slot_lane[:, : 2 * HD] == cols[:, 4 + n : 5 + n], rows, 0.0)
         owners = hot(iota((N, SPANS), 0).astype(F32) == row_ref[2 + n : 3 + n, :])
         out = out + mm(owners, rows.astype(BF))
-    place = iota((N, 2, HD), 1)
-    wd_ref[...] = jnp.where(place == 0, out[:, None, :HD], out[:, None, HD:]).astype(BF)
+    place = iota((N, C, HD), 1)
+    wd_ref[...] = jnp.where(
+        place == 0, out[:, None, :HD], jnp.where(place == 1, out[:, None, HD:], 0.0)
+    ).astype(BF)
 
 
 def attended_body(back_ref, col_ref, wts_ref, att_ref, cat, pa, pb, ca, cb):
@@ -350,11 +353,11 @@
 
 def scale_body(wd_ref, a_ref, b_ref, out_ref):
     count = wd_ref.shape[0]
-    flat = wd_ref[...].astype(F32).reshape(2 * count, HD)
+    flat = wd_ref[...].astype(F32).reshape(C * count, HD)
     cols = jnp.transpose(flat)
     for k in range(count):
-        w = cols[:, 2 * k : 2 * k + 1]
-        delta = cols[:, 2 * k + 1 : 2 * k + 2]
+        w = cols[:, C * k : C * k + 1]
+        delta = cols[:, C * k + 1 : C * k + 2]
         out_ref[k] = (
             w * (a_ref[k].astype(F32) - delta * b_ref[k].astype(F32)) * SCALE
         ).astype(BF)
@@ -377,10 +380,22 @@
     return lax.all_to_all(rows, "seq", split_axis=0, concat_axis=0, tiled=True)
 
 
+def whole(*shape):
+    return pl.BlockSpec(shape, lambda i: (0,) * len(shape))
+
+
+def k_block(count, rows):
+    return pl.BlockSpec((count, rows, HD), lambda i: (i, 0, 0))
+
+
 def route(first, base):
+    per = 8
     return call(
         functools.partial(route_body, base),
-        (sds((N, U * S, HD), BF), sds((8, SPANS), F32), sds((SPANS, HD), F32)),
+        (pltpu.HBM((N, U * S, HD), BF), sds((8, SPANS), F32), sds((SPANS, HD), F32)),
+        grid=(N // per,),
+        in_specs=[whole(*first.shape)],
+        out_specs=(k_block(per, U * S), whole(8, SPANS), whole(SPANS, HD)),
         scratch_shapes=[pltpu.VMEM((SPANS, W), BF)],
         flops=1.1e9,
     )(first)
@@ -391,8 +406,19 @@
     digits = jnp.concatenate([owner, place], axis=1).astype(BF)
     digits = jnp.pad(digits, ((0, 0), (0, HD - 4)))
     rows_in = 2 * U * C + C
+    order = pltpu.VMEM((C * SPAN, C * SPAN), BF)
+    one_head = pl.BlockSpec((C * SPAN, HD), lambda i: (0, i))
     first = swap(
-        call(prep_body, sds((N, rows_in, HD), BF), flops=5e8)(queries, out_grad, digits)
+        call(
+            prep_body,
+            pltpu.HBM((N, rows_in, HD), BF),
+            grid=(H,),
+            in_specs=[one_head, one_head, whole(C, HD)],
+            out_specs=k_block(TB, rows_in),
+            scratch_shapes=[order],
+            flops=5e8,
+            vmem=60,
+        )(queries, out_grad, digits)
     )
     square_sums = jnp.sum(jnp.square(neighbours.astype(F32)), axis=-1)
     row_scale = lax.rsqrt(lax.psum(square_sums, "head") / D + 1e-06)
@@ -410,18 +436,16 @@
 
     half_piece = pl.BlockSpec((N, U, HALF, HD), lambda i: (0, 0, i, 0))
     by_slot = lambda *tail: pl.BlockSpec((HALF, H // 2) + tail, lambda i: (i, 0, 0, 0))
-    whole = lambda *shape: pl.BlockSpec(shape, lambda i: (0,) * len(shape))
     diagonal = pltpu.VMEM((HALF, H // 2, 2 * SPAN, 2 * HD), BF)
     stat_acc = pltpu.VMEM((H // 2, 2 * SPAN, HD), F32)
-    expo, keys, values, p_send, b_rows, stats = call(
+    expo, keys, values, back_send, b_rows = call(
         forward_body,
         (
             sds((S, H // 2, 2 * SPAN, R), F32),
             sds((S, H // 2, R, 2 * HD), BF),
             sds((S, H // 2, R, 2 * HD), BF),
+            pltpu.HBM((N, U * S + C, HD), BF),
             sds((N, U, S, HD), BF),
-            sds((N, U, S, HD), BF),
-            sds((2, N, HD), BF),
         ),
         grid=(2,),
         in_specs=[
@@ -433,9 +457,8 @@
             by_slot(2 * SPAN, R),
             by_slot(R, 2 * HD),
             by_slot(R, 2 * HD),
+            whole(N, U * S + C, HD),
             half_piece,
-            half_piece,
-            whole(2, N, HD),
         ),
         scratch_shapes=[
             diagonal,
@@ -447,16 +470,13 @@
         nbytes=3e7,
         vmem=36,
     )(cut(got_q), neighbours, row_scale)
-    stats = jnp.pad(jnp.transpose(stats, (1, 0, 2)), ((0, 0), (0, C - 2), (0, 0)))
-    back_send = jnp.concatenate([p_send.reshape(N, U * S, HD), stats], axis=1)
     group = 16
-    k_block = lambda rows: pl.BlockSpec((group, rows, HD), lambda i: (i, 0, 0))
     stat_block = pl.BlockSpec((group, C, HD), lambda i: (i, U * S // C, 0))
     back_send = call(
         product_body,
-        sds((N, U * S + C, HD), BF),
+        pltpu.HBM((N, U * S + C, HD), BF),
         grid=(N // group,),
-        in_specs=[k_block(U * S + C), k_block(U * S)],
+        in_specs=[k_block(group, U * S + C), k_block(group, U * S)],
         out_specs=stat_block,
         input_output_aliases={0: 0},
         vmem=16,
@@ -480,14 +500,14 @@
     cat = pltpu.VMEM((SLOTS, W), BF)
     wd_send, wts = call(
         weight_body,
-        (sds((N, 2, HD), BF), sds((SPANS, HD), BF)),
+        (sds((N, C, HD), BF), sds((SPANS, HD), BF)),
         grid=(1,),
         in_specs=[
             pl.BlockSpec((N, C, HD), lambda i: (0, U * S // C, 0)),
             whole(8, SPANS),
             whole(SPANS, HD),
         ],
-        out_specs=(whole(N, 2, HD), whole(SPANS, HD)),
+        out_specs=(whole(N, C, HD), whole(SPANS, HD)),
         scratch_shapes=[pltpu.VMEM((N * C, HD), F32)],
         vmem=20,
     )(back, rowv, colv)
@@ -503,9 +523,9 @@
         scale_body,
         sds((N, U * S, HD), BF),
         grid=(N // group,),
-        in_specs=[pl.BlockSpec((group, 2, HD), lambda i: (i, 0, 0)), k_block(U * S), k_block(U * S)],
-        out_specs=k_block(U * S),
-        vmem=16,
+        in_specs=[k_block(group, C), k_block(group, U * S), k_block(group, U * S)],
+        out_specs=k_block(group, U * S),
+        vmem=60,
     )(wd, a_rows.reshape(N, U * S, HD), b_rows.reshape(N, U * S, HD))
     last = call(
         sum_body,
@@ -515,7 +535,13 @@
         vmem=20,
     )(swap(terms), attended, colv)
     return call(
-        final_body, (sds(queries.shape, BF), sds(queries.shape, BF)), flops=5e8
+        final_body,
+        (sds(queries.shape, BF), sds(queries.shape, BF)),
+        grid=(H,),
+        in_specs=[k_block(TB, 2 * U * C)],
+        out_specs=(one_head, one_head),
+        scratch_shapes=[order],
+        flops=5e8,
     )(swap(last))
 
 

time: 354 us -> 356 us (level)
  Pallas kernels: 77.3 us -> 84.2 us
  local copies, waits for them, and re-layouts: 24.1 us -> 19.6 us
    pallas_call x7, Pallas kernels: 20.7 us -> 27.6 us  [the longest x2 9.3 us: route(): call(functools.partial(route_body, base), (pltpu.HBM((N, U * S, HD), BF),...]
    unnamed x35 -> x25, local copies, waits for them, and re-layouts: 23.9 us -> 19.5 us
  transfers between devices with their start and end apart: 5 -> 5, of which waited for: 5 -> 5; matrix products, arithmetic and copies ran while one was open for 2% -> 1% of each run, Pallas kernels for 16% -> 17%
where the time goes in v4:
time: 356 us; the launch traced here: 355 us
  waiting for transfers between devices  143 us (40%)
  Pallas kernels  84.2 us (24%)
  blocking collectives  65.7 us (18%)
  starting transfers between devices  35.9 us (10%)
  local copies, waits for them, and re-layouts  19.6 us (6%)
  other arithmetic  5.78 us (2%)
    all_to_all x5, waiting for transfers between devices, swap(): return lax.all_to_all(rows, 'seq', split_axis=0, concat_axis=0, tiled=True)  143 us
    all_to_all x2, blocking collectives, swap(): return lax.all_to_all(rows, 'seq', split_axis=0, concat_axis=0, tiled=True)  50.5 us
    pallas_call x1, Pallas kernels, local(): call(forward_body, (sds((S, H // 2, 2 * SPAN, R), F32), sds((S, H // 2, R...  37.2 us
    all_to_all x5, starting transfers between devices, swap(): return lax.all_to_all(rows, 'seq', split_axis=0, concat_axis=0, tiled=True)  35.9 us
    unnamed x25, local copies, waits for them, and re-layouts  19.5 us
    psum x1, blocking collectives, local(): row_scale = lax.rsqrt(lax.psum(square_sums, 'head') / D + 1e-06)  15.2 us
    pallas_call x1, Pallas kernels, local(): call(backward_body, sds((N, U, S, HD), BF), grid=(2,), in_specs=[half_pie...  10.6 us
    pallas_call x2, Pallas kernels, route(): call(functools.partial(route_body, base), (pltpu.HBM((N, U * S, HD), BF),...  9.3 us
  transfers between devices with their start and end apart: 5, of which 5 were waited for; matrix products, arithmetic and copies ran while one was open for 1% of the time, Pallas kernels for 17%

profile of v4, /device:TPU:1, one launch (start us, length us, event | category | flops | bytes accessed | tf_op | source)
XLA Modules:
  0.0 354.7 jit_solution(17818896524933155934)
XLA Ops:
  2.1 4.2 %shard_map.59 = bf16[64,72,128]{2,1,0:T(8,128)(2,1)} custom-call(bf16[512,512]{1,0:T(8,128)(2,1)} %q_ref.1, bf16[512,512]{1,0:T(8,128)(2,1)} %g_ref.1, bf16[8,128]{1,0:T(8,128)(2,1)} %fusion.6.digits_ref), custom_call_target="tpu_custom_call" | custom-call | flops 500000000 | bytes 4000000 | tf_op jit(solution)/shard_map/pallas_call | solution.py:412
  6.2 13.0 %all-to-all-start = ((bf16[64,72,128]{2,1,0:T(8,128)(2,1)}), bf16[64,72,128]{2,1,0:T(8,128)(2,1)S(1)}, u32[]{:S(2)}, u32[]{:S(2)}) async-start(bf16[64,72,128]{2,1,0:T(8,128)(2,1)} %shard_map.59), calls=%async_computation | async-start | bytes 2359296 | tf_op jit(solution)/shard_map/all_to_all | solution.py:380
  19.2 5.1 %multiply_reduce_fusion = f32[32,128]{1,0:T(8,128)S(1)} fusion(bf16[32,128,1024]{2,1,0:T(8,128)(2,1)} %nb_ref.1), kind=kLoop, calls=%fused_computation | loop fusion | flops 12578816 | bytes 8404992 | tf_op jit(solution)/shard_map/reduce_sum | solution.py:423
  24.4 15.2 %psum.7 = f32[32,128]{0,1:T(8,128)S(1)} all-reduce(f32[32,128]{0,1:T(8,128)S(1)} %copy.15), channel_id=1, replica_groups=mesh['seq'=64,'head'=4] {'head'}, use_global_device_ids=true, to_apply=%region_1.2 | all-reduce | flops 4096 | bytes 32768 | tf_op jit(solution)/shard_map/psum | solution.py:424
  39.7 10.9 %all-to-all-done.first_ref = bf16[64,72,128]{2,1,0:T(8,128)(2,1)S(1)} async-done(((bf16[64,72,128]{2,1,0:T(8,128)(2,1)}), bf16[64,72,128]{2,1,0:T(8,128)(2,1)S(1)}, u32[]{:S(2)}, u32[]{:S(2)}) %all-to-all-start) | async-done | bytes 1179680 | tf_op jit(solution)/shard_map/all_to_all | solution.py:380
  50.6 4.6 %shard_map.61 = (bf16[64,128,128]{2,1,0:T(8,128)(2,1)}, f32[8,512]{1,0:T(8,128)S(1)}, f32[512,128]{1,0:T(8,128)S(1)}) custom-call(bf16[64,72,128]{2,1,0:T(8,128)(2,1)S(1)} %all-to-all-done.first_ref), custom_call_target="tpu_custom_call" | custom-call | flops 1100000000 | bytes 4000000 | tf_op jit(solution)/shard_map/pallas_call | solution.py:393
  55.9 6.2 %all-to-all-start.1 = ((bf16[64,128,128]{2,1,0:T(8,128)(2,1)}), bf16[64,128,128]{2,1,0:T(8,128)(2,1)S(1)}, u32[]{:S(2)}, u32[]{:S(2)}) async-start(bf16[64,128,128]{2,1,0:T(8,128)(2,1)} %get-tuple-element.21), calls=%async_computation.1 | async-start | bytes 4194304 | tf_op jit(solution)/shard_map/all_to_all | solution.py:380
  62.1 4.7 %shard_map.60 = (bf16[64,128,128]{2,1,0:T(8,128)(2,1)}, f32[8,512]{1,0:T(8,128)}, f32[512,128]{1,0:T(8,128)}) custom-call(bf16[64,72,128]{2,1,0:T(8,128)(2,1)S(1)} %all-to-all-done.first_ref), custom_call_target="tpu_custom_call" | custom-call | flops 1100000000 | bytes 4000000 | tf_op jit(solution)/shard_map/pallas_call | solution.py:393
  66.8 46.5 %all-to-all-done.1 = bf16[64,128,128]{2,1,0:T(8,128)(2,1)S(1)} async-done(((bf16[64,128,128]{2,1,0:T(8,128)(2,1)}), bf16[64,128,128]{2,1,0:T(8,128)(2,1)S(1)}, u32[]{:S(2)}, u32[]{:S(2)}) %all-to-all-start.1) | async-done | bytes 2097184 | tf_op jit(solution)/shard_map/all_to_all | solution.py:380
  114.7 5.8 %all-to-all-start.2 = ((bf16[64,128,128]{2,1,0:T(8,128)(2,1)}), bf16[64,128,128]{2,1,0:T(8,128)(2,1)S(1)}, u32[]{:S(2)}, u32[]{:S(2)}) async-start(bf16[64,128,128]{2,1,0:T(8,128)(2,1)} %get-tuple-element.25), calls=%async_computation.2 | async-start | bytes 4194304 | tf_op jit(solution)/shard_map/all_to_all | solution.py:380
  122.1 37.2 %shard_map.62 = (f32[32,2,128,128]{3,2,1,0:T(8,128)S(1)}, bf16[32,2,128,256]{3,2,1,0:T(8,128)(2,1)S(1)}, bf16[32,2,128,256]{3,2,1,0:T(8,128)(2,1)S(1)}, bf16[64,...) custom-call(bf16[64,4,32,128]{3,2,1,0:T(8,128)(2,1)S(1)} %bitcast.7, bf16[32,128,1024]{2,1,0:T(8,128)(2,1)} %nb_ref.1, ...), custom_call_target="tpu_custom_call" | custom-call | flops 2000000000 | bytes 30000000 | tf_op jit(solution)/shard_map/pallas_call | solution.py:441
  166.5 5.2 %all-to-all-done.2.g_ref = bf16[64,128,128]{2,1,0:T(8,128)(2,1)S(1)} async-done(((bf16[64,128,128]{2,1,0:T(8,128)(2,1)}), bf16[64,128,128]{2,1,0:T(8,128)(2,1)S(1)}, u32[]{:S(2)}, u32[]{:S(2)}) %all-to-all-start.2) | async-done | bytes 2097184 | tf_op jit(solution)/shard_map/all_to_all | solution.py:380
  171.8 4.1 %shard_map.63 = bf16[64,136,128]{2,1,0:T(8,128)(2,1)} custom-call(bf16[64,136,128]{2,1,0:T(8,128)(2,1)} %get-tuple-element.24.back_ref, bf16[64,128,128]{2,1,0:T(8,128)(2,1)S(1)} %all-to-all-done.2.g_ref), custom_call_target="tpu_custom_call", output_to_operand_aliasing={{}: (0, {})} | custom-call | flops 100000000 | bytes 4000000 | tf_op jit(solution)/shard_map/pallas_call | solution.py:475
  175.9 6.0 %all-to-all-start.3 = ((bf16[64,136,128]{2,1,0:T(8,128)(2,1)}), bf16[64,136,128]{2,1,0:T(8,128)(2,1)}, u32[]{:S(2)}, u32[]{:S(2)}) async-start(bf16[64,136,128]{2,1,0:T(8,128)(2,1)} %shard_map.63), calls=%async_computation.3 | async-start | bytes 4456448 | tf_op jit(solution)/shard_map/all_to_all | solution.py:380
  188.4 10.6 %shard_map.64 = bf16[64,4,32,128]{3,2,1,0:T(8,128)(2,1)S(1)} custom-call(bf16[64,4,32,128]{3,2,1,0:T(8,128)(2,1)S(1)} %bitcast.6, f32[32,2,128,128]{3,2,1,0:T(8,128)S(1)} %copy-done.4, bf16[32,2,128,256]{3,2,1,0:T(8,128)(2,1)S(1)} %copy-done.6, bf16[32,2,128,256]{3,2,1,0:T(8,128)(2,1)S(1)} %copy-done.8), custom_call_target="tpu_custom_call" | custom-call | flops 1000000000 | bytes 20000000 | tf_op jit(solution)/shard_map/pallas_call | solution.py:485
  200.4 35.2 %all-to-all-done.3.stat_ref.back_ref = bf16[64,136,128]{2,1,0:T(8,128)(2,1)} async-done(((bf16[64,136,128]{2,1,0:T(8,128)(2,1)}), bf16[64,136,128]{2,1,0:T(8,128)(2,1)}, u32[]{:S(2)}, u32[]{:S(2)}) %all-to-all-start.3) | async-done | bytes 2228256 | tf_op jit(solution)/shard_map/all_to_all | solution.py:380
  235.6 2.5 shard_map.65
  238.1 16.3 %all_to_all.35.wd_ref = bf16[64,8,128]{2,1,0:T(8,128)(2,1)} all-to-all(bf16[64,8,128]{2,1,0:T(8,128)(2,1)S(1)} %get-tuple-element.32), channel_id=1, replica_groups=mesh['seq'=64,'head'=4] {'seq'}, dimensions={0} | all-to-all | bytes 262144 | tf_op jit(solution)/shard_map/all_to_all | solution.py:380
  254.4 5.1 %shard_map.66 = bf16[64,128,128]{2,1,0:T(8,128)(2,1)} custom-call(bf16[64,8,128]{2,1,0:T(8,128)(2,1)} %all_to_all.35.wd_ref, bf16[64,128,128]{2,1,0:T(8,128)(2,1)} %bitcast.8, bf16[64,128,128]{2,1,0:T(8,128)(2,1)} %bitcast.9), custom_call_target="tpu_custom_call" | custom-call | flops 100000000 | bytes 4000000 | tf_op jit(solution)/shard_map/pallas_call | solution.py:522
  259.5 4.9 %all-to-all-start.5 = ((bf16[64,128,128]{2,1,0:T(8,128)(2,1)}), bf16[64,128,128]{2,1,0:T(8,128)(2,1)S(1)}, u32[]{:S(2)}, u32[]{:S(2)}) async-start(bf16[64,128,128]{2,1,0:T(8,128)(2,1)} %shard_map.66), calls=%async_computation.5 | async-start | bytes 4194304 | tf_op jit(solution)/shard_map/all_to_all | solution.py:380
  264.4 6.4 %shard_map.67.att_ref = bf16[64,32,128]{2,1,0:T(8,128)(2,1)S(1)} custom-call(bf16[64,136,128]{2,1,0:T(8,128)(2,1)} %all-to-all-done.3.stat_ref.back_ref, f32[512,128]{1,0:T(8,128)S(1)} %copy-done.11, bf16[512,128]{1,0:T(8,128)(2,1)S(1)} %get-tuple-element.35.wts_ref), custom_call_target="tpu_custom_call" | custom-call | flops 2200000000 | bytes 4000000 | tf_op jit(solution)/shard_map/pallas_call | solution.py:515
  270.8 44.9 %all-to-all-done.5.terms_ref = bf16[64,128,128]{2,1,0:T(8,128)(2,1)S(1)} async-done(((bf16[64,128,128]{2,1,0:T(8,128)(2,1)}), bf16[64,128,128]{2,1,0:T(8,128)(2,1)S(1)}, u32[]{:S(2)}, u32[]{:S(2)}) %all-to-all-start.5) | async-done | bytes 2097184 | tf_op jit(solution)/shard_map/all_to_all | solution.py:380
  315.7 2.4 shard_map.68
  318.1 34.2 %all_to_all.36.in_ref = bf16[64,64,128]{2,1,0:T(8,128)(2,1)S(1)} all-to-all(bf16[64,64,128]{2,1,0:T(8,128)(2,1)S(1)} %shard_map.68), channel_id=1, replica_groups=mesh['seq'=64,'head'=4] {'seq'}, dimensions={0} | all-to-all | bytes 2097152 | tf_op jit(solution)/shard_map/all_to_all | solution.py:380
  (31 shorter events, 22.7 us)
Async XLA Ops:
  6.2 44.4 %all-to-all-start = ((bf16[64,72,128]{2,1,0:T(8,128)(2,1)}), bf16[64,72,128]{2,1,0:T(8,128)(2,1)S(1)}, u32[]{:S(2)}, u32[]{:S(2)}) async-start(bf16[64,72,128]{2,1,0:T(8,128)(2,1)} %shard_map.59), calls=%async_computation | async-start | bytes 2359296 | tf_op jit(solution)/shard_map/all_to_all | solution.py:380
  55.2 0.7 copy-start.10
  55.9 57.4 %all-to-all-start.1 = ((bf16[64,128,128]{2,1,0:T(8,128)(2,1)}), bf16[64,128,128]{2,1,0:T(8,128)(2,1)S(1)}, u32[]{:S(2)}, u32[]{:S(2)}) async-start(bf16[64,128,128]{2,1,0:T(8,128)(2,1)} %get-tuple-element.21), calls=%async_computation.1 | async-start | bytes 4194304 | tf_op jit(solution)/shard_map/all_to_all | solution.py:380
  113.3 1.3 copy-start
  114.7 57.1 %all-to-all-start.2 = ((bf16[64,128,128]{2,1,0:T(8,128)(2,1)}), bf16[64,128,128]{2,1,0:T(8,128)(2,1)S(1)}, u32[]{:S(2)}, u32[]{:S(2)}) async-start(bf16[64,128,128]{2,1,0:T(8,128)(2,1)} %get-tuple-element.25), calls=%async_computation.2 | async-start | bytes 4194304 | tf_op jit(solution)/shard_map/all_to_all | solution.py:380
  120.5 1.6 copy-start.1
  159.3 1.9 copy-start.3
  161.2 2.0 copy-start.5
  163.2 2.0 copy-start.7
  165.2 1.4 copy-start.9
  175.9 59.8 %all-to-all-start.3 = ((bf16[64,136,128]{2,1,0:T(8,128)(2,1)}), bf16[64,136,128]{2,1,0:T(8,128)(2,1)}, u32[]{:S(2)}, u32[]{:S(2)}) async-start(bf16[64,136,128]{2,1,0:T(8,128)(2,1)} %shard_map.63), calls=%async_computation.3 | async-start | bytes 4456448 | tf_op jit(solution)/shard_map/all_to_all | solution.py:380
  181.9 2.2 copy-start.4
  184.1 2.2 copy-start.6
  186.2 2.2 copy-start.8
  188.4 47.2 %copy-start.11 = (f32[512,128]{1,0:T(8,128)S(1)}, f32[512,128]{1,0:T(8,128)}, u32[]{:S(2)}) copy-start(f32[512,128]{1,0:T(8,128)} %copy-done.10) | copy-start | bytes 786436
  199.1 1.3 copy-start.2
  259.5 56.1 %all-to-all-start.5 = ((bf16[64,128,128]{2,1,0:T(8,128)(2,1)}), bf16[64,128,128]{2,1,0:T(8,128)(2,1)S(1)}, u32[]{:S(2)}, u32[]{:S(2)}) async-start(bf16[64,128,128]{2,1,0:T(8,128)(2,1)} %shard_map.66), calls=%async_computation.5 | async-start | bytes 4194304 | tf_op jit(solution)/shard_map/all_to_all | solution.py:380

commit v5 on v3

--- a/solution.py
+++ b/solution.py
@@ -22,6 +22,8 @@
 SPANS = N * C
 SLOTS = N * S
 HALF = S // 2
+ROUTE_STEPS = 8
+PRODUCT_STEPS = 8
 SCALE = 1.0 / math.sqrt(HD)
 BF = jnp.bfloat16
 F32 = jnp.float32
@@ -48,7 +50,7 @@
     return lax.dot_general(a, b, (((0,), (0,)), ((), ())), preferred_element_type=F32)
 
 
-def call(body, out_shape, flops=1e8, nbytes=4e6, vmem=20, **kw):
+def call(body, out_shape, flops=1e8, nbytes=4e6, vmem=40, **kw):
     return pl.pallas_call(
         body,
         out_shape=out_shape,
@@ -68,16 +70,34 @@
     return (piece_row % C) * SPAN + ((piece_row // C) % U) * TB + piece_row // (U * C)
 
 
-def prep_body(q_ref, g_ref, digits_ref, out_ref):
+def prep_body(q_hbm, g_hbm, digits_ref, out_hbm, q_ref, g_ref, order, stage, in_sem, out_sem):
     size = C * SPAN
-    order = hot(iota((size, size), 1) == token_row(iota((size, size), 0)))
-    for base, ref in ((0, q_ref), (U * C, g_ref)):
-        rows = mm(order, ref[...]).astype(BF)
-        for h in range(H):
-            out_ref[h * TB : (h + 1) * TB, base : base + U * C, :] = rows[
-                :, h * HD : (h + 1) * HD
-            ].reshape(TB, U * C, HD)
-    out_ref[:, 2 * U * C :, :] = jnp.broadcast_to(digits_ref[...][None], (N, C, HD))
+    loads = [
+        pltpu.make_async_copy(src, dst, in_sem.at[i])
+        for i, (src, dst) in enumerate(((q_hbm, q_ref), (g_hbm, g_ref)))
+    ]
+    for load in loads:
+        load.start()
+    order[...] = hot(iota((size, size), 1) == token_row(iota((size, size), 0)))
+    stage[:, 2 * U * C :, :] = jnp.broadcast_to(digits_ref[...][None], (N, C, HD))
+    for load in loads:
+        load.wait()
+    stores = []
+    half = H // 2
+    for i in range(2):
+        lanes = slice(i * half * HD, (i + 1) * half * HD)
+        for base, ref in ((0, q_ref), (U * C, g_ref)):
+            rows = mm(order[...], ref[:, lanes]).astype(BF)
+            for j in range(half):
+                h = i * half + j
+                stage[h * TB : (h + 1) * TB, base : base + U * C, :] = rows[
+                    :, j * HD : (j + 1) * HD
+                ].reshape(TB, U * C, HD)
+        part = pl.ds(i * half * TB, half * TB)
+        stores.append(pltpu.make_async_copy(stage.at[part], out_hbm.at[part], out_sem.at[i]))
+        stores[-1].start()
+    for store in stores:
+        store.wait()
 
 
 def final_body(in_ref, att_ref, qg_ref):
@@ -99,20 +119,23 @@
     return [wide[:, u * C : (u + 1) * C, :].reshape(SPANS, HD) for u in range(U)]
 
 
-def route_body(base, first_ref, out_ref, row_ref, col_ref, x_ref):
+def route_body(base, first_ref, out_hbm, row_ref, x_ref, out_ref, out_sem):
     digits = first_ref[:, 2 * U * C :, :].astype(F32).reshape(SPANS, HD)
     lane = iota((SPANS, HD), 1)
     slot_part = pltpu.roll(digits, HD - 2, 1)
     cols = jnp.where(lane < 2, digits * float(S) + slot_part, 0.0)
     cols = cols + jnp.where((lane >= 2) & (lane < 6), pltpu.roll(digits, 2, 1), 0.0)
-    col_ref[...] = cols
     rows = jnp.transpose(cols)[:8]
     row_ref[...] = rows
     for u, part in enumerate(span_rows(first_ref[:, base : base + U * C, :])):
         x_ref[:, u * HD : (u + 1) * HD] = part.astype(BF)
-    per = 8
+    per = N // ROUTE_STEPS
     slot_a = rows[0:1]
     slot_b = rows[1:2]
+
+    def store(j):
+        at = pl.ds(pl.multiple_of(j * per, per), per)
+        return pltpu.make_async_copy(out_ref.at[at], out_hbm.at[at], out_sem.at[j])
 
     def step(j, _):
         ids = (iota((per * S, SPANS), 0) + j * (per * S)).astype(F32)
@@ -123,9 +146,12 @@
             out_ref[at, u * S : (u + 1) * S, :] = got[:, u * HD : (u + 1) * HD].reshape(
                 per, S, HD
             )
+        store(j).start()
         return 0
 
-    lax.fori_loop(0, N // per, step, 0)
+    lax.fori_loop(0, ROUTE_STEPS, step, 0)
+    for j in range(ROUTE_STEPS):
+        store(j).wait()
 
 
 def swap_order():
@@ -153,10 +179,21 @@
                 ].reshape(HALF, TB, HD)
 
 
+def in_hbm(rows):
+    return pltpu.with_memory_space_constraint(rows, pltpu.HBM)
+
+
+def load_half(src_hbm, dst_ref, sem):
+    part = pl.ds(pl.multiple_of(pl.program_id(0) * HALF, HALF), HALF)
+    return pltpu.make_async_copy(src_hbm.at[:, :, part, :], dst_ref, sem)
+
+
 def forward_body(
-    q_ref, nb_ref, rs_ref, e_ref, k_ref, v_ref, p_ref, b_ref, stat_ref, qs, pbs, tops, totals
+    q_hbm, nb_ref, rs_ref, e_ref, k_ref, v_ref, p_ref, b_ref, stat_ref, q_ref, qs, pbs, tops, totals, sem
 ):
     step = pl.program_id(0)
+    load = load_half(q_hbm, q_ref, sem)
+    load.start()
     order = swap_order()
 
     @pl.when(step == 0)
@@ -165,6 +202,7 @@
         totals[...] = jnp.zeros_like(totals)
         qs[...] = jnp.zeros_like(qs)
 
+    load.wait()
     to_slots(order, q_ref, qs)
     row = iota((2 * SPAN, HD), 0) % SPAN
 
@@ -218,13 +256,18 @@
 
     @pl.when(step == 1)
     def _():
+        place = iota((TB, C, HD), 1)
         for h in range(H):
             lo = (h % 2) * SPAN
-            for i, acc in enumerate((tops, totals)):
-                rows = acc[h // 2, lo : lo + TB]
+            rows = []
+            for acc in (tops, totals):
+                total = acc[h // 2, lo : lo + TB]
                 for u in range(1, U):
-                    rows = rows + acc[h // 2, lo + u * TB : lo + (u + 1) * TB]
-                stat_ref[i, h * TB : (h + 1) * TB, :] = rows.astype(BF)
+                    total = total + acc[h // 2, lo + u * TB : lo + (u + 1) * TB]
+                rows.append(total[:, None, :])
+            stat_ref[h * TB : (h + 1) * TB] = jnp.where(
+                place == 0, rows[0], jnp.where(place == 1, rows[1], 0.0)
+            )
 
 
 def backward_body(g_ref, e_ref, k_ref, v_ref, a_ref, gs, as_):
@@ -261,10 +304,9 @@
                 ].reshape(TB, HALF, HD)
 
 
-def choose_rows(in_ref, picks, out_refs, cat_ref):
+def choose_rows(in_ref, picks, out_refs, cat_ref, size=128):
     for u in range(U):
         cat_ref[:, u * HD : (u + 1) * HD] = in_ref[:, u * S : (u + 1) * S, :].reshape(SLOTS, HD)
-    size = 128
     for cols, out_ref in zip(picks, out_refs):
 
         def step(i, _, cols=cols, out_ref=out_ref):
@@ -279,21 +321,50 @@
         lax.fori_loop(0, SPANS // size, step, 0)
 
 
-def product_body(back_ref, g_ref, out_ref):
-    ones = jnp.ones((C, HD), BF)
-    for k in range(back_ref.shape[0]):
-        prod = back_ref[k, : U * S, :].astype(F32) * g_ref[k].astype(F32)
-        high = prod.astype(BF)
-        rest = (prod - high.astype(F32)).astype(BF)
-        rows = mm_t(ones, high) + mm_t(ones, rest)
-        part = rows.astype(BF).astype(F32)
-        stats = back_ref[k, U * S :, :].astype(F32)
-        row = iota((C, HD), 0)
-        out_ref[k] = jnp.where(row == 2, part, jnp.where(row == 3, rows - part, stats)).astype(BF)
-
-
-def weight_body(stat_ref, row_ref, col_ref, wd_ref, wts_ref, flat):
-    cols = col_ref[...]
+def product_body(p_hbm, stat_hbm, g_ref, out_hbm, rows_ref, stat_ref, in_sem, out_sem):
+    size = U * S
+    per = N // PRODUCT_STEPS
+    diagonal = iota((size, HD), 0) == iota((size, HD), 1)
+    row = iota((C, HD), 0)
+
+    def load(i):
+        at = pl.ds(i * per, per)
+        return (
+            pltpu.make_async_copy(p_hbm.at[at], rows_ref.at[at, pl.ds(0, size)], in_sem.at[0, i]),
+            pltpu.make_async_copy(stat_hbm.at[at], stat_ref.at[at], in_sem.at[1, i]),
+        )
+
+    def store(i):
+        at = pl.ds(i * per, per)
+        return pltpu.make_async_copy(rows_ref.at[at], out_hbm.at[at], out_sem.at[i])
+
+    for i in range(PRODUCT_STEPS):
+        for copy in load(i):
+            copy.start()
+    for i in range(PRODUCT_STEPS):
+        for copy in load(i):
+            copy.wait()
+        for k in range(i * per, (i + 1) * per):
+            prod = rows_ref[k, :size, :].astype(F32) * g_ref[k].astype(F32)
+            prod = jnp.where(diagonal, jnp.sum(prod, axis=1, keepdims=True), 0.0)
+            total = jnp.sum(prod, axis=0, keepdims=True)
+            high = total.astype(BF).astype(F32)
+            rows_ref[k, size:, :] = jnp.where(
+                row == 2, high, jnp.where(row == 3, total - high, stat_ref[k])
+            ).astype(BF)
+        store(i).start()
+    for i in range(PRODUCT_STEPS):
+        store(i).wait()
+
+
+def weight_body(stat_ref, row_ref, a_hbm, b_hbm, wd_ref, wts_ref, a_ref, b_ref, flat, sem):
+    loads = [
+        pltpu.make_async_copy(src, dst, sem.at[i])
+        for i, (src, dst) in enumerate(((a_hbm, a_ref), (b_hbm, b_ref)))
+    ]
+    for load in loads:
+        load.start()
+    cols = jnp.transpose(row_ref[...])
     lane = iota((SPANS, HD), 1)
     flat[...] = stat_ref[...].astype(F32).reshape(N * C, HD)
     stats = jnp.concatenate(
@@ -326,12 +397,18 @@
         rows = jnp.where(slot_lane[:, : 2 * HD] == cols[:, 4 + n : 5 + n], rows, 0.0)
         owners = hot(iota((N, SPANS), 0).astype(F32) == row_ref[2 + n : 3 + n, :])
         out = out + mm(owners, rows.astype(BF))
-    place = iota((N, 2, HD), 1)
-    wd_ref[...] = jnp.where(place == 0, out[:, None, :HD], out[:, None, HD:]).astype(BF)
-
-
-def attended_body(back_ref, col_ref, wts_ref, att_ref, cat, pa, pb, ca, cb):
-    cols = col_ref[...]
+    place = iota((N, C, HD), 1)
+    wd_ref[...] = jnp.where(
+        place == 0, out[:, None, :HD], jnp.where(place == 1, out[:, None, HD:], 0.0)
+    ).astype(BF)
+    for load in loads:
+        load.wait()
+
+
+def attended_body(
+    back_ref, row_ref, wts_ref, att_ref, cat, pa, pb, ca, cb
+):
+    cols = jnp.transpose(row_ref[...])
     ca[...] = cols[:, 0:1]
     cb[...] = cols[:, 1:2]
     choose_rows(back_ref, ((ca,), (cb,)), (pa, pb), cat)
@@ -348,23 +425,32 @@
         ).astype(BF)
 
 
-def scale_body(wd_ref, a_ref, b_ref, out_ref):
-    count = wd_ref.shape[0]
-    flat = wd_ref[...].astype(F32).reshape(2 * count, HD)
+def scale_body(wd_ref, a_ref, b_ref, out_hbm, out_ref, sem):
+    per = N // PRODUCT_STEPS
+
+    def store(i):
+        at = pl.ds(i * per, per)
+        return pltpu.make_async_copy(out_ref.at[at], out_hbm.at[at], sem.at[i])
+
+    flat = wd_ref[...].astype(F32).reshape(C * N, HD)
     cols = jnp.transpose(flat)
-    for k in range(count):
-        w = cols[:, 2 * k : 2 * k + 1]
-        delta = cols[:, 2 * k + 1 : 2 * k + 2]
-        out_ref[k] = (
-            w * (a_ref[k].astype(F32) - delta * b_ref[k].astype(F32)) * SCALE
-        ).astype(BF)
-
-
-def sum_body(terms_ref, att_ref, col_ref, out_ref, cat, acc, ca, cb):
-    cols = col_ref[...]
+    for i in range(PRODUCT_STEPS):
+        for k in range(i * per, (i + 1) * per):
+            w = cols[:, C * k : C * k + 1]
+            delta = cols[:, C * k + 1 : C * k + 2]
+            out_ref[k] = (
+                w * (a_ref[k].astype(F32) - delta * b_ref[k].astype(F32)) * SCALE
+            ).astype(BF)
+        store(i).start()
+    for i in range(PRODUCT_STEPS):
+        store(i).wait()
+
+
+def sum_body(terms_ref, att_ref, row_ref, out_ref, cat, acc, ca, cb):
+    cols = jnp.transpose(row_ref[...])
     ca[...] = cols[:, 0:1]
     cb[...] = cols[:, 1:2]
-    choose_rows(terms_ref, ((ca, cb),), (acc,), cat)
+    choose_rows(terms_ref, ((ca, cb),), (acc,), cat, 256)
     out_ref[:, : U * C, :] = att_ref[...]
     for u in range(0, U, 2):
         base = U * C + u * C
@@ -377,11 +463,25 @@
     return lax.all_to_all(rows, "seq", split_axis=0, concat_axis=0, tiled=True)
 
 
+HBM = pl.BlockSpec(memory_space=pltpu.HBM)
+VMEM = pl.BlockSpec(memory_space=pltpu.VMEM)
+
+
+def whole(*shape):
+    return pl.BlockSpec(shape, lambda i: (0,) * len(shape))
+
+
 def route(first, base):
     return call(
         functools.partial(route_body, base),
-        (sds((N, U * S, HD), BF), sds((8, SPANS), F32), sds((SPANS, HD), F32)),
-        scratch_shapes=[pltpu.VMEM((SPANS, W), BF)],
+        (pltpu.HBM((N, U * S, HD), BF), sds((8, SPANS), F32)),
+        in_specs=[VMEM],
+        out_specs=(HBM, VMEM),
+        scratch_shapes=[
+            pltpu.VMEM((SPANS, W), BF),
+            pltpu.VMEM((N, U * S, HD), BF),
+            pltpu.SemaphoreType.DMA((ROUTE_STEPS,)),
+        ],
         flops=1.1e9,
     )(first)
 
@@ -391,18 +491,32 @@
     digits = jnp.concatenate([owner, place], axis=1).astype(BF)
     digits = jnp.pad(digits, ((0, 0), (0, HD - 4)))
     rows_in = 2 * U * C + C
+    tokens = pltpu.VMEM(queries.shape, BF)
     first = swap(
-        call(prep_body, sds((N, rows_in, HD), BF), flops=5e8)(queries, out_grad, digits)
+        call(
+            prep_body,
+            pltpu.HBM((N, rows_in, HD), BF),
+            in_specs=[HBM, HBM, VMEM],
+            out_specs=HBM,
+            scratch_shapes=[
+                tokens,
+                tokens,
+                pltpu.VMEM((C * SPAN, C * SPAN), BF),
+                pltpu.VMEM((N, rows_in, HD), BF),
+                pltpu.SemaphoreType.DMA((2,)),
+                pltpu.SemaphoreType.DMA((2,)),
+            ],
+            flops=5e8,
+        )(in_hbm(queries), in_hbm(out_grad), digits)
     )
     square_sums = jnp.sum(jnp.square(neighbours.astype(F32)), axis=-1)
     row_scale = lax.rsqrt(lax.psum(square_sums, "head") / D + 1e-06)
     row_scale = jnp.pad(row_scale.T, ((0, 0), (0, HD - S)))
 
     first, row_scale = lax.optimization_barrier((first, row_scale))
-    q_send, rowv, colv = route(first, 0)
+    q_send, rowv = route(first, 0)
     got_q = swap(q_send)
     g_send = route(first, U * C)[0]
-    g_send, got_q = lax.optimization_barrier((g_send, got_q))
     got_g = swap(g_send)
 
     def cut(rows):
@@ -410,7 +524,7 @@
 
     half_piece = pl.BlockSpec((N, U, HALF, HD), lambda i: (0, 0, i, 0))
     by_slot = lambda *tail: pl.BlockSpec((HALF, H // 2) + tail, lambda i: (i, 0, 0, 0))
-    whole = lambda *shape: pl.BlockSpec(shape, lambda i: (0,) * len(shape))
+    half_rows = pltpu.VMEM((N, U, HALF, HD), BF)
     diagonal = pltpu.VMEM((HALF, H // 2, 2 * SPAN, 2 * HD), BF)
     stat_acc = pltpu.VMEM((H // 2, 2 * SPAN, HD), F32)
     expo, keys, values, p_send, b_rows, stats = call(
@@ -419,13 +533,13 @@
             sds((S, H // 2, 2 * SPAN, R), F32),
             sds((S, H // 2, R, 2 * HD), BF),
             sds((S, H // 2, R, 2 * HD), BF),
-            sds((N, U, S, HD), BF),
-            sds((N, U, S, HD), BF),
-            sds((2, N, HD), BF),
+            pltpu.HBM((N, U, S, HD), BF),
+            pltpu.HBM((N, U, S, HD), BF),
+            pltpu.HBM((N, C, HD), F32),
         ),
         grid=(2,),
         in_specs=[
-            half_piece,
+            HBM,
             pl.BlockSpec((HALF, R, 2 * H * HD), lambda i: (i, 0, 0)),
             whole(R, HD),
         ],
@@ -435,85 +549,96 @@
             by_slot(R, 2 * HD),
             half_piece,
             half_piece,
-            whole(2, N, HD),
+            whole(N, C, HD),
         ),
         scratch_shapes=[
+            half_rows,
             diagonal,
             pltpu.VMEM((HALF, H, SPAN, 2 * HD), BF),
             stat_acc,
             stat_acc,
+            pltpu.SemaphoreType.DMA,
         ],
         flops=2e9,
         nbytes=3e7,
-        vmem=36,
-    )(cut(got_q), neighbours, row_scale)
-    stats = jnp.pad(jnp.transpose(stats, (1, 0, 2)), ((0, 0), (0, C - 2), (0, 0)))
-    back_send = jnp.concatenate([p_send.reshape(N, U * S, HD), stats], axis=1)
-    group = 16
-    k_block = lambda rows: pl.BlockSpec((group, rows, HD), lambda i: (i, 0, 0))
-    stat_block = pl.BlockSpec((group, C, HD), lambda i: (i, U * S // C, 0))
-    back_send = call(
-        product_body,
-        sds((N, U * S + C, HD), BF),
-        grid=(N // group,),
-        in_specs=[k_block(U * S + C), k_block(U * S)],
-        out_specs=stat_block,
-        input_output_aliases={0: 0},
-        vmem=16,
-    )(back_send, got_g)
-    back = swap(back_send)
+        vmem=56,
+    )(in_hbm(cut(got_q)), neighbours, row_scale)
+    back = swap(
+        call(
+            product_body,
+            pltpu.HBM((N, U * S + C, HD), BF),
+            in_specs=[HBM, HBM, VMEM],
+            out_specs=HBM,
+            scratch_shapes=[
+                pltpu.VMEM((N, U * S + C, HD), BF),
+                pltpu.VMEM((N, C, HD), F32),
+                pltpu.SemaphoreType.DMA((2, PRODUCT_STEPS)),
+                pltpu.SemaphoreType.DMA((PRODUCT_STEPS,)),
+            ],
+        )(in_hbm(p_send.reshape(N, U * S, HD)), in_hbm(stats), got_g)
+    )
     a_rows = call(
         backward_body,
-        sds((N, U, S, HD), BF),
+        pltpu.HBM((N, U, S, HD), BF),
         grid=(2,),
         in_specs=[half_piece, by_slot(2 * SPAN, R), by_slot(R, 2 * HD), by_slot(R, 2 * HD)],
         out_specs=half_piece,
         scratch_shapes=[diagonal, pltpu.VMEM((HALF, H, SPAN, HD), BF)],
         flops=1e9,
         nbytes=2e7,
-        vmem=26,
+        vmem=48,
     )(cut(got_g), expo, keys, values)
 
     back, a_rows = lax.optimization_barrier((back, a_rows))
     span_table = pltpu.VMEM((SPANS, W), F32)
     column = pltpu.VMEM((SPANS, 1), F32)
     cat = pltpu.VMEM((SLOTS, W), BF)
-    wd_send, wts = call(
+    rows = sds((N, U * S, HD), BF)
+    wd_send, wts, a_rows, b_rows = call(
         weight_body,
-        (sds((N, 2, HD), BF), sds((SPANS, HD), BF)),
+        (sds((N, C, HD), BF), sds((SPANS, HD), BF), rows, rows),
         grid=(1,),
         in_specs=[
             pl.BlockSpec((N, C, HD), lambda i: (0, U * S // C, 0)),
             whole(8, SPANS),
-            whole(SPANS, HD),
+            HBM,
+            HBM,
         ],
-        out_specs=(whole(N, 2, HD), whole(SPANS, HD)),
-        scratch_shapes=[pltpu.VMEM((N * C, HD), F32)],
-        vmem=20,
-    )(back, rowv, colv)
+        out_specs=(whole(N, C, HD), whole(SPANS, HD), VMEM, VMEM),
+        scratch_shapes=[pltpu.VMEM((N * C, HD), F32), pltpu.SemaphoreType.DMA((2,))],
+        vmem=40,
+    )(
+        back,
+        rowv,
+        in_hbm(a_rows.reshape(N, U * S, HD)),
+        in_hbm(b_rows.reshape(N, U * S, HD)),
+    )
     wd = swap(wd_send)
+    terms = call(
+        scale_body,
+        pltpu.HBM((N, U * S, HD), BF),
+        in_specs=[VMEM, VMEM, VMEM],
+        out_specs=HBM,
+        scratch_shapes=[
+            pltpu.VMEM((N, U * S, HD), BF),
+            pltpu.SemaphoreType.DMA((PRODUCT_STEPS,)),
+        ],
+    )(wd, a_rows, b_rows)
+    terms, wts = lax.optimization_barrier((terms, wts))
     attended = call(
         attended_body,
         sds((N, U * C, HD), BF),
         scratch_shapes=[cat, span_table, span_table, column, column],
         flops=2.2e9,
-        vmem=24,
-    )(back, colv, wts)
-    terms = call(
-        scale_body,
-        sds((N, U * S, HD), BF),
-        grid=(N // group,),
-        in_specs=[pl.BlockSpec((group, 2, HD), lambda i: (i, 0, 0)), k_block(U * S), k_block(U * S)],
-        out_specs=k_block(U * S),
-        vmem=16,
-    )(wd, a_rows.reshape(N, U * S, HD), b_rows.reshape(N, U * S, HD))
+        vmem=40,
+    )(back, rowv, wts)
     last = call(
         sum_body,
         sds((N, 2 * U * C, HD), BF),
         scratch_shapes=[cat, span_table, column, column],
         flops=1.1e9,
-        vmem=20,
-    )(swap(terms), attended, colv)
+        vmem=48,
+    )(swap(terms), attended, rowv)
     return call(
         final_body, (sds(queries.shape, BF), sds(queries.shape, BF)), flops=5e8
     )(swap(last))

time: 354 us -> 348 us (0.983)
  local copies, waits for them, and re-layouts: 24.1 us -> 2.79 us
  Pallas kernels: 77.3 us -> 86.9 us
  waiting for transfers between devices: 143 us -> 150 us
    unnamed x35 -> x3, local copies, waits for them, and re-layouts: 23.9 us -> 2.06 us
    all_to_all x5, waiting for transfers between devices: 143 us -> 150 us  [swap(): return lax.all_to_all(rows, 'seq', split_axis=0, concat_axis=0, tiled=True)]
    pallas_call x1, Pallas kernels: 37.1 us -> 42.6 us  [local(): call(forward_body, (sds((S, H // 2, 2 * SPAN, R), F32), sds((S, H // 2, R...]
    pallas_call x7, Pallas kernels: 29.8 us -> 34.2 us  [the longest x1 14.3 us: local(): call(backward_body, pltpu.HBM((N, U, S, HD), BF), grid=(2,), in_specs=[ha...]
  transfers between devices with their start and end apart: 5 -> 5, of which waited for: 5 -> 5; matrix products, arithmetic and copies ran while one was open for 2% -> 2% of each run, Pallas kernels for 16% -> 19%
where the time goes in v5:
time: 348 us; the launch traced here: 347 us
  waiting for transfers between devices  150 us (43%)
  Pallas kernels  86.9 us (25%)
  blocking collectives  65.5 us (19%)
  starting transfers between devices  35.9 us (10%)
  other arithmetic  5.2 us (1%)
    all_to_all x5, waiting for transfers between devices, swap(): return lax.all_to_all(rows, 'seq', split_axis=0, concat_axis=0, tiled=True)  150 us
    all_to_all x2, blocking collectives, swap(): return lax.all_to_all(rows, 'seq', split_axis=0, concat_axis=0, tiled=True)  50.3 us
    pallas_call x1, Pallas kernels, local(): call(forward_body, (sds((S, H // 2, 2 * SPAN, R), F32), sds((S, H // 2, R...  42.6 us
    all_to_all x5, starting transfers between devices, swap(): return lax.all_to_all(rows, 'seq', split_axis=0, concat_axis=0, tiled=True)  35.9 us
    psum x1, blocking collectives, local(): row_scale = lax.rsqrt(lax.psum(square_sums, 'head') / D + 1e-06)  15.2 us
    pallas_call x1, Pallas kernels, local(): call(backward_body, pltpu.HBM((N, U, S, HD), BF), grid=(2,), in_specs=[ha...  14.3 us
    pallas_call x2, Pallas kernels, route(): call(functools.partial(route_body, base), (pltpu.HBM((N, U * S, HD), BF),...  7.75 us
  transfers between devices with their start and end apart: 5, of which 5 were waited for; matrix products, arithmetic and copies ran while one was open for 2% of the time, Pallas kernels for 19%

profile of v5, /device:TPU:1, one launch (start us, length us, event | category | flops | bytes accessed | tf_op | source)
XLA Modules:
  0.0 347.3 jit_solution(4549900041729260404)
XLA Ops:
  1.5 2.8 shard_map.59
  4.2 13.0 %all-to-all-start = ((bf16[64,72,128]{2,1,0:T(8,128)(2,1)}), bf16[64,72,128]{2,1,0:T(8,128)(2,1)S(1)}, u32[]{:S(2)}, u32[]{:S(2)}) async-start(bf16[64,72,128]{2,1,0:T(8,128)(2,1)} %shard_map.59), calls=%async_computation | async-start | bytes 2359296 | tf_op jit(solution)/shard_map/all_to_all | solution.py:463
  17.3 5.1 %multiply_reduce_fusion = f32[32,128]{1,0:T(8,128)S(1)} fusion(bf16[32,128,1024]{2,1,0:T(8,128)(2,1)} %nb_ref.1), kind=kLoop, calls=%fused_computation | loop fusion | flops 12578816 | bytes 8404992 | tf_op jit(solution)/shard_map/reduce_sum | solution.py:512
  22.4 15.2 %psum.7 = f32[32,128]{0,1:T(8,128)S(1)} all-reduce(f32[32,128]{0,1:T(8,128)S(1)} %copy.14), channel_id=1, replica_groups=mesh['seq'=64,'head'=4] {'head'}, use_global_device_ids=true, to_apply=%region_1.2 | all-reduce | flops 4096 | bytes 32768 | tf_op jit(solution)/shard_map/psum | solution.py:513
  38.3 10.3 %all-to-all-done.first_ref = bf16[64,72,128]{2,1,0:T(8,128)(2,1)S(1)} async-done(((bf16[64,72,128]{2,1,0:T(8,128)(2,1)}), bf16[64,72,128]{2,1,0:T(8,128)(2,1)S(1)}, u32[]{:S(2)}, u32[]{:S(2)}) %all-to-all-start) | async-done | bytes 1179680 | tf_op jit(solution)/shard_map/all_to_all | solution.py:463
  48.6 3.6 %shard_map.60 = (bf16[64,128,128]{2,1,0:T(8,128)(2,1)}, f32[8,512]{1,0:T(8,128)S(1)}) custom-call(bf16[64,72,128]{2,1,0:T(8,128)(2,1)S(1)} %all-to-all-done.first_ref), custom_call_target="tpu_custom_call" | custom-call | flops 1100000000 | bytes 4000000 | tf_op jit(solution)/shard_map/pallas_call | solution.py:475
  52.2 6.2 %all-to-all-start.1 = ((bf16[64,128,128]{2,1,0:T(8,128)(2,1)}), bf16[64,128,128]{2,1,0:T(8,128)(2,1)S(1)}, u32[]{:S(2)}, u32[]{:S(2)}) async-start(bf16[64,128,128]{2,1,0:T(8,128)(2,1)} %get-tuple-element.22), calls=%async_computation.1 | async-start | bytes 4194304 | tf_op jit(solution)/shard_map/all_to_all | solution.py:463
  58.4 4.2 %shard_map.62 = (bf16[64,128,128]{2,1,0:T(8,128)(2,1)}, f32[8,512]{1,0:T(8,128)}) custom-call(bf16[64,72,128]{2,1,0:T(8,128)(2,1)S(1)} %all-to-all-done.first_ref), custom_call_target="tpu_custom_call" | custom-call | flops 1100000000 | bytes 4000000 | tf_op jit(solution)/shard_map/pallas_call | solution.py:475
  62.6 47.1 %all-to-all-done.1 = bf16[64,128,128]{2,1,0:T(8,128)(2,1)S(1)} async-done(((bf16[64,128,128]{2,1,0:T(8,128)(2,1)}), bf16[64,128,128]{2,1,0:T(8,128)(2,1)S(1)}, u32[]{:S(2)}, u32[]{:S(2)}) %all-to-all-start.1) | async-done | bytes 2097184 | tf_op jit(solution)/shard_map/all_to_all | solution.py:463
  111.0 5.8 %all-to-all-start.2 = ((bf16[64,128,128]{2,1,0:T(8,128)(2,1)}), bf16[64,128,128]{2,1,0:T(8,128)(2,1)S(1)}, u32[]{:S(2)}, u32[]{:S(2)}) async-start(bf16[64,128,128]{2,1,0:T(8,128)(2,1)} %get-tuple-element.26), calls=%async_computation.2 | async-start | bytes 4194304 | tf_op jit(solution)/shard_map/all_to_all | solution.py:463
  116.8 42.6 %shard_map.61 = (f32[32,2,128,128]{3,2,1,0:T(8,128)}, bf16[32,2,128,256]{3,2,1,0:T(8,128)(2,1)}, bf16[32,2,128,256]{3,2,1,0:T(8,128)(2,1)}, bf16[64,4,32,128]{3,...) custom-call(bf16[64,4,32,128]{3,2,1,0:T(8,128)(2,1)} %bitcast.8, ...), custom_call_target="tpu_custom_call" | custom-call | flops 2000000000 | bytes 30000000 | tf_op jit(solution)/shard_map/pallas_call | solution.py:530
  159.4 8.6 %all-to-all-done.2.g_ref = bf16[64,128,128]{2,1,0:T(8,128)(2,1)S(1)} async-done(((bf16[64,128,128]{2,1,0:T(8,128)(2,1)}), bf16[64,128,128]{2,1,0:T(8,128)(2,1)S(1)}, u32[]{:S(2)}, u32[]{:S(2)}) %all-to-all-start.2) | async-done | bytes 2097184 | tf_op jit(solution)/shard_map/all_to_all | solution.py:463
  168.0 3.7 %shard_map.63 = bf16[64,136,128]{2,1,0:T(8,128)(2,1)} custom-call(bf16[64,128,128]{2,1,0:T(8,128)(2,1)} %bitcast.11, f32[64,8,128]{2,1,0:T(8,128)} %get-tuple-element.25.stat_hbm, bf16[64,128,128]{2,1,0:T(8,128)(2,1)S(1)} %all-to-all-done.2.g_ref), custom_call_target="tpu_custom_call" | custom-call | flops 100000000 | bytes 4000000 | tf_op jit(solution)/shard_map/pallas_call | solution.py:567
  171.7 6.0 %all-to-all-start.3 = ((bf16[64,136,128]{2,1,0:T(8,128)(2,1)}), bf16[64,136,128]{2,1,0:T(8,128)(2,1)}, u32[]{:S(2)}, u32[]{:S(2)}) async-start(bf16[64,136,128]{2,1,0:T(8,128)(2,1)} %shard_map.63), calls=%async_computation.3 | async-start | bytes 4456448 | tf_op jit(solution)/shard_map/all_to_all | solution.py:463
  177.8 14.3 %shard_map.64 = bf16[64,4,32,128]{3,2,1,0:T(8,128)(2,1)} custom-call(bf16[64,4,32,128]{3,2,1,0:T(8,128)(2,1)S(1)} %bitcast.7, f32[32,2,128,128]{3,2,1,0:T(8,128)} %get-tuple-element.27.e_ref, bf16[32,2,128,256]{3,2,1,0:T(8,128)(2,1)} %get-tuple-element.28.k_ref, bf16[32,2,128,256]{3,2,1,0:T(8,128)(2,1)} %get-tuple-element.29.v_ref), custom_call_target="tpu_custom_call" | custom-call | flops 1000000000 | bytes 20000000 | tf_op jit(solution)/shard_map/pallas_call | solution.py:580
  192.1 39.5 %all-to-all-done.3.stat_ref.back_ref = bf16[64,136,128]{2,1,0:T(8,128)(2,1)} async-done(((bf16[64,136,128]{2,1,0:T(8,128)(2,1)}), bf16[64,136,128]{2,1,0:T(8,128)(2,1)}, u32[]{:S(2)}, u32[]{:S(2)}) %all-to-all-start.3) | async-done | bytes 2228256 | tf_op jit(solution)/shard_map/all_to_all | solution.py:463
  231.5 3.1 shard_map.65
  234.7 16.2 %all_to_all.35.wd_ref = bf16[64,8,128]{2,1,0:T(8,128)(2,1)S(1)} all-to-all(bf16[64,8,128]{2,1,0:T(8,128)(2,1)S(1)} %get-tuple-element.34), channel_id=1, replica_groups=mesh['seq'=64,'head'=4] {'seq'}, dimensions={0} | all-to-all | bytes 262144 | tf_op jit(solution)/shard_map/all_to_all | solution.py:463
  250.8 2.5 shard_map.66
  253.4 4.9 %all-to-all-start.5 = ((bf16[64,128,128]{2,1,0:T(8,128)(2,1)}), bf16[64,128,128]{2,1,0:T(8,128)(2,1)S(1)}, u32[]{:S(2)}, u32[]{:S(2)}) async-start(bf16[64,128,128]{2,1,0:T(8,128)(2,1)} %shard_map.66), calls=%async_computation.5 | async-start | bytes 4194304 | tf_op jit(solution)/shard_map/all_to_all | solution.py:463
  258.3 6.5 %shard_map.67.att_ref = bf16[64,32,128]{2,1,0:T(8,128)(2,1)S(1)} custom-call(bf16[64,136,128]{2,1,0:T(8,128)(2,1)} %all-to-all-done.3.stat_ref.back_ref, f32[8,512]{1,0:T(8,128)S(1)} %get-tuple-element.31.row_ref, bf16[512,128]{1,0:T(8,128)(2,1)S(1)} %get-tuple-element.39.wts_ref), custom_call_target="tpu_custom_call" | custom-call | flops 2200000000 | bytes 4000000 | tf_op jit(solution)/shard_map/pallas_call | solution.py:628
  264.8 44.8 %all-to-all-done.5.terms_ref = bf16[64,128,128]{2,1,0:T(8,128)(2,1)S(1)} async-done(((bf16[64,128,128]{2,1,0:T(8,128)(2,1)}), bf16[64,128,128]{2,1,0:T(8,128)(2,1)S(1)}, u32[]{:S(2)}, u32[]{:S(2)}) %all-to-all-start.5) | async-done | bytes 2097184 | tf_op jit(solution)/shard_map/all_to_all | solution.py:463
  309.5 2.1 shard_map.68
  311.6 34.2 %all_to_all.36.in_ref = bf16[64,64,128]{2,1,0:T(8,128)(2,1)S(1)} all-to-all(bf16[64,64,128]{2,1,0:T(8,128)(2,1)S(1)} %shard_map.68), channel_id=1, replica_groups=mesh['seq'=64,'head'=4] {'seq'}, dimensions={0} | all-to-all | bytes 2097152 | tf_op jit(solution)/shard_map/all_to_all | solution.py:463
  (9 shorter events, 4.4 us)
Async XLA Ops:
  4.2 44.4 %all-to-all-start = ((bf16[64,72,128]{2,1,0:T(8,128)(2,1)}), bf16[64,72,128]{2,1,0:T(8,128)(2,1)S(1)}, u32[]{:S(2)}, u32[]{:S(2)}) async-start(bf16[64,72,128]{2,1,0:T(8,128)(2,1)} %shard_map.59), calls=%async_computation | async-start | bytes 2359296 | tf_op jit(solution)/shard_map/all_to_all | solution.py:463
  52.2 57.5 %all-to-all-start.1 = ((bf16[64,128,128]{2,1,0:T(8,128)(2,1)}), bf16[64,128,128]{2,1,0:T(8,128)(2,1)S(1)}, u32[]{:S(2)}, u32[]{:S(2)}) async-start(bf16[64,128,128]{2,1,0:T(8,128)(2,1)} %get-tuple-element.22), calls=%async_computation.1 | async-start | bytes 4194304 | tf_op jit(solution)/shard_map/all_to_all | solution.py:463
  109.7 1.3 copy-start
  111.0 57.1 %all-to-all-start.2 = ((bf16[64,128,128]{2,1,0:T(8,128)(2,1)}), bf16[64,128,128]{2,1,0:T(8,128)(2,1)S(1)}, u32[]{:S(2)}, u32[]{:S(2)}) async-start(bf16[64,128,128]{2,1,0:T(8,128)(2,1)} %get-tuple-element.26), calls=%async_computation.2 | async-start | bytes 4194304 | tf_op jit(solution)/shard_map/all_to_all | solution.py:463
  171.7 59.8 %all-to-all-start.3 = ((bf16[64,136,128]{2,1,0:T(8,128)(2,1)}), bf16[64,136,128]{2,1,0:T(8,128)(2,1)}, u32[]{:S(2)}, u32[]{:S(2)}) async-start(bf16[64,136,128]{2,1,0:T(8,128)(2,1)} %shard_map.63), calls=%async_computation.3 | async-start | bytes 4456448 | tf_op jit(solution)/shard_map/all_to_all | solution.py:463
  253.4 56.1 %all-to-all-start.5 = ((bf16[64,128,128]{2,1,0:T(8,128)(2,1)}), bf16[64,128,128]{2,1,0:T(8,128)(2,1)S(1)}, u32[]{:S(2)}, u32[]{:S(2)}) async-start(bf16[64,128,128]{2,1,0:T(8,128)(2,1)} %shard_map.66), calls=%async_computation.5 | async-start | bytes 4194304 | tf_op jit(solution)/shard_map/all_to_all | solution.py:463

commit v6 on v5

--- a/solution.py
+++ b/solution.py
@@ -267,7 +267,7 @@
                 rows.append(total[:, None, :])
             stat_ref[h * TB : (h + 1) * TB] = jnp.where(
                 place == 0, rows[0], jnp.where(place == 1, rows[1], 0.0)
-            )
+            ).astype(BF)
 
 
 def backward_body(g_ref, e_ref, k_ref, v_ref, a_ref, gs, as_):
@@ -321,52 +321,41 @@
         lax.fori_loop(0, SPANS // size, step, 0)
 
 
-def product_body(p_hbm, stat_hbm, g_ref, out_hbm, rows_ref, stat_ref, in_sem, out_sem):
+def weight_body(
+    back_ref, g_hbm, row_ref, a_hbm, b_hbm, wd_ref, wts_ref, a_ref, b_ref, g_ref, flat, in_sem, sem
+):
     size = U * S
     per = N // PRODUCT_STEPS
-    diagonal = iota((size, HD), 0) == iota((size, HD), 1)
-    row = iota((C, HD), 0)
 
     def load(i):
         at = pl.ds(i * per, per)
-        return (
-            pltpu.make_async_copy(p_hbm.at[at], rows_ref.at[at, pl.ds(0, size)], in_sem.at[0, i]),
-            pltpu.make_async_copy(stat_hbm.at[at], stat_ref.at[at], in_sem.at[1, i]),
-        )
-
-    def store(i):
-        at = pl.ds(i * per, per)
-        return pltpu.make_async_copy(rows_ref.at[at], out_hbm.at[at], out_sem.at[i])
-
+        return pltpu.make_async_copy(g_hbm.at[at], g_ref.at[at], in_sem.at[i])
+
+    later = [
+        pltpu.make_async_copy(src, dst, sem.at[i])
+        for i, (src, dst) in enumerate(((a_hbm, a_ref), (b_hbm, b_ref)))
+    ]
     for i in range(PRODUCT_STEPS):
-        for copy in load(i):
-            copy.start()
+        load(i).start()
+    cols = jnp.transpose(row_ref[...])
+    lane = iota((SPANS, HD), 1)
+    diagonal = iota((size, HD), 0) == iota((size, HD), 1)
+    place = iota((C, HD), 0)
     for i in range(PRODUCT_STEPS):
-        for copy in load(i):
-            copy.wait()
-        for k in range(i * per, (i + 1) * per):
-            prod = rows_ref[k, :size, :].astype(F32) * g_ref[k].astype(F32)
+        load(i).wait()
+        if i == PRODUCT_STEPS // 2:
+            for copy in later:
+                copy.start()
+        for j in range(i * per, (i + 1) * per):
+            prod = back_ref[j, :size, :].astype(F32) * g_ref[j].astype(F32)
             prod = jnp.where(diagonal, jnp.sum(prod, axis=1, keepdims=True), 0.0)
             total = jnp.sum(prod, axis=0, keepdims=True)
             high = total.astype(BF).astype(F32)
-            rows_ref[k, size:, :] = jnp.where(
-                row == 2, high, jnp.where(row == 3, total - high, stat_ref[k])
-            ).astype(BF)
-        store(i).start()
-    for i in range(PRODUCT_STEPS):
-        store(i).wait()
-
-
-def weight_body(stat_ref, row_ref, a_hbm, b_hbm, wd_ref, wts_ref, a_ref, b_ref, flat, sem):
-    loads = [
-        pltpu.make_async_copy(src, dst, sem.at[i])
-        for i, (src, dst) in enumerate(((a_hbm, a_ref), (b_hbm, b_ref)))
-    ]
-    for load in loads:
-        load.start()
-    cols = jnp.transpose(row_ref[...])
-    lane = iota((SPANS, HD), 1)
-    flat[...] = stat_ref[...].astype(F32).reshape(N * C, HD)
+            flat[j * C : (j + 1) * C, :] = jnp.where(
+                place == 2,
+                high,
+                jnp.where(place == 3, total - high, back_ref[j, size:, :].astype(F32)),
+            )
     stats = jnp.concatenate(
         [flat[pl.ds(i, N, stride=C), :].astype(BF) for i in range(4)], axis=1
     )
@@ -401,8 +390,8 @@
     wd_ref[...] = jnp.where(
         place == 0, out[:, None, :HD], jnp.where(place == 1, out[:, None, HD:], 0.0)
     ).astype(BF)
-    for load in loads:
-        load.wait()
+    for copy in later:
+        copy.wait()
 
 
 def attended_body(
@@ -535,7 +524,7 @@
             sds((S, H // 2, R, 2 * HD), BF),
             pltpu.HBM((N, U, S, HD), BF),
             pltpu.HBM((N, U, S, HD), BF),
-            pltpu.HBM((N, C, HD), F32),
+            sds((N, C, HD), BF),
         ),
         grid=(2,),
         in_specs=[
@@ -563,20 +552,9 @@
         nbytes=3e7,
         vmem=56,
     )(in_hbm(cut(got_q)), neighbours, row_scale)
-    back = swap(
-        call(
-            product_body,
-            pltpu.HBM((N, U * S + C, HD), BF),
-            in_specs=[HBM, HBM, VMEM],
-            out_specs=HBM,
-            scratch_shapes=[
-                pltpu.VMEM((N, U * S + C, HD), BF),
-                pltpu.VMEM((N, C, HD), F32),
-                pltpu.SemaphoreType.DMA((2, PRODUCT_STEPS)),
-                pltpu.SemaphoreType.DMA((PRODUCT_STEPS,)),
-            ],
-        )(in_hbm(p_send.reshape(N, U * S, HD)), in_hbm(stats), got_g)
-    )
+    back_send = jnp.concatenate([p_send.reshape(N, U * S, HD), stats], axis=1)
+    back_send, got_g = lax.optimization_barrier((back_send, got_g))
+    back = swap(back_send)
     a_rows = call(
         backward_body,
         pltpu.HBM((N, U, S, HD), BF),
@@ -597,18 +575,16 @@
     wd_send, wts, a_rows, b_rows = call(
         weight_body,
         (sds((N, C, HD), BF), sds((SPANS, HD), BF), rows, rows),
-        grid=(1,),
-        in_specs=[
-            pl.BlockSpec((N, C, HD), lambda i: (0, U * S // C, 0)),
-            whole(8, SPANS),
-            HBM,
-            HBM,
+        in_specs=[VMEM, HBM, VMEM, HBM, HBM],
+        scratch_shapes=[
+            pltpu.VMEM((N, U * S, HD), BF),
+            pltpu.VMEM((N * C, HD), F32),
+            pltpu.SemaphoreType.DMA((PRODUCT_STEPS,)),
+            pltpu.SemaphoreType.DMA((2,)),
         ],
-        out_specs=(whole(N, C, HD), whole(SPANS, HD), VMEM, VMEM),
-        scratch_shapes=[pltpu.VMEM((N * C, HD), F32), pltpu.SemaphoreType.DMA((2,))],
-        vmem=40,
     )(
         back,
+        in_hbm(g_send),
         rowv,
         in_hbm(a_rows.reshape(N, U * S, HD)),
         in_hbm(b_rows.reshape(N, U * S, HD)),
@@ -631,7 +607,7 @@
         scratch_shapes=[cat, span_table, span_table, column, column],
         flops=2.2e9,
         vmem=40,
-    )(back, rowv, wts)
+    )(in_hbm(back), rowv, wts)
     last = call(
         sum_body,
         sds((N, 2 * U * C, HD), BF),

time: 348 us -> 347 us (level)
  waiting for transfers between devices: 150 us -> 146 us
    all_to_all x5, waiting for transfers between devices: 150 us -> 146 us  [swap(): return lax.all_to_all(rows, 'seq', split_axis=0, concat_axis=0, tiled=True)]
    pallas_call x1 -> x0, Pallas kernels: 3.7 us -> none  [local(): call(product_body, pltpu.HBM((N, U * S + C, HD), BF), in_specs=[HBM, HBM,...]
  transfers between devices with their start and end apart: 5 -> 5, of which waited for: 5 -> 5; matrix products, arithmetic and copies ran while one was open for 2% -> 3% of each run, Pallas kernels for 19% -> 19%
where the time goes in v6:
time: 347 us; the launch traced here: 346 us
  waiting for transfers between devices  146 us (42%)
  Pallas kernels  84.7 us (24%)
  blocking collectives  65.5 us (19%)
  starting transfers between devices  35.7 us (10%)
  other arithmetic  8.45 us (2%)
  local copies, waits for them, and re-layouts  5.72 us (2%)
    all_to_all x5, waiting for transfers between devices, swap(): return lax.all_to_all(rows, 'seq', split_axis=0, concat_axis=0, tiled=True)  146 us
    all_to_all x2, blocking collectives, swap(): return lax.all_to_all(rows, 'seq', split_axis=0, concat_axis=0, tiled=True)  50.3 us
    pallas_call x1, Pallas kernels, local(): call(forward_body, (sds((S, H // 2, 2 * SPAN, R), F32), sds((S, H // 2, R...  42.6 us
    all_to_all x5, starting transfers between devices, swap(): return lax.all_to_all(rows, 'seq', split_axis=0, concat_axis=0, tiled=True)  35.7 us
    psum x1, blocking collectives, local(): row_scale = lax.rsqrt(lax.psum(square_sums, 'head') / D + 1e-06)  15.2 us
    pallas_call x1, Pallas kernels, local(): call(backward_body, pltpu.HBM((N, U, S, HD), BF), grid=(2,), in_specs=[ha...  14.3 us
    pallas_call x2, Pallas kernels, route(): call(functools.partial(route_body, base), (pltpu.HBM((N, U * S, HD), BF),...  7.76 us
  transfers between devices with their start and end apart: 5, of which 5 were waited for; matrix products, arithmetic and copies ran while one was open for 3% of the time, Pallas kernels for 19%

profile of v6, /device:TPU:1, one launch (start us, length us, event | category | flops | bytes accessed | tf_op | source)
XLA Modules:
  0.0 346.4 jit_solution(228203237167660371)
XLA Ops:
  1.5 2.8 shard_map.59
  4.2 13.0 %all-to-all-start = ((bf16[64,72,128]{2,1,0:T(8,128)(2,1)}), bf16[64,72,128]{2,1,0:T(8,128)(2,1)S(1)}, u32[]{:S(2)}, u32[]{:S(2)}) async-start(bf16[64,72,128]{2,1,0:T(8,128)(2,1)} %shard_map.59), calls=%async_computation | async-start | bytes 2359296 | tf_op jit(solution)/shard_map/all_to_all | solution.py:452
  17.2 5.1 %multiply_reduce_fusion = f32[32,128]{1,0:T(8,128)S(1)} fusion(bf16[32,128,1024]{2,1,0:T(8,128)(2,1)} %nb_ref.1), kind=kLoop, calls=%fused_computation | loop fusion | flops 12578816 | bytes 8404992 | tf_op jit(solution)/shard_map/reduce_sum | solution.py:501
  22.4 15.2 %psum.7 = f32[32,128]{0,1:T(8,128)S(1)} all-reduce(f32[32,128]{0,1:T(8,128)S(1)} %copy.14), channel_id=1, replica_groups=mesh['seq'=64,'head'=4] {'head'}, use_global_device_ids=true, to_apply=%region_1.2 | all-reduce | flops 4096 | bytes 32768 | tf_op jit(solution)/shard_map/psum | solution.py:502
  38.3 10.3 %all-to-all-done.first_ref = bf16[64,72,128]{2,1,0:T(8,128)(2,1)S(1)} async-done(((bf16[64,72,128]{2,1,0:T(8,128)(2,1)}), bf16[64,72,128]{2,1,0:T(8,128)(2,1)S(1)}, u32[]{:S(2)}, u32[]{:S(2)}) %all-to-all-start) | async-done | bytes 1179680 | tf_op jit(solution)/shard_map/all_to_all | solution.py:452
  48.6 3.6 %shard_map.60 = (bf16[64,128,128]{2,1,0:T(8,128)(2,1)}, f32[8,512]{1,0:T(8,128)S(1)}) custom-call(bf16[64,72,128]{2,1,0:T(8,128)(2,1)S(1)} %all-to-all-done.first_ref), custom_call_target="tpu_custom_call" | custom-call | flops 1100000000 | bytes 4000000 | tf_op jit(solution)/shard_map/pallas_call | solution.py:464
  52.2 6.2 %all-to-all-start.1 = ((bf16[64,128,128]{2,1,0:T(8,128)(2,1)}), bf16[64,128,128]{2,1,0:T(8,128)(2,1)S(1)}, u32[]{:S(2)}, u32[]{:S(2)}) async-start(bf16[64,128,128]{2,1,0:T(8,128)(2,1)} %get-tuple-element.24), calls=%async_computation.1 | async-start | bytes 4194304 | tf_op jit(solution)/shard_map/all_to_all | solution.py:452
  58.4 4.2 %shard_map.62 = (bf16[64,128,128]{2,1,0:T(8,128)(2,1)}, f32[8,512]{1,0:T(8,128)}) custom-call(bf16[64,72,128]{2,1,0:T(8,128)(2,1)S(1)} %all-to-all-done.first_ref), custom_call_target="tpu_custom_call" | custom-call | flops 1100000000 | bytes 4000000 | tf_op jit(solution)/shard_map/pallas_call | solution.py:464
  62.6 47.1 %all-to-all-done.1 = bf16[64,128,128]{2,1,0:T(8,128)(2,1)S(1)} async-done(((bf16[64,128,128]{2,1,0:T(8,128)(2,1)}), bf16[64,128,128]{2,1,0:T(8,128)(2,1)S(1)}, u32[]{:S(2)}, u32[]{:S(2)}) %all-to-all-start.1) | async-done | bytes 2097184 | tf_op jit(solution)/shard_map/all_to_all | solution.py:452
  111.0 5.8 %all-to-all-start.2 = ((bf16[64,128,128]{2,1,0:T(8,128)(2,1)}), bf16[64,128,128]{2,1,0:T(8,128)(2,1)S(1)}, u32[]{:S(2)}, u32[]{:S(2)}) async-start(bf16[64,128,128]{2,1,0:T(8,128)(2,1)} %get-tuple-element.28.g_hbm), calls=%async_computation.2 | async-start | bytes 4194304 | tf_op jit(solution)/shard_map/all_to_all | solution.py:452
  116.8 42.6 %shard_map.61 = (f32[32,2,128,128]{3,2,1,0:T(8,128)}, bf16[32,2,128,256]{3,2,1,0:T(8,128)(2,1)}, bf16[32,2,128,256]{3,2,1,0:T(8,128)(2,1)}, bf16[64,4,32,128]{3,...) custom-call(bf16[64,4,32,128]{3,2,1,0:T(8,128)(2,1)} %bitcast.8, ...), custom_call_target="tpu_custom_call" | custom-call | flops 2000000000 | bytes 30000000 | tf_op jit(solution)/shard_map/pallas_call | solution.py:519
  159.4 3.2 pad_maximum_fusion
  162.6 5.4 %all-to-all-done.2 = bf16[64,128,128]{2,1,0:T(8,128)(2,1)S(1)} async-done(((bf16[64,128,128]{2,1,0:T(8,128)(2,1)}), bf16[64,128,128]{2,1,0:T(8,128)(2,1)S(1)}, u32[]{:S(2)}, u32[]{:S(2)}) %all-to-all-start.2) | async-done | bytes 2097184 | tf_op jit(solution)/shard_map/all_to_all | solution.py:452
  169.4 5.8 %all-to-all-start.3 = ((bf16[64,136,128]{2,1,0:T(8,128)(2,1)}), bf16[64,136,128]{2,1,0:T(8,128)(2,1)S(1)}, u32[]{:S(2)}, u32[]{:S(2)}) async-start(bf16[64,136,128]{2,1,0:T(8,128)(2,1)} %pad_maximum_fusion), calls=%async_computation.3 | async-start | bytes 4456448 | tf_op jit(solution)/shard_map/all_to_all | solution.py:452
  176.8 14.3 %shard_map.63 = bf16[64,4,32,128]{3,2,1,0:T(8,128)(2,1)} custom-call(bf16[64,4,32,128]{3,2,1,0:T(8,128)(2,1)S(1)} %bitcast.7, f32[32,2,128,128]{3,2,1,0:T(8,128)} %get-tuple-element.31.e_ref, bf16[32,2,128,256]{3,2,1,0:T(8,128)(2,1)} %get-tuple-element.32.k_ref, bf16[32,2,128,256]{3,2,1,0:T(8,128)(2,1)} %get-tuple-element.33.v_ref), custom_call_target="tpu_custom_call" | custom-call | flops 1000000000 | bytes 20000000 | tf_op jit(solution)/shard_map/pallas_call | solution.py:558
  191.1 37.9 %all-to-all-done.3.back_ref = bf16[64,136,128]{2,1,0:T(8,128)(2,1)S(1)} async-done(((bf16[64,136,128]{2,1,0:T(8,128)(2,1)}), bf16[64,136,128]{2,1,0:T(8,128)(2,1)S(1)}, u32[]{:S(2)}, u32[]{:S(2)}) %all-to-all-start.3) | async-done | bytes 2228256 | tf_op jit(solution)/shard_map/all_to_all | solution.py:452
  229.0 4.7 %shard_map.64 = (bf16[64,8,128]{2,1,0:T(8,128)(2,1)S(1)}, bf16[512,128]{1,0:T(8,128)(2,1)S(1)}, bf16[64,128,128]{2,1,0:T(8,128)(2,1)S(1)}, bf16[64,128,128]{2,1,0:T(8,128)(2,1)S(1)}) custom-call(bf16[64,136,128]{2,1,0:T(8,128)(2,1)S(1)} %all-to-all-done.3.back_ref, bf16[64,128,128]{2,1,0:T(8,128)(2,1)} %get-tuple-element.28.g_hbm, ...), custom_call_target="tpu_custom_call" | custom-call | flops 100000000 | bytes 4000000 | tf_op jit(solution)/shard_map/pallas_call | solution.py:575
  233.8 16.2 %all_to_all.35.wd_ref = bf16[64,8,128]{2,1,0:T(8,128)(2,1)S(1)} all-to-all(bf16[64,8,128]{2,1,0:T(8,128)(2,1)S(1)} %get-tuple-element.38), channel_id=1, replica_groups=mesh['seq'=64,'head'=4] {'seq'}, dimensions={0} | all-to-all | bytes 262144 | tf_op jit(solution)/shard_map/all_to_all | solution.py:452
  250.0 2.5 shard_map.65
  252.5 4.9 %all-to-all-start.5 = ((bf16[64,128,128]{2,1,0:T(8,128)(2,1)}), bf16[64,128,128]{2,1,0:T(8,128)(2,1)S(1)}, u32[]{:S(2)}, u32[]{:S(2)}) async-start(bf16[64,128,128]{2,1,0:T(8,128)(2,1)} %shard_map.65), calls=%async_computation.5 | async-start | bytes 4194304 | tf_op jit(solution)/shard_map/all_to_all | solution.py:452
  257.4 6.5 %shard_map.66.att_ref = bf16[64,32,128]{2,1,0:T(8,128)(2,1)S(1)} custom-call(bf16[64,136,128]{2,1,0:T(8,128)(2,1)} %copy-done, f32[8,512]{1,0:T(8,128)S(1)} %get-tuple-element.35.row_ref, bf16[512,128]{1,0:T(8,128)(2,1)S(1)} %get-tuple-element.43.wts_ref), custom_call_target="tpu_custom_call" | custom-call | flops 2200000000 | bytes 4000000 | tf_op jit(solution)/shard_map/pallas_call | solution.py:604
  263.9 44.8 %all-to-all-done.5.terms_ref = bf16[64,128,128]{2,1,0:T(8,128)(2,1)S(1)} async-done(((bf16[64,128,128]{2,1,0:T(8,128)(2,1)}), bf16[64,128,128]{2,1,0:T(8,128)(2,1)S(1)}, u32[]{:S(2)}, u32[]{:S(2)}) %all-to-all-start.5) | async-done | bytes 2097184 | tf_op jit(solution)/shard_map/all_to_all | solution.py:452
  308.6 2.1 shard_map.67
  310.7 34.2 %all_to_all.36.in_ref = bf16[64,64,128]{2,1,0:T(8,128)(2,1)S(1)} all-to-all(bf16[64,64,128]{2,1,0:T(8,128)(2,1)S(1)} %shard_map.67), channel_id=1, replica_groups=mesh['seq'=64,'head'=4] {'seq'}, dimensions={0} | all-to-all | bytes 2097152 | tf_op jit(solution)/shard_map/all_to_all | solution.py:452
  (15 shorter events, 7.3 us)
Async XLA Ops:
  4.2 44.4 %all-to-all-start = ((bf16[64,72,128]{2,1,0:T(8,128)(2,1)}), bf16[64,72,128]{2,1,0:T(8,128)(2,1)S(1)}, u32[]{:S(2)}, u32[]{:S(2)}) async-start(bf16[64,72,128]{2,1,0:T(8,128)(2,1)} %shard_map.59), calls=%async_computation | async-start | bytes 2359296 | tf_op jit(solution)/shard_map/all_to_all | solution.py:452
  52.2 57.5 %all-to-all-start.1 = ((bf16[64,128,128]{2,1,0:T(8,128)(2,1)}), bf16[64,128,128]{2,1,0:T(8,128)(2,1)S(1)}, u32[]{:S(2)}, u32[]{:S(2)}) async-start(bf16[64,128,128]{2,1,0:T(8,128)(2,1)} %get-tuple-element.24), calls=%async_computation.1 | async-start | bytes 4194304 | tf_op jit(solution)/shard_map/all_to_all | solution.py:452
  109.7 1.3 copy-start.3
  111.0 57.1 %all-to-all-start.2 = ((bf16[64,128,128]{2,1,0:T(8,128)(2,1)}), bf16[64,128,128]{2,1,0:T(8,128)(2,1)S(1)}, u32[]{:S(2)}, u32[]{:S(2)}) async-start(bf16[64,128,128]{2,1,0:T(8,128)(2,1)} %get-tuple-element.28.g_hbm), calls=%async_computation.2 | async-start | bytes 4194304 | tf_op jit(solution)/shard_map/all_to_all | solution.py:452
  168.1 1.3 copy-start.1
  169.4 59.7 %all-to-all-start.3 = ((bf16[64,136,128]{2,1,0:T(8,128)(2,1)}), bf16[64,136,128]{2,1,0:T(8,128)(2,1)S(1)}, u32[]{:S(2)}, u32[]{:S(2)}) async-start(bf16[64,136,128]{2,1,0:T(8,128)(2,1)} %pad_maximum_fusion), calls=%async_computation.3 | async-start | bytes 4456448 | tf_op jit(solution)/shard_map/all_to_all | solution.py:452
  175.2 1.6 copy-start.2
  229.0 4.7 %copy-start = (bf16[64,136,128]{2,1,0:T(8,128)(2,1)}, bf16[64,136,128]{2,1,0:T(8,128)(2,1)S(1)}, u32[]{:S(2)}) copy-start(bf16[64,136,128]{2,1,0:T(8,128)(2,1)S(1)} %all-to-all-done.3.back_ref) | copy-start | bytes 6684676
  252.5 56.1 %all-to-all-start.5 = ((bf16[64,128,128]{2,1,0:T(8,128)(2,1)}), bf16[64,128,128]{2,1,0:T(8,128)(2,1)S(1)}, u32[]{:S(2)}, u32[]{:S(2)}) async-start(bf16[64,128,128]{2,1,0:T(8,128)(2,1)} %shard_map.65), calls=%async_computation.5 | async-start | bytes 4194304 | tf_op jit(solution)/shard_map/all_to_all | solution.py:452

commit v7 on v6

--- a/solution.py
+++ b/solution.py
@@ -70,17 +70,28 @@
     return (piece_row % C) * SPAN + ((piece_row // C) % U) * TB + piece_row // (U * C)
 
 
-def prep_body(q_hbm, g_hbm, digits_ref, out_hbm, q_ref, g_ref, order, stage, in_sem, out_sem):
+def prep_body(
+    q_hbm, g_hbm, slot_hbm, out_hbm, q_ref, g_ref, slot_ref, table, order, stage, in_sem, out_sem
+):
     size = C * SPAN
     loads = [
         pltpu.make_async_copy(src, dst, in_sem.at[i])
-        for i, (src, dst) in enumerate(((q_hbm, q_ref), (g_hbm, g_ref)))
+        for i, (src, dst) in enumerate(
+            ((slot_hbm, slot_ref), (q_hbm, q_ref), (g_hbm, g_ref))
+        )
     ]
     for load in loads:
         load.start()
     order[...] = hot(iota((size, size), 1) == token_row(iota((size, size), 0)))
-    stage[:, 2 * U * C :, :] = jnp.broadcast_to(digits_ref[...][None], (N, C, HD))
-    for load in loads:
+    loads[0].wait()
+    table[...] = jnp.zeros_like(table)
+    table[0:2, 0:C] = (slot_ref[...] // S).astype(F32)
+    table[2:4, 0:C] = (slot_ref[...] % S).astype(F32)
+    digits = jnp.transpose(table[...])[:C]
+    table[...] = jnp.zeros_like(table)
+    table[:, 0:C] = digits
+    stage[:, 2 * U * C :, :] = jnp.broadcast_to(table[...][None], (N, C, HD)).astype(BF)
+    for load in loads[1:]:
         load.wait()
     stores = []
     half = H // 2
@@ -119,7 +130,7 @@
     return [wide[:, u * C : (u + 1) * C, :].reshape(SPANS, HD) for u in range(U)]
 
 
-def route_body(base, first_ref, out_hbm, row_ref, x_ref, out_ref, out_sem):
+def route_body(base, first_ref, out_hbm, row_ref, x_ref, ids_ref, out_ref, out_sem):
     digits = first_ref[:, 2 * U * C :, :].astype(F32).reshape(SPANS, HD)
     lane = iota((SPANS, HD), 1)
     slot_part = pltpu.roll(digits, HD - 2, 1)
@@ -137,9 +148,13 @@
         at = pl.ds(pl.multiple_of(j * per, per), per)
         return pltpu.make_async_copy(out_ref.at[at], out_hbm.at[at], out_sem.at[j])
 
+    ids_ref[...] = iota((per * S, SPANS), 0).astype(F32).astype(BF)
+
     def step(j, _):
-        ids = (iota((per * S, SPANS), 0) + j * (per * S)).astype(F32)
-        hit = hot((ids == slot_a) | (ids == slot_b))
+        first_id = (j * (per * S)).astype(F32)
+        ids = ids_ref[...]
+        hit = (ids == (slot_a - first_id).astype(BF)) | (ids == (slot_b - first_id).astype(BF))
+        hit = jnp.where(hit, jnp.ones_like(ids), jnp.zeros_like(ids))
         got = mm(hit, x_ref[...]).astype(BF)
         at = pl.ds(pl.multiple_of(j * per, per), per)
         for u in range(U):
@@ -468,6 +483,7 @@
         out_specs=(HBM, VMEM),
         scratch_shapes=[
             pltpu.VMEM((SPANS, W), BF),
+            pltpu.VMEM((SLOTS // ROUTE_STEPS, SPANS), BF),
             pltpu.VMEM((N, U * S, HD), BF),
             pltpu.SemaphoreType.DMA((ROUTE_STEPS,)),
         ],
@@ -476,27 +492,26 @@
 
 
 def local(queries, out_grad, neighbours, placement):
-    owner, place = placement // S, placement % S
-    digits = jnp.concatenate([owner, place], axis=1).astype(BF)
-    digits = jnp.pad(digits, ((0, 0), (0, HD - 4)))
     rows_in = 2 * U * C + C
     tokens = pltpu.VMEM(queries.shape, BF)
     first = swap(
         call(
             prep_body,
             pltpu.HBM((N, rows_in, HD), BF),
-            in_specs=[HBM, HBM, VMEM],
+            in_specs=[HBM, HBM, HBM],
             out_specs=HBM,
             scratch_shapes=[
                 tokens,
                 tokens,
+                pltpu.VMEM((2, C), jnp.int32),
+                pltpu.VMEM((C, HD), F32),
                 pltpu.VMEM((C * SPAN, C * SPAN), BF),
                 pltpu.VMEM((N, rows_in, HD), BF),
-                pltpu.SemaphoreType.DMA((2,)),
+                pltpu.SemaphoreType.DMA((3,)),
                 pltpu.SemaphoreType.DMA((2,)),
             ],
             flops=5e8,
-        )(in_hbm(queries), in_hbm(out_grad), digits)
+        )(in_hbm(queries), in_hbm(out_grad), in_hbm(placement.T))
     )
     square_sums = jnp.sum(jnp.square(neighbours.astype(F32)), axis=-1)
     row_scale = lax.rsqrt(lax.psum(square_sums, "head") / D + 1e-06)

time: 347 us -> 346 us (level)
  transfers between devices with their start and end apart: 5 -> 5, of which waited for: 5 -> 5; matrix products, arithmetic and copies ran while one was open for 3% -> 3% of each run, Pallas kernels for 19% -> 20%
where the time goes in v7:
time: 346 us; the launch traced here: 345 us
  waiting for transfers between devices  146 us (42%)
  Pallas kernels  84.5 us (24%)
  blocking collectives  65.5 us (19%)
  starting transfers between devices  35.7 us (10%)
  other arithmetic  8.36 us (2%)
  local copies, waits for them, and re-layouts  4.95 us (1%)
    all_to_all x5, waiting for transfers between devices, swap(): return lax.all_to_all(rows, 'seq', split_axis=0, concat_axis=0, tiled=True)  146 us
    all_to_all x2, blocking collectives, swap(): return lax.all_to_all(rows, 'seq', split_axis=0, concat_axis=0, tiled=True)  50.3 us
    pallas_call x1, Pallas kernels, local(): call(forward_body, (sds((S, H // 2, 2 * SPAN, R), F32), sds((S, H // 2, R...  42.6 us
    all_to_all x5, starting transfers between devices, swap(): return lax.all_to_all(rows, 'seq', split_axis=0, concat_axis=0, tiled=True)  35.7 us
    psum x1, blocking collectives, local(): row_scale = lax.rsqrt(lax.psum(square_sums, 'head') / D + 1e-06)  15.2 us
    pallas_call x1, Pallas kernels, local(): call(backward_body, pltpu.HBM((N, U, S, HD), BF), grid=(2,), in_specs=[ha...  14.3 us
    pallas_call x2, Pallas kernels, route(): call(functools.partial(route_body, base), (pltpu.HBM((N, U * S, HD), BF),...  7.56 us
  transfers between devices with their start and end apart: 5, of which 5 were waited for; matrix products, arithmetic and copies ran while one was open for 3% of the time, Pallas kernels for 20%

profile of v7, /device:TPU:1, one launch (start us, length us, event | category | flops | bytes accessed | tf_op | source)
XLA Modules:
  0.0 345.5 jit_solution(10010218732222889239)
XLA Ops:
  0.6 2.8 shard_map.59
  3.4 13.0 %all-to-all-start = ((bf16[64,72,128]{2,1,0:T(8,128)(2,1)}), bf16[64,72,128]{2,1,0:T(8,128)(2,1)S(1)}, u32[]{:S(2)}, u32[]{:S(2)}) async-start(bf16[64,72,128]{2,1,0:T(8,128)(2,1)} %shard_map.59), calls=%async_computation | async-start | bytes 2359296 | tf_op jit(solution)/shard_map/all_to_all | solution.py:467
  16.4 5.1 %multiply_reduce_fusion = f32[32,128]{1,0:T(8,128)S(1)} fusion(bf16[32,128,1024]{2,1,0:T(8,128)(2,1)} %nb_ref.1), kind=kLoop, calls=%fused_computation | loop fusion | flops 12578816 | bytes 8404992 | tf_op jit(solution)/shard_map/reduce_sum | solution.py:516
  21.6 15.2 %psum.7 = f32[32,128]{0,1:T(8,128)S(1)} all-reduce(f32[32,128]{0,1:T(8,128)S(1)} %copy.6), channel_id=1, replica_groups=mesh['seq'=64,'head'=4] {'head'}, use_global_device_ids=true, to_apply=%region_1.0 | all-reduce | flops 4096 | bytes 32768 | tf_op jit(solution)/shard_map/psum | solution.py:517
  37.5 10.3 %all-to-all-done.first_ref = bf16[64,72,128]{2,1,0:T(8,128)(2,1)S(1)} async-done(((bf16[64,72,128]{2,1,0:T(8,128)(2,1)}), bf16[64,72,128]{2,1,0:T(8,128)(2,1)S(1)}, u32[]{:S(2)}, u32[]{:S(2)}) %all-to-all-start) | async-done | bytes 1179680 | tf_op jit(solution)/shard_map/all_to_all | solution.py:467
  47.8 3.5 %shard_map.60 = (bf16[64,128,128]{2,1,0:T(8,128)(2,1)}, f32[8,512]{1,0:T(8,128)S(1)}) custom-call(bf16[64,72,128]{2,1,0:T(8,128)(2,1)S(1)} %all-to-all-done.first_ref), custom_call_target="tpu_custom_call" | custom-call | flops 1100000000 | bytes 4000000 | tf_op jit(solution)/shard_map/pallas_call | solution.py:479
  51.3 6.2 %all-to-all-start.1 = ((bf16[64,128,128]{2,1,0:T(8,128)(2,1)}), bf16[64,128,128]{2,1,0:T(8,128)(2,1)S(1)}, u32[]{:S(2)}, u32[]{:S(2)}) async-start(bf16[64,128,128]{2,1,0:T(8,128)(2,1)} %get-tuple-element.24), calls=%async_computation.1 | async-start | bytes 4194304 | tf_op jit(solution)/shard_map/all_to_all | solution.py:467
  57.5 4.1 %shard_map.62 = (bf16[64,128,128]{2,1,0:T(8,128)(2,1)}, f32[8,512]{1,0:T(8,128)}) custom-call(bf16[64,72,128]{2,1,0:T(8,128)(2,1)S(1)} %all-to-all-done.first_ref), custom_call_target="tpu_custom_call" | custom-call | flops 1100000000 | bytes 4000000 | tf_op jit(solution)/shard_map/pallas_call | solution.py:479
  61.6 47.2 %all-to-all-done.1 = bf16[64,128,128]{2,1,0:T(8,128)(2,1)S(1)} async-done(((bf16[64,128,128]{2,1,0:T(8,128)(2,1)}), bf16[64,128,128]{2,1,0:T(8,128)(2,1)S(1)}, u32[]{:S(2)}, u32[]{:S(2)}) %all-to-all-start.1) | async-done | bytes 2097184 | tf_op jit(solution)/shard_map/all_to_all | solution.py:467
  110.1 5.8 %all-to-all-start.2 = ((bf16[64,128,128]{2,1,0:T(8,128)(2,1)}), bf16[64,128,128]{2,1,0:T(8,128)(2,1)S(1)}, u32[]{:S(2)}, u32[]{:S(2)}) async-start(bf16[64,128,128]{2,1,0:T(8,128)(2,1)} %get-tuple-element.28.g_hbm), calls=%async_computation.2 | async-start | bytes 4194304 | tf_op jit(solution)/shard_map/all_to_all | solution.py:467
  115.9 42.6 %shard_map.61 = (f32[32,2,128,128]{3,2,1,0:T(8,128)}, bf16[32,2,128,256]{3,2,1,0:T(8,128)(2,1)}, bf16[32,2,128,256]{3,2,1,0:T(8,128)(2,1)}, bf16[64,4,32,128]{3,...) custom-call(bf16[64,4,32,128]{3,2,1,0:T(8,128)(2,1)} %bitcast.9, ...), custom_call_target="tpu_custom_call" | custom-call | flops 2000000000 | bytes 30000000 | tf_op jit(solution)/shard_map/pallas_call | solution.py:534
  158.5 3.3 pad_maximum_fusion
  161.7 5.4 %all-to-all-done.2 = bf16[64,128,128]{2,1,0:T(8,128)(2,1)S(1)} async-done(((bf16[64,128,128]{2,1,0:T(8,128)(2,1)}), bf16[64,128,128]{2,1,0:T(8,128)(2,1)S(1)}, u32[]{:S(2)}, u32[]{:S(2)}) %all-to-all-start.2) | async-done | bytes 2097184 | tf_op jit(solution)/shard_map/all_to_all | solution.py:467
  168.5 5.8 %all-to-all-start.3 = ((bf16[64,136,128]{2,1,0:T(8,128)(2,1)}), bf16[64,136,128]{2,1,0:T(8,128)(2,1)S(1)}, u32[]{:S(2)}, u32[]{:S(2)}) async-start(bf16[64,136,128]{2,1,0:T(8,128)(2,1)} %pad_maximum_fusion), calls=%async_computation.3 | async-start | bytes 4456448 | tf_op jit(solution)/shard_map/all_to_all | solution.py:467
  175.9 14.3 %shard_map.63 = bf16[64,4,32,128]{3,2,1,0:T(8,128)(2,1)} custom-call(bf16[64,4,32,128]{3,2,1,0:T(8,128)(2,1)S(1)} %bitcast.8, f32[32,2,128,128]{3,2,1,0:T(8,128)} %get-tuple-element.31.e_ref, bf16[32,2,128,256]{3,2,1,0:T(8,128)(2,1)} %get-tuple-element.32.k_ref, bf16[32,2,128,256]{3,2,1,0:T(8,128)(2,1)} %get-tuple-element.33.v_ref), custom_call_target="tpu_custom_call" | custom-call | flops 1000000000 | bytes 20000000 | tf_op jit(solution)/shard_map/pallas_call | solution.py:573
  190.2 37.9 %all-to-all-done.3.back_ref = bf16[64,136,128]{2,1,0:T(8,128)(2,1)S(1)} async-done(((bf16[64,136,128]{2,1,0:T(8,128)(2,1)}), bf16[64,136,128]{2,1,0:T(8,128)(2,1)S(1)}, u32[]{:S(2)}, u32[]{:S(2)}) %all-to-all-start.3) | async-done | bytes 2228256 | tf_op jit(solution)/shard_map/all_to_all | solution.py:467
  228.1 4.7 %shard_map.64 = (bf16[64,8,128]{2,1,0:T(8,128)(2,1)S(1)}, bf16[512,128]{1,0:T(8,128)(2,1)S(1)}, bf16[64,128,128]{2,1,0:T(8,128)(2,1)S(1)}, bf16[64,128,128]{2,1,0:T(8,128)(2,1)S(1)}) custom-call(bf16[64,136,128]{2,1,0:T(8,128)(2,1)S(1)} %all-to-all-done.3.back_ref, bf16[64,128,128]{2,1,0:T(8,128)(2,1)} %get-tuple-element.28.g_hbm, ...), custom_call_target="tpu_custom_call" | custom-call | flops 100000000 | bytes 4000000 | tf_op jit(solution)/shard_map/pallas_call | solution.py:590
  232.9 16.2 %all_to_all.35.wd_ref = bf16[64,8,128]{2,1,0:T(8,128)(2,1)S(1)} all-to-all(bf16[64,8,128]{2,1,0:T(8,128)(2,1)S(1)} %get-tuple-element.38), channel_id=1, replica_groups=mesh['seq'=64,'head'=4] {'seq'}, dimensions={0} | all-to-all | bytes 262144 | tf_op jit(solution)/shard_map/all_to_all | solution.py:467
  249.0 2.5 shard_map.65
  251.6 4.9 %all-to-all-start.5 = ((bf16[64,128,128]{2,1,0:T(8,128)(2,1)}), bf16[64,128,128]{2,1,0:T(8,128)(2,1)S(1)}, u32[]{:S(2)}, u32[]{:S(2)}) async-start(bf16[64,128,128]{2,1,0:T(8,128)(2,1)} %shard_map.65), calls=%async_computation.5 | async-start | bytes 4194304 | tf_op jit(solution)/shard_map/all_to_all | solution.py:467
  256.5 6.5 %shard_map.66.att_ref = bf16[64,32,128]{2,1,0:T(8,128)(2,1)S(1)} custom-call(bf16[64,136,128]{2,1,0:T(8,128)(2,1)} %copy-done, f32[8,512]{1,0:T(8,128)S(1)} %get-tuple-element.35.row_ref, bf16[512,128]{1,0:T(8,128)(2,1)S(1)} %get-tuple-element.43.wts_ref), custom_call_target="tpu_custom_call" | custom-call | flops 2200000000 | bytes 4000000 | tf_op jit(solution)/shard_map/pallas_call | solution.py:619
  263.0 44.8 %all-to-all-done.5.terms_ref = bf16[64,128,128]{2,1,0:T(8,128)(2,1)S(1)} async-done(((bf16[64,128,128]{2,1,0:T(8,128)(2,1)}), bf16[64,128,128]{2,1,0:T(8,128)(2,1)S(1)}, u32[]{:S(2)}, u32[]{:S(2)}) %all-to-all-start.5) | async-done | bytes 2097184 | tf_op jit(solution)/shard_map/all_to_all | solution.py:467
  307.7 2.1 shard_map.67
  309.8 34.2 %all_to_all.36.in_ref = bf16[64,64,128]{2,1,0:T(8,128)(2,1)S(1)} all-to-all(bf16[64,64,128]{2,1,0:T(8,128)(2,1)S(1)} %shard_map.67), channel_id=1, replica_groups=mesh['seq'=64,'head'=4] {'seq'}, dimensions={0} | all-to-all | bytes 2097152 | tf_op jit(solution)/shard_map/all_to_all | solution.py:467
  (12 shorter events, 6.5 us)
Async XLA Ops:
  3.4 44.4 %all-to-all-start = ((bf16[64,72,128]{2,1,0:T(8,128)(2,1)}), bf16[64,72,128]{2,1,0:T(8,128)(2,1)S(1)}, u32[]{:S(2)}, u32[]{:S(2)}) async-start(bf16[64,72,128]{2,1,0:T(8,128)(2,1)} %shard_map.59), calls=%async_computation | async-start | bytes 2359296 | tf_op jit(solution)/shard_map/all_to_all | solution.py:467
  51.3 57.5 %all-to-all-start.1 = ((bf16[64,128,128]{2,1,0:T(8,128)(2,1)}), bf16[64,128,128]{2,1,0:T(8,128)(2,1)S(1)}, u32[]{:S(2)}, u32[]{:S(2)}) async-start(bf16[64,128,128]{2,1,0:T(8,128)(2,1)} %get-tuple-element.24), calls=%async_computation.1 | async-start | bytes 4194304 | tf_op jit(solution)/shard_map/all_to_all | solution.py:467
  108.8 1.3 copy-start.3
  110.1 57.1 %all-to-all-start.2 = ((bf16[64,128,128]{2,1,0:T(8,128)(2,1)}), bf16[64,128,128]{2,1,0:T(8,128)(2,1)S(1)}, u32[]{:S(2)}, u32[]{:S(2)}) async-start(bf16[64,128,128]{2,1,0:T(8,128)(2,1)} %get-tuple-element.28.g_hbm), calls=%async_computation.2 | async-start | bytes 4194304 | tf_op jit(solution)/shard_map/all_to_all | solution.py:467
  167.1 1.3 copy-start.1
  168.5 59.7 %all-to-all-start.3 = ((bf16[64,136,128]{2,1,0:T(8,128)(2,1)}), bf16[64,136,128]{2,1,0:T(8,128)(2,1)S(1)}, u32[]{:S(2)}, u32[]{:S(2)}) async-start(bf16[64,136,128]{2,1,0:T(8,128)(2,1)} %pad_maximum_fusion), calls=%async_computation.3 | async-start | bytes 4456448 | tf_op jit(solution)/shard_map/all_to_all | solution.py:467
  174.3 1.6 copy-start.2
  228.1 4.8 %copy-start = (bf16[64,136,128]{2,1,0:T(8,128)(2,1)}, bf16[64,136,128]{2,1,0:T(8,128)(2,1)S(1)}, u32[]{:S(2)}) copy-start(bf16[64,136,128]{2,1,0:T(8,128)(2,1)S(1)} %all-to-all-done.3.back_ref) | copy-start | bytes 6684676
  251.6 56.1 %all-to-all-start.5 = ((bf16[64,128,128]{2,1,0:T(8,128)(2,1)}), bf16[64,128,128]{2,1,0:T(8,128)(2,1)S(1)}, u32[]{:S(2)}, u32[]{:S(2)}) async-start(bf16[64,128,128]{2,1,0:T(8,128)(2,1)} %shard_map.65), calls=%async_computation.5 | async-start | bytes 4194304 | tf_op jit(solution)/shard_map/all_to_all | solution.py:467

commit v8 on v7

--- a/solution.py
+++ b/solution.py
@@ -354,6 +354,31 @@
         load(i).start()
     cols = jnp.transpose(row_ref[...])
     lane = iota((SPANS, HD), 1)
+    slot_lane = (iota((SPANS, 2 * HD), 1) % S).astype(F32)
+    owner = [hot(iota((SPANS, N), 1).astype(F32) == cols[:, 2 + n : 3 + n]) for n in range(2)]
+
+    def span_stats(first, lanes):
+        rows = jnp.concatenate(
+            [flat[pl.ds(first + i, N, stride=C), :].astype(BF) for i in range(2)], axis=1
+        )
+        row, col = iota((2 * HD, HD), 0), iota((2 * HD, HD), 1)
+        group = hot(lanes * (row // HD) + row % HD // S == col)
+        out = []
+        for n in range(2):
+            got = mm(owner[n], rows)
+            got = jnp.where(slot_lane == cols[:, 4 + n : 5 + n], got, 0.0).astype(BF)
+            out.append(mm(got, group))
+        return out
+
+    for j in range(N):
+        flat[j * C : (j + 1) * C, :] = back_ref[j, size:, :].astype(F32)
+    tops = span_stats(0, U)
+    totals = [pltpu.roll(rows, HD - U, 1) for rows in tops]
+    highest = jnp.maximum(tops[0], tops[1])
+    factor = [jnp.exp(t - highest) for t in tops]
+    denominator = factor[0] * totals[0] + factor[1] * totals[1]
+    low = [jnp.where(lane < U, f / denominator, 0.0).astype(BF).astype(F32) for f in factor]
+    wts_ref[...] = (low[0] + pltpu.roll(low[1], U, 1)).astype(BF)
     diagonal = iota((size, HD), 0) == iota((size, HD), 1)
     place = iota((C, HD), 0)
     for i in range(PRODUCT_STEPS):
@@ -366,45 +391,19 @@
             prod = jnp.where(diagonal, jnp.sum(prod, axis=1, keepdims=True), 0.0)
             total = jnp.sum(prod, axis=0, keepdims=True)
             high = total.astype(BF).astype(F32)
-            flat[j * C : (j + 1) * C, :] = jnp.where(
-                place == 2,
-                high,
-                jnp.where(place == 3, total - high, back_ref[j, size:, :].astype(F32)),
-            )
-    stats = jnp.concatenate(
-        [flat[pl.ds(i, N, stride=C), :].astype(BF) for i in range(4)], axis=1
-    )
-    row, col = iota((4 * HD, HD), 0), iota((4 * HD, HD), 1)
-    stat = jnp.minimum(row // HD, 2)
-    group = hot(stat * U + row % HD // S == col)
-    slot_lane = (iota((SPANS, 4 * HD), 1) % S).astype(F32)
-    tops, totals, products = [], [], []
-    for n in range(2):
-        owner = hot(iota((SPANS, N), 1).astype(F32) == cols[:, 2 + n : 3 + n])
-        rows = mm(owner, stats)
-        rows = jnp.where(slot_lane == cols[:, 4 + n : 5 + n], rows, 0.0).astype(BF)
-        rows = mm(rows, group)
-        tops.append(rows)
-        totals.append(pltpu.roll(rows, HD - U, 1))
-        products.append(pltpu.roll(rows, HD - 2 * U, 1))
-    highest = jnp.maximum(tops[0], tops[1])
-    factor = [jnp.exp(t - highest) for t in tops]
-    denominator = factor[0] * totals[0] + factor[1] * totals[1]
-    low = [jnp.where(lane < U, f / denominator, 0.0).astype(BF).astype(F32) for f in factor]
+            flat[j * C : (j + 1) * C, :] = jnp.where(place == 2, high, total - high)
+    products = span_stats(2, 0)
     delta = jnp.where(lane < U, low[0] * products[0] + low[1] * products[1], 0.0)
-    wts_ref[...] = (low[0] + pltpu.roll(low[1], U, 1)).astype(BF)
     delta = pltpu.roll(delta, U, 1)
     spread = hot(iota((HD, 2 * HD), 0) == iota((HD, 2 * HD), 1) // S)
     out = jnp.zeros((N, 2 * HD), F32)
     for n in range(2):
         rows = mm((low[n] + delta).astype(BF), spread)
-        rows = jnp.where(slot_lane[:, : 2 * HD] == cols[:, 4 + n : 5 + n], rows, 0.0)
+        rows = jnp.where(slot_lane == cols[:, 4 + n : 5 + n], rows, 0.0)
         owners = hot(iota((N, SPANS), 0).astype(F32) == row_ref[2 + n : 3 + n, :])
         out = out + mm(owners, rows.astype(BF))
-    place = iota((N, C, HD), 1)
-    wd_ref[...] = jnp.where(
-        place == 0, out[:, None, :HD], jnp.where(place == 1, out[:, None, HD:], 0.0)
-    ).astype(BF)
+    place = iota((N, 2, HD), 1)
+    wd_ref[...] = jnp.where(place == 0, out[:, None, :HD], out[:, None, HD:]).astype(BF)
     for copy in later:
         copy.wait()
 
@@ -436,12 +435,12 @@
         at = pl.ds(i * per, per)
         return pltpu.make_async_copy(out_ref.at[at], out_hbm.at[at], sem.at[i])
 
-    flat = wd_ref[...].astype(F32).reshape(C * N, HD)
+    flat = wd_ref[...].astype(F32).reshape(2 * N, HD)
     cols = jnp.transpose(flat)
     for i in range(PRODUCT_STEPS):
         for k in range(i * per, (i + 1) * per):
-            w = cols[:, C * k : C * k + 1]
-            delta = cols[:, C * k + 1 : C * k + 2]
+            w = cols[:, 2 * k : 2 * k + 1]
+            delta = cols[:, 2 * k + 1 : 2 * k + 2]
             out_ref[k] = (
                 w * (a_ref[k].astype(F32) - delta * b_ref[k].astype(F32)) * SCALE
             ).astype(BF)
@@ -589,7 +588,7 @@
     rows = sds((N, U * S, HD), BF)
     wd_send, wts, a_rows, b_rows = call(
         weight_body,
-        (sds((N, C, HD), BF), sds((SPANS, HD), BF), rows, rows),
+        (sds((N, 2, HD), BF), sds((SPANS, HD), BF), rows, rows),
         in_specs=[VMEM, HBM, VMEM, HBM, HBM],
         scratch_shapes=[
             pltpu.VMEM((N, U * S, HD), BF),

time: 346 us -> 346 us (level)
  no operation moved by 1% of the time
where the time goes in v8:
time: 346 us; the launch traced here: 345 us
  waiting for transfers between devices  146 us (42%)
  Pallas kernels  85.3 us (25%)
  blocking collectives  64.5 us (19%)
  starting transfers between devices  35.6 us (10%)
  other arithmetic  8.36 us (2%)
  local copies, waits for them, and re-layouts  4.95 us (1%)
    all_to_all x5, waiting for transfers between devices, swap(): return lax.all_to_all(rows, 'seq', split_axis=0, concat_axis=0, tiled=True)  146 us
    all_to_all x2, blocking collectives, swap(): return lax.all_to_all(rows, 'seq', split_axis=0, concat_axis=0, tiled=True)  49.3 us
    pallas_call x1, Pallas kernels, local(): call(forward_body, (sds((S, H // 2, 2 * SPAN, R), F32), sds((S, H // 2, R...  42.6 us
    all_to_all x5, starting transfers between devices, swap(): return lax.all_to_all(rows, 'seq', split_axis=0, concat_axis=0, tiled=True)  35.6 us
    psum x1, blocking collectives, local(): row_scale = lax.rsqrt(lax.psum(square_sums, 'head') / D + 1e-06)  15.2 us
    pallas_call x1, Pallas kernels, local(): call(backward_body, pltpu.HBM((N, U, S, HD), BF), grid=(2,), in_specs=[ha...  14.3 us
    pallas_call x2, Pallas kernels, route(): call(functools.partial(route_body, base), (pltpu.HBM((N, U * S, HD), BF),...  7.56 us
  transfers between devices with their start and end apart: 5, of which 5 were waited for; matrix products, arithmetic and copies ran while one was open for 3% of the time, Pallas kernels for 20%

profile of v8, /device:TPU:1, one launch (start us, length us, event | category | flops | bytes accessed | tf_op | source)
XLA Modules:
  0.0 345.2 jit_solution(14872140247170413778)
XLA Ops:
  0.6 2.8 shard_map.59
  3.4 13.0 %all-to-all-start = ((bf16[64,72,128]{2,1,0:T(8,128)(2,1)}), bf16[64,72,128]{2,1,0:T(8,128)(2,1)S(1)}, u32[]{:S(2)}, u32[]{:S(2)}) async-start(bf16[64,72,128]{2,1,0:T(8,128)(2,1)} %shard_map.59), calls=%async_computation | async-start | bytes 2359296 | tf_op jit(solution)/shard_map/all_to_all | solution.py:466
  16.4 5.1 %multiply_reduce_fusion = f32[32,128]{1,0:T(8,128)S(1)} fusion(bf16[32,128,1024]{2,1,0:T(8,128)(2,1)} %nb_ref.1), kind=kLoop, calls=%fused_computation | loop fusion | flops 12578816 | bytes 8404992 | tf_op jit(solution)/shard_map/reduce_sum | solution.py:515
  21.6 15.2 %psum.7 = f32[32,128]{0,1:T(8,128)S(1)} all-reduce(f32[32,128]{0,1:T(8,128)S(1)} %copy.6), channel_id=1, replica_groups=mesh['seq'=64,'head'=4] {'head'}, use_global_device_ids=true, to_apply=%region_1.0 | all-reduce | flops 4096 | bytes 32768 | tf_op jit(solution)/shard_map/psum | solution.py:516
  37.5 10.3 %all-to-all-done.first_ref = bf16[64,72,128]{2,1,0:T(8,128)(2,1)S(1)} async-done(((bf16[64,72,128]{2,1,0:T(8,128)(2,1)}), bf16[64,72,128]{2,1,0:T(8,128)(2,1)S(1)}, u32[]{:S(2)}, u32[]{:S(2)}) %all-to-all-start) | async-done | bytes 1179680 | tf_op jit(solution)/shard_map/all_to_all | solution.py:466
  47.8 3.5 %shard_map.60 = (bf16[64,128,128]{2,1,0:T(8,128)(2,1)}, f32[8,512]{1,0:T(8,128)S(1)}) custom-call(bf16[64,72,128]{2,1,0:T(8,128)(2,1)S(1)} %all-to-all-done.first_ref), custom_call_target="tpu_custom_call" | custom-call | flops 1100000000 | bytes 4000000 | tf_op jit(solution)/shard_map/pallas_call | solution.py:478
  51.3 6.2 %all-to-all-start.1 = ((bf16[64,128,128]{2,1,0:T(8,128)(2,1)}), bf16[64,128,128]{2,1,0:T(8,128)(2,1)S(1)}, u32[]{:S(2)}, u32[]{:S(2)}) async-start(bf16[64,128,128]{2,1,0:T(8,128)(2,1)} %get-tuple-element.24), calls=%async_computation.1 | async-start | bytes 4194304 | tf_op jit(solution)/shard_map/all_to_all | solution.py:466
  57.5 4.1 %shard_map.62 = (bf16[64,128,128]{2,1,0:T(8,128)(2,1)}, f32[8,512]{1,0:T(8,128)}) custom-call(bf16[64,72,128]{2,1,0:T(8,128)(2,1)S(1)} %all-to-all-done.first_ref), custom_call_target="tpu_custom_call" | custom-call | flops 1100000000 | bytes 4000000 | tf_op jit(solution)/shard_map/pallas_call | solution.py:478
  61.6 47.2 %all-to-all-done.1 = bf16[64,128,128]{2,1,0:T(8,128)(2,1)S(1)} async-done(((bf16[64,128,128]{2,1,0:T(8,128)(2,1)}), bf16[64,128,128]{2,1,0:T(8,128)(2,1)S(1)}, u32[]{:S(2)}, u32[]{:S(2)}) %all-to-all-start.1) | async-done | bytes 2097184 | tf_op jit(solution)/shard_map/all_to_all | solution.py:466
  110.1 5.8 %all-to-all-start.2 = ((bf16[64,128,128]{2,1,0:T(8,128)(2,1)}), bf16[64,128,128]{2,1,0:T(8,128)(2,1)S(1)}, u32[]{:S(2)}, u32[]{:S(2)}) async-start(bf16[64,128,128]{2,1,0:T(8,128)(2,1)} %get-tuple-element.28.g_hbm), calls=%async_computation.2 | async-start | bytes 4194304 | tf_op jit(solution)/shard_map/all_to_all | solution.py:466
  115.9 42.6 %shard_map.61 = (f32[32,2,128,128]{3,2,1,0:T(8,128)}, bf16[32,2,128,256]{3,2,1,0:T(8,128)(2,1)}, bf16[32,2,128,256]{3,2,1,0:T(8,128)(2,1)}, bf16[64,4,32,128]{3,...) custom-call(bf16[64,4,32,128]{3,2,1,0:T(8,128)(2,1)} %bitcast.9, ...), custom_call_target="tpu_custom_call" | custom-call | flops 2000000000 | bytes 30000000 | tf_op jit(solution)/shard_map/pallas_call | solution.py:533
  158.5 3.3 pad_maximum_fusion
  161.7 5.4 %all-to-all-done.2 = bf16[64,128,128]{2,1,0:T(8,128)(2,1)S(1)} async-done(((bf16[64,128,128]{2,1,0:T(8,128)(2,1)}), bf16[64,128,128]{2,1,0:T(8,128)(2,1)S(1)}, u32[]{:S(2)}, u32[]{:S(2)}) %all-to-all-start.2) | async-done | bytes 2097184 | tf_op jit(solution)/shard_map/all_to_all | solution.py:466
  168.5 5.8 %all-to-all-start.3 = ((bf16[64,136,128]{2,1,0:T(8,128)(2,1)}), bf16[64,136,128]{2,1,0:T(8,128)(2,1)S(1)}, u32[]{:S(2)}, u32[]{:S(2)}) async-start(bf16[64,136,128]{2,1,0:T(8,128)(2,1)} %pad_maximum_fusion), calls=%async_computation.3 | async-start | bytes 4456448 | tf_op jit(solution)/shard_map/all_to_all | solution.py:466
  175.9 14.3 %shard_map.63 = bf16[64,4,32,128]{3,2,1,0:T(8,128)(2,1)} custom-call(bf16[64,4,32,128]{3,2,1,0:T(8,128)(2,1)S(1)} %bitcast.8, f32[32,2,128,128]{3,2,1,0:T(8,128)} %get-tuple-element.31.e_ref, bf16[32,2,128,256]{3,2,1,0:T(8,128)(2,1)} %get-tuple-element.32.k_ref, bf16[32,2,128,256]{3,2,1,0:T(8,128)(2,1)} %get-tuple-element.33.v_ref), custom_call_target="tpu_custom_call" | custom-call | flops 1000000000 | bytes 20000000 | tf_op jit(solution)/shard_map/pallas_call | solution.py:572
  190.2 37.9 %all-to-all-done.3.back_ref = bf16[64,136,128]{2,1,0:T(8,128)(2,1)S(1)} async-done(((bf16[64,136,128]{2,1,0:T(8,128)(2,1)}), bf16[64,136,128]{2,1,0:T(8,128)(2,1)S(1)}, u32[]{:S(2)}, u32[]{:S(2)}) %all-to-all-start.3) | async-done | bytes 2228256 | tf_op jit(solution)/shard_map/all_to_all | solution.py:466
  228.1 4.7 %shard_map.64 = (bf16[64,2,128]{2,1,0:T(2,128)(2,1)S(1)}, bf16[512,128]{1,0:T(8,128)(2,1)S(1)}, bf16[64,128,128]{2,1,0:T(8,128)(2,1)S(1)}, bf16[64,128,128]{2,1,0:T(8,128)(2,1)S(1)}) custom-call(bf16[64,136,128]{2,1,0:T(8,128)(2,1)S(1)} %all-to-all-done.3.back_ref, bf16[64,128,128]{2,1,0:T(8,128)(2,1)} %get-tuple-element.28.g_hbm, ...), custom_call_target="tpu_custom_call" | custom-call | flops 100000000 | bytes 4000000 | tf_op jit(solution)/shard_map/pallas_call | solution.py:589
  232.8 15.1 %all_to_all.35.wd_ref = bf16[64,2,128]{2,1,0:T(2,128)(2,1)S(1)} all-to-all(bf16[64,2,128]{2,1,0:T(2,128)(2,1)S(1)} %get-tuple-element.38), channel_id=1, replica_groups=mesh['seq'=64,'head'=4] {'seq'}, dimensions={0} | all-to-all | bytes 65536 | tf_op jit(solution)/shard_map/all_to_all | solution.py:466
  247.9 3.3 shard_map.65
  251.2 4.8 %all-to-all-start.5 = ((bf16[64,128,128]{2,1,0:T(8,128)(2,1)}), bf16[64,128,128]{2,1,0:T(8,128)(2,1)S(1)}, u32[]{:S(2)}, u32[]{:S(2)}) async-start(bf16[64,128,128]{2,1,0:T(8,128)(2,1)} %shard_map.65), calls=%async_computation.5 | async-start | bytes 4194304 | tf_op jit(solution)/shard_map/all_to_all | solution.py:466
  256.0 6.5 %shard_map.66.att_ref = bf16[64,32,128]{2,1,0:T(8,128)(2,1)S(1)} custom-call(bf16[64,136,128]{2,1,0:T(8,128)(2,1)} %copy-done, f32[8,512]{1,0:T(8,128)S(1)} %get-tuple-element.35.row_ref, bf16[512,128]{1,0:T(8,128)(2,1)S(1)} %get-tuple-element.43.wts_ref), custom_call_target="tpu_custom_call" | custom-call | flops 2200000000 | bytes 4000000 | tf_op jit(solution)/shard_map/pallas_call | solution.py:618
  262.5 44.9 %all-to-all-done.5.terms_ref = bf16[64,128,128]{2,1,0:T(8,128)(2,1)S(1)} async-done(((bf16[64,128,128]{2,1,0:T(8,128)(2,1)}), bf16[64,128,128]{2,1,0:T(8,128)(2,1)S(1)}, u32[]{:S(2)}, u32[]{:S(2)}) %all-to-all-start.5) | async-done | bytes 2097184 | tf_op jit(solution)/shard_map/all_to_all | solution.py:466
  307.4 2.1 shard_map.67
  309.5 34.2 %all_to_all.36.in_ref = bf16[64,64,128]{2,1,0:T(8,128)(2,1)S(1)} all-to-all(bf16[64,64,128]{2,1,0:T(8,128)(2,1)S(1)} %shard_map.67), channel_id=1, replica_groups=mesh['seq'=64,'head'=4] {'seq'}, dimensions={0} | all-to-all | bytes 2097152 | tf_op jit(solution)/shard_map/all_to_all | solution.py:466
  (12 shorter events, 6.5 us)
Async XLA Ops:
  3.4 44.4 %all-to-all-start = ((bf16[64,72,128]{2,1,0:T(8,128)(2,1)}), bf16[64,72,128]{2,1,0:T(8,128)(2,1)S(1)}, u32[]{:S(2)}, u32[]{:S(2)}) async-start(bf16[64,72,128]{2,1,0:T(8,128)(2,1)} %shard_map.59), calls=%async_computation | async-start | bytes 2359296 | tf_op jit(solution)/shard_map/all_to_all | solution.py:466
  51.3 57.5 %all-to-all-start.1 = ((bf16[64,128,128]{2,1,0:T(8,128)(2,1)}), bf16[64,128,128]{2,1,0:T(8,128)(2,1)S(1)}, u32[]{:S(2)}, u32[]{:S(2)}) async-start(bf16[64,128,128]{2,1,0:T(8,128)(2,1)} %get-tuple-element.24), calls=%async_computation.1 | async-start | bytes 4194304 | tf_op jit(solution)/shard_map/all_to_all | solution.py:466
  108.8 1.3 copy-start.3
  110.1 57.1 %all-to-all-start.2 = ((bf16[64,128,128]{2,1,0:T(8,128)(2,1)}), bf16[64,128,128]{2,1,0:T(8,128)(2,1)S(1)}, u32[]{:S(2)}, u32[]{:S(2)}) async-start(bf16[64,128,128]{2,1,0:T(8,128)(2,1)} %get-tuple-element.28.g_hbm), calls=%async_computation.2 | async-start | bytes 4194304 | tf_op jit(solution)/shard_map/all_to_all | solution.py:466
  167.1 1.3 copy-start.1
  168.5 59.7 %all-to-all-start.3 = ((bf16[64,136,128]{2,1,0:T(8,128)(2,1)}), bf16[64,136,128]{2,1,0:T(8,128)(2,1)S(1)}, u32[]{:S(2)}, u32[]{:S(2)}) async-start(bf16[64,136,128]{2,1,0:T(8,128)(2,1)} %pad_maximum_fusion), calls=%async_computation.3 | async-start | bytes 4456448 | tf_op jit(solution)/shard_map/all_to_all | solution.py:466
  174.3 1.6 copy-start.2
  228.1 4.7 %copy-start = (bf16[64,136,128]{2,1,0:T(8,128)(2,1)}, bf16[64,136,128]{2,1,0:T(8,128)(2,1)S(1)}, u32[]{:S(2)}) copy-start(bf16[64,136,128]{2,1,0:T(8,128)(2,1)S(1)} %all-to-all-done.3.back_ref) | copy-start | bytes 6684676
  251.2 56.2 %all-to-all-start.5 = ((bf16[64,128,128]{2,1,0:T(8,128)(2,1)}), bf16[64,128,128]{2,1,0:T(8,128)(2,1)S(1)}, u32[]{:S(2)}, u32[]{:S(2)}) async-start(bf16[64,128,128]{2,1,0:T(8,128)(2,1)} %shard_map.65), calls=%async_computation.5 | async-start | bytes 4194304 | tf_op jit(solution)/shard_map/all_to_all | solution.py:466

commit v9 on v8

--- a/solution.py
+++ b/solution.py
@@ -402,8 +402,10 @@
         rows = jnp.where(slot_lane == cols[:, 4 + n : 5 + n], rows, 0.0)
         owners = hot(iota((N, SPANS), 0).astype(F32) == row_ref[2 + n : 3 + n, :])
         out = out + mm(owners, rows.astype(BF))
-    place = iota((N, 2, HD), 1)
-    wd_ref[...] = jnp.where(place == 0, out[:, None, :HD], out[:, None, HD:]).astype(BF)
+    place = iota((N, C, HD), 1)
+    wd_ref[...] = jnp.where(
+        place == 0, out[:, None, :HD], jnp.where(place == 1, out[:, None, HD:], 0.0)
+    ).astype(BF)
     for copy in later:
         copy.wait()
 
@@ -435,12 +437,12 @@
         at = pl.ds(i * per, per)
         return pltpu.make_async_copy(out_ref.at[at], out_hbm.at[at], sem.at[i])
 
-    flat = wd_ref[...].astype(F32).reshape(2 * N, HD)
+    flat = wd_ref[...].astype(F32).reshape(C * N, HD)
     cols = jnp.transpose(flat)
     for i in range(PRODUCT_STEPS):
         for k in range(i * per, (i + 1) * per):
-            w = cols[:, 2 * k : 2 * k + 1]
-            delta = cols[:, 2 * k + 1 : 2 * k + 2]
+            w = cols[:, C * k : C * k + 1]
+            delta = cols[:, C * k + 1 : C * k + 2]
             out_ref[k] = (
                 w * (a_ref[k].astype(F32) - delta * b_ref[k].astype(F32)) * SCALE
             ).astype(BF)
@@ -588,7 +590,7 @@
     rows = sds((N, U * S, HD), BF)
     wd_send, wts, a_rows, b_rows = call(
         weight_body,
-        (sds((N, 2, HD), BF), sds((SPANS, HD), BF), rows, rows),
+        (sds((N, C, HD), BF), sds((SPANS, HD), BF), rows, rows),
         in_specs=[VMEM, HBM, VMEM, HBM, HBM],
         scratch_shapes=[
             pltpu.VMEM((N, U * S, HD), BF),

time: 346 us -> 346 us (level)
  no operation moved by 1% of the time
where the time goes in v9:
time: 346 us; the launch traced here: 345 us
  waiting for transfers between devices  146 us (42%)
  Pallas kernels  84.5 us (24%)
  blocking collectives  65.5 us (19%)
  starting transfers between devices  35.7 us (10%)
  other arithmetic  8.36 us (2%)
  local copies, waits for them, and re-layouts  4.95 us (1%)
    all_to_all x5, waiting for transfers between devices, swap(): return lax.all_to_all(rows, 'seq', split_axis=0, concat_axis=0, tiled=True)  146 us
    all_to_all x2, blocking collectives, swap(): return lax.all_to_all(rows, 'seq', split_axis=0, concat_axis=0, tiled=True)  50.3 us
    pallas_call x1, Pallas kernels, local(): call(forward_body, (sds((S, H // 2, 2 * SPAN, R), F32), sds((S, H // 2, R...  42.6 us
    all_to_all x5, starting transfers between devices, swap(): return lax.all_to_all(rows, 'seq', split_axis=0, concat_axis=0, tiled=True)  35.7 us
    psum x1, blocking collectives, local(): row_scale = lax.rsqrt(lax.psum(square_sums, 'head') / D + 1e-06)  15.2 us
    pallas_call x1, Pallas kernels, local(): call(backward_body, pltpu.HBM((N, U, S, HD), BF), grid=(2,), in_specs=[ha...  14.3 us
    pallas_call x2, Pallas kernels, route(): call(functools.partial(route_body, base), (pltpu.HBM((N, U * S, HD), BF),...  7.56 us
  transfers between devices with their start and end apart: 5, of which 5 were waited for; matrix products, arithmetic and copies ran while one was open for 3% of the time, Pallas kernels for 20%

profile of v9, /device:TPU:1, one launch (start us, length us, event | category | flops | bytes accessed | tf_op | source)
XLA Modules:
  0.0 345.4 jit_solution(10343161432808327504)
XLA Ops:
  0.6 2.8 shard_map.59
  3.4 13.0 %all-to-all-start = ((bf16[64,72,128]{2,1,0:T(8,128)(2,1)}), bf16[64,72,128]{2,1,0:T(8,128)(2,1)S(1)}, u32[]{:S(2)}, u32[]{:S(2)}) async-start(bf16[64,72,128]{2,1,0:T(8,128)(2,1)} %shard_map.59), calls=%async_computation | async-start | bytes 2359296 | tf_op jit(solution)/shard_map/all_to_all | solution.py:468
  16.4 5.1 %multiply_reduce_fusion = f32[32,128]{1,0:T(8,128)S(1)} fusion(bf16[32,128,1024]{2,1,0:T(8,128)(2,1)} %nb_ref.1), kind=kLoop, calls=%fused_computation | loop fusion | flops 12578816 | bytes 8404992 | tf_op jit(solution)/shard_map/reduce_sum | solution.py:517
  21.6 15.2 %psum.7 = f32[32,128]{0,1:T(8,128)S(1)} all-reduce(f32[32,128]{0,1:T(8,128)S(1)} %copy.6), channel_id=1, replica_groups=mesh['seq'=64,'head'=4] {'head'}, use_global_device_ids=true, to_apply=%region_1.0 | all-reduce | flops 4096 | bytes 32768 | tf_op jit(solution)/shard_map/psum | solution.py:518
  37.5 10.3 %all-to-all-done.first_ref = bf16[64,72,128]{2,1,0:T(8,128)(2,1)S(1)} async-done(((bf16[64,72,128]{2,1,0:T(8,128)(2,1)}), bf16[64,72,128]{2,1,0:T(8,128)(2,1)S(1)}, u32[]{:S(2)}, u32[]{:S(2)}) %all-to-all-start) | async-done | bytes 1179680 | tf_op jit(solution)/shard_map/all_to_all | solution.py:468
  47.8 3.5 %shard_map.60 = (bf16[64,128,128]{2,1,0:T(8,128)(2,1)}, f32[8,512]{1,0:T(8,128)S(1)}) custom-call(bf16[64,72,128]{2,1,0:T(8,128)(2,1)S(1)} %all-to-all-done.first_ref), custom_call_target="tpu_custom_call" | custom-call | flops 1100000000 | bytes 4000000 | tf_op jit(solution)/shard_map/pallas_call | solution.py:480
  51.3 6.2 %all-to-all-start.1 = ((bf16[64,128,128]{2,1,0:T(8,128)(2,1)}), bf16[64,128,128]{2,1,0:T(8,128)(2,1)S(1)}, u32[]{:S(2)}, u32[]{:S(2)}) async-start(bf16[64,128,128]{2,1,0:T(8,128)(2,1)} %get-tuple-element.24), calls=%async_computation.1 | async-start | bytes 4194304 | tf_op jit(solution)/shard_map/all_to_all | solution.py:468
  57.5 4.1 %shard_map.62 = (bf16[64,128,128]{2,1,0:T(8,128)(2,1)}, f32[8,512]{1,0:T(8,128)}) custom-call(bf16[64,72,128]{2,1,0:T(8,128)(2,1)S(1)} %all-to-all-done.first_ref), custom_call_target="tpu_custom_call" | custom-call | flops 1100000000 | bytes 4000000 | tf_op jit(solution)/shard_map/pallas_call | solution.py:480
  61.6 47.2 %all-to-all-done.1 = bf16[64,128,128]{2,1,0:T(8,128)(2,1)S(1)} async-done(((bf16[64,128,128]{2,1,0:T(8,128)(2,1)}), bf16[64,128,128]{2,1,0:T(8,128)(2,1)S(1)}, u32[]{:S(2)}, u32[]{:S(2)}) %all-to-all-start.1) | async-done | bytes 2097184 | tf_op jit(solution)/shard_map/all_to_all | solution.py:468
  110.1 5.8 %all-to-all-start.2 = ((bf16[64,128,128]{2,1,0:T(8,128)(2,1)}), bf16[64,128,128]{2,1,0:T(8,128)(2,1)S(1)}, u32[]{:S(2)}, u32[]{:S(2)}) async-start(bf16[64,128,128]{2,1,0:T(8,128)(2,1)} %get-tuple-element.28.g_hbm), calls=%async_computation.2 | async-start | bytes 4194304 | tf_op jit(solution)/shard_map/all_to_all | solution.py:468
  115.9 42.6 %shard_map.61 = (f32[32,2,128,128]{3,2,1,0:T(8,128)}, bf16[32,2,128,256]{3,2,1,0:T(8,128)(2,1)}, bf16[32,2,128,256]{3,2,1,0:T(8,128)(2,1)}, bf16[64,4,32,128]{3,...) custom-call(bf16[64,4,32,128]{3,2,1,0:T(8,128)(2,1)} %bitcast.9, ...), custom_call_target="tpu_custom_call" | custom-call | flops 2000000000 | bytes 30000000 | tf_op jit(solution)/shard_map/pallas_call | solution.py:535
  158.5 3.3 pad_maximum_fusion
  161.7 5.4 %all-to-all-done.2 = bf16[64,128,128]{2,1,0:T(8,128)(2,1)S(1)} async-done(((bf16[64,128,128]{2,1,0:T(8,128)(2,1)}), bf16[64,128,128]{2,1,0:T(8,128)(2,1)S(1)}, u32[]{:S(2)}, u32[]{:S(2)}) %all-to-all-start.2) | async-done | bytes 2097184 | tf_op jit(solution)/shard_map/all_to_all | solution.py:468
  168.5 5.8 %all-to-all-start.3 = ((bf16[64,136,128]{2,1,0:T(8,128)(2,1)}), bf16[64,136,128]{2,1,0:T(8,128)(2,1)S(1)}, u32[]{:S(2)}, u32[]{:S(2)}) async-start(bf16[64,136,128]{2,1,0:T(8,128)(2,1)} %pad_maximum_fusion), calls=%async_computation.3 | async-start | bytes 4456448 | tf_op jit(solution)/shard_map/all_to_all | solution.py:468
  175.9 14.3 %shard_map.63 = bf16[64,4,32,128]{3,2,1,0:T(8,128)(2,1)} custom-call(bf16[64,4,32,128]{3,2,1,0:T(8,128)(2,1)S(1)} %bitcast.8, f32[32,2,128,128]{3,2,1,0:T(8,128)} %get-tuple-element.31.e_ref, bf16[32,2,128,256]{3,2,1,0:T(8,128)(2,1)} %get-tuple-element.32.k_ref, bf16[32,2,128,256]{3,2,1,0:T(8,128)(2,1)} %get-tuple-element.33.v_ref), custom_call_target="tpu_custom_call" | custom-call | flops 1000000000 | bytes 20000000 | tf_op jit(solution)/shard_map/pallas_call | solution.py:574
  190.2 37.9 %all-to-all-done.3.back_ref = bf16[64,136,128]{2,1,0:T(8,128)(2,1)S(1)} async-done(((bf16[64,136,128]{2,1,0:T(8,128)(2,1)}), bf16[64,136,128]{2,1,0:T(8,128)(2,1)S(1)}, u32[]{:S(2)}, u32[]{:S(2)}) %all-to-all-start.3) | async-done | bytes 2228256 | tf_op jit(solution)/shard_map/all_to_all | solution.py:468
  228.1 4.7 %shard_map.64 = (bf16[64,8,128]{2,1,0:T(8,128)(2,1)S(1)}, bf16[512,128]{1,0:T(8,128)(2,1)S(1)}, bf16[64,128,128]{2,1,0:T(8,128)(2,1)S(1)}, bf16[64,128,128]{2,1,0:T(8,128)(2,1)S(1)}) custom-call(bf16[64,136,128]{2,1,0:T(8,128)(2,1)S(1)} %all-to-all-done.3.back_ref, bf16[64,128,128]{2,1,0:T(8,128)(2,1)} %get-tuple-element.28.g_hbm, ...), custom_call_target="tpu_custom_call" | custom-call | flops 100000000 | bytes 4000000 | tf_op jit(solution)/shard_map/pallas_call | solution.py:591
  232.8 16.2 %all_to_all.35.wd_ref = bf16[64,8,128]{2,1,0:T(8,128)(2,1)S(1)} all-to-all(bf16[64,8,128]{2,1,0:T(8,128)(2,1)S(1)} %get-tuple-element.38), channel_id=1, replica_groups=mesh['seq'=64,'head'=4] {'seq'}, dimensions={0} | all-to-all | bytes 262144 | tf_op jit(solution)/shard_map/all_to_all | solution.py:468
  249.0 2.5 shard_map.65
  251.5 4.9 %all-to-all-start.5 = ((bf16[64,128,128]{2,1,0:T(8,128)(2,1)}), bf16[64,128,128]{2,1,0:T(8,128)(2,1)S(1)}, u32[]{:S(2)}, u32[]{:S(2)}) async-start(bf16[64,128,128]{2,1,0:T(8,128)(2,1)} %shard_map.65), calls=%async_computation.5 | async-start | bytes 4194304 | tf_op jit(solution)/shard_map/all_to_all | solution.py:468
  256.4 6.5 %shard_map.66.att_ref = bf16[64,32,128]{2,1,0:T(8,128)(2,1)S(1)} custom-call(bf16[64,136,128]{2,1,0:T(8,128)(2,1)} %copy-done, f32[8,512]{1,0:T(8,128)S(1)} %get-tuple-element.35.row_ref, bf16[512,128]{1,0:T(8,128)(2,1)S(1)} %get-tuple-element.43.wts_ref), custom_call_target="tpu_custom_call" | custom-call | flops 2200000000 | bytes 4000000 | tf_op jit(solution)/shard_map/pallas_call | solution.py:620
  262.9 44.8 %all-to-all-done.5.terms_ref = bf16[64,128,128]{2,1,0:T(8,128)(2,1)S(1)} async-done(((bf16[64,128,128]{2,1,0:T(8,128)(2,1)}), bf16[64,128,128]{2,1,0:T(8,128)(2,1)S(1)}, u32[]{:S(2)}, u32[]{:S(2)}) %all-to-all-start.5) | async-done | bytes 2097184 | tf_op jit(solution)/shard_map/all_to_all | solution.py:468
  307.7 2.1 shard_map.67
  309.7 34.2 %all_to_all.36.in_ref = bf16[64,64,128]{2,1,0:T(8,128)(2,1)S(1)} all-to-all(bf16[64,64,128]{2,1,0:T(8,128)(2,1)S(1)} %shard_map.67), channel_id=1, replica_groups=mesh['seq'=64,'head'=4] {'seq'}, dimensions={0} | all-to-all | bytes 2097152 | tf_op jit(solution)/shard_map/all_to_all | solution.py:468
  (12 shorter events, 6.5 us)
Async XLA Ops:
  3.4 44.4 %all-to-all-start = ((bf16[64,72,128]{2,1,0:T(8,128)(2,1)}), bf16[64,72,128]{2,1,0:T(8,128)(2,1)S(1)}, u32[]{:S(2)}, u32[]{:S(2)}) async-start(bf16[64,72,128]{2,1,0:T(8,128)(2,1)} %shard_map.59), calls=%async_computation | async-start | bytes 2359296 | tf_op jit(solution)/shard_map/all_to_all | solution.py:468
  51.3 57.5 %all-to-all-start.1 = ((bf16[64,128,128]{2,1,0:T(8,128)(2,1)}), bf16[64,128,128]{2,1,0:T(8,128)(2,1)S(1)}, u32[]{:S(2)}, u32[]{:S(2)}) async-start(bf16[64,128,128]{2,1,0:T(8,128)(2,1)} %get-tuple-element.24), calls=%async_computation.1 | async-start | bytes 4194304 | tf_op jit(solution)/shard_map/all_to_all | solution.py:468
  108.8 1.3 copy-start.3
  110.1 57.1 %all-to-all-start.2 = ((bf16[64,128,128]{2,1,0:T(8,128)(2,1)}), bf16[64,128,128]{2,1,0:T(8,128)(2,1)S(1)}, u32[]{:S(2)}, u32[]{:S(2)}) async-start(bf16[64,128,128]{2,1,0:T(8,128)(2,1)} %get-tuple-element.28.g_hbm), calls=%async_computation.2 | async-start | bytes 4194304 | tf_op jit(solution)/shard_map/all_to_all | solution.py:468
  167.1 1.3 copy-start.1
  168.5 59.7 %all-to-all-start.3 = ((bf16[64,136,128]{2,1,0:T(8,128)(2,1)}), bf16[64,136,128]{2,1,0:T(8,128)(2,1)S(1)}, u32[]{:S(2)}, u32[]{:S(2)}) async-start(bf16[64,136,128]{2,1,0:T(8,128)(2,1)} %pad_maximum_fusion), calls=%async_computation.3 | async-start | bytes 4456448 | tf_op jit(solution)/shard_map/all_to_all | solution.py:468
  174.3 1.6 copy-start.2
  228.1 4.7 %copy-start = (bf16[64,136,128]{2,1,0:T(8,128)(2,1)}, bf16[64,136,128]{2,1,0:T(8,128)(2,1)S(1)}, u32[]{:S(2)}) copy-start(bf16[64,136,128]{2,1,0:T(8,128)(2,1)S(1)} %all-to-all-done.3.back_ref) | copy-start | bytes 6684676
  251.5 56.1 %all-to-all-start.5 = ((bf16[64,128,128]{2,1,0:T(8,128)(2,1)}), bf16[64,128,128]{2,1,0:T(8,128)(2,1)S(1)}, u32[]{:S(2)}, u32[]{:S(2)}) async-start(bf16[64,128,128]{2,1,0:T(8,128)(2,1)} %shard_map.65), calls=%async_computation.5 | async-start | bytes 4194304 | tf_op jit(solution)/shard_map/all_to_all | solution.py:468
